TPU v7x, 32 devices: a whole 2x2x4 slice. The times are simulated.
32 devices in a mesh: dir: 8 (over y, x, core), region: 4 (over z).
Axes of the slice: x: 2, y: 2, z: 4, core: 2. Of those that a mesh axis runs over, the one named last changes fastest.
Arguments:
- currents: bfloat16 [4, 48, 128, 256], P('region', 'dir'), may hold values from -6 to 6
- radiate: bfloat16 [1536, 128], replicated, may hold values from -0.5 to 0.5
- receive: bfloat16 [128, 1536], replicated, may hold values from -0.15625 to 0.15625
- transfer_table: bfloat16 [316, 1536], replicated, may hold values from -0.875 to 0.875
- near_blocks: bfloat16 [4, 48, 27, 128, 128], P('region', 'dir'), may hold values from -0.109375 to 0.109375
- dir_offsets: int32 [9], replicated, may hold values from 0 to 1536, as said below
- trans_src: int32 [4, 48, 48], P('region'), may hold values from -1 to 95, as said below
- trans_tid: int32 [4, 48, 48], P('region'), may hold values from 0 to 315
- near_src: int32 [4, 48, 27], P('region', 'dir'), may hold values from -1 to 71, as said below
Outputs:
- scattered: bfloat16 [4, 48, 128, 256], P('region', 'dir')
Inputs may be any that keep to these rules, and one draw needn't show every extreme that they name: dir_offsets starts at 0, ends at 1536 and rises; every band holds 96 to 288 direction samples, and some band holds exactly 288. `trans_src`: in each box's list the non-empty slots come first and name distinct boxes; a list holds 24 to 48 of them, and some list is full. `near_src`: each box's list starts with the box itself, then names distinct other boxes, then empty slots; a list holds 13 to 27 non-empty slots, and some list is full.
All inputs are finite; a program needn't handle non-finite values.
Results may differ from a plain program's by a relative error of at most 0.005.
Values may be sent and summed in bfloat16 or wider, within the bound.
No kernel may reach another device: no remote copies, remote signals or barrier semaphores. Data moves between devices by JAX's collectives and lax.ppermute only.
A program may use at most 192 MiB of HBM per device.

v0:
```python
import functools

import jax
import jax.numpy as jnp
from jax import lax
from jax.experimental import pallas as pl
from jax.experimental.pallas import tpu as pltpu
from jax.sharding import PartitionSpec as P

BF16, F32, I32 = jnp.bfloat16, jnp.float32, jnp.int32
NT_DIMS = (((1,), (1,)), ((), ()))
LANES = 128
ROWS = 8
UNROLL = 16
TAIL = 4
GROUP = 4
MIB = 2**20


def pad_to(size, tile):
    return -(-size // tile) * tile


def whole(memory_space):
    return pl.BlockSpec(memory_space=memory_space)


def lookup(parts, hot):
    return lax.dot_general(parts.astype(F32).astype(BF16), hot.astype(BF16), NT_DIMS, preferred_element_type=F32).astype(I32)


def fill_operators(low, high, used_ref, rows_ref, weighted_ref, rad_ref, out_ref, list_ref):
    def note(n, count):
        list_ref[count] = n
        return count + (used_ref[0, n] > 0).astype(I32)

    count = lax.fori_loop(low, high, note, 0, unroll=8)
    for u in range(TAIL):
        list_ref[count + u] = list_ref[jnp.maximum(count - 1, 0)]

    def step(at, wide):
        for u in range(wide):
            n = list_ref[at + u]
            row = rows_ref[pl.ds(n - low, 1), :].astype(BF16)
            product = weighted_ref[...] * row
            out_ref[n] = jnp.dot(product, rad_ref[...], preferred_element_type=F32).astype(BF16)

    def main_step(i, carry):
        step(i * UNROLL, UNROLL)
        return carry

    def tail_step(i, carry):
        step(main * UNROLL + i * TAIL, TAIL)
        return carry

    main = count // UNROLL
    lax.fori_loop(0, main, main_step, 0)
    lax.fori_loop(0, (count - main * UNROLL + TAIL - 1) // TAIL, tail_step, 0)


def first_kernel(
    half,
    boxes,
    halo,
    region_boxes,
    off_ref,
    src_hbm,
    tid_hbm,
    table_hbm,
    recv_hbm,
    rad_hbm,
    t_ref,
    weighted_ref,
    rad_ref,
    rows_ref,
    used_ref,
    cls_ref,
    src_ref,
    tid_ref,
    table_ref,
    recv_ref,
    low_ref,
    used_smem,
    list_ref,
    sems,
):
    pairs = [(src_hbm, src_ref), (tid_hbm, tid_ref), (recv_hbm, recv_ref), (table_hbm, table_ref), (rad_hbm, rad_ref)]
    copies = [pltpu.make_async_copy(a, b, sems.at[i]) for i, (a, b) in enumerate(pairs)]
    for copy in copies:
        copy.start()
    classes = table_ref.shape[0]
    directions = recv_ref.shape[1]
    position = lax.broadcasted_iota(I32, (1, directions), 1)
    band_size = jnp.ones((1, directions), I32)
    bands = off_ref.shape[0] - 1
    for d in range(bands):
        start, end = off_ref[d], off_ref[d + 1]
        band_size = jnp.where((position >= start) & (position < end), end - start, band_size)
    weight = directions / (bands * band_size.astype(F32))

    me = lax.axis_index("dir")
    slots = src_ref.shape[2]
    width = cls_ref.shape[1]
    used_width = used_ref.shape[1]
    ext_at = lax.broadcasted_iota(I32, (width, slots), 0)
    class_at = lax.broadcasted_iota(I32, (used_width, slots), 0)
    row_at = lax.broadcasted_iota(I32, (ROWS, slots), 0)
    out_row = lax.broadcasted_iota(I32, cls_ref.shape, 0)
    seen = jnp.zeros((used_width, slots), F32)
    cls = jnp.full(cls_ref.shape, classes, I32)
    copies[0].wait()
    copies[1].wait()
    for j in range(2 * boxes):
        target = (me if j < boxes else me ^ 1) * boxes + j % boxes
        src = src_ref[0, pl.ds(target, 1), :]
        tid = tid_ref[0, pl.ds(target, 1), :]
        owner = (src - halo + region_boxes) // boxes
        here = (src >= 0) & (((owner ^ me) & 1) == 0)
        seen = jnp.where((class_at == tid) & here, 1.0, seen)
        parts = jnp.where(row_at == 0, tid // 16, jnp.where(row_at == 1, tid % 16, 1))
        found = lookup(parts, jnp.where(ext_at == src, 1.0, 0.0))
        value = jnp.where(found[2:3] > 0, found[0:1] * 16 + found[1:2], classes)
        cls = jnp.where(out_row == j, value, cls)
    used_ref[...] = lookup(jnp.ones((ROWS, slots), I32), seen)
    cls_ref[...] = cls
    to_smem = pltpu.make_async_copy(used_ref, used_smem, sems.at[len(pairs)])
    to_smem.start()
    copies[2].wait()
    weighted_ref[...] = (recv_ref[...].astype(F32) * weight).astype(BF16)
    copies[3].wait()
    low_ref[...] = table_ref[:half, :].astype(F32)
    rows_ref[...] = table_ref[half:, :].astype(F32)
    copies[4].wait()
    to_smem.wait()
    fill_operators(0, half, used_smem, low_ref, weighted_ref, rad_ref, t_ref, list_ref)


def second_kernel(
    half,
    near_shift,
    used_ref,
    rows_ref,
    weighted_ref,
    rad_ref,
    near_src_ref,
    near_src_other_ref,
    near_hbm,
    near_other_hbm,
    low_ref,
    t_ref,
    near_ref,
    near_map_ref,
    list_ref,
    sems,
):
    boxes, near_slots = near_hbm.shape[1:3]
    copies = []
    for i, array in enumerate((near_hbm, near_other_hbm)):
        for j in range(boxes):
            row = i * boxes + j
            copies.append(
                pltpu.make_async_copy(array.at[0, j], near_ref.at[row, pl.ds(0, near_slots)], sems.at[row])
            )
            copies[-1].start()
    copies.append(pltpu.make_async_copy(low_ref, t_ref.at[pl.ds(0, half)], sems.at[2 * boxes]))
    copies[-1].start()
    t_ref[t_ref.shape[0] - 1] = jnp.zeros(t_ref.shape[1:], BF16)
    for row in range(2 * boxes):
        near_ref[row, near_slots] = jnp.zeros(near_ref.shape[2:], BF16)
    width = near_map_ref.shape[1]
    near_at = lax.broadcasted_iota(I32, (width, near_slots), 0)
    row_at = lax.broadcasted_iota(I32, (ROWS, near_slots), 0)
    lane_at = lax.broadcasted_iota(I32, (ROWS, near_slots), 1)
    out_row = lax.broadcasted_iota(I32, near_map_ref.shape, 0)
    near_map = jnp.full(near_map_ref.shape, near_slots, I32)
    for j in range(2 * boxes):
        near = (near_src_ref if j < boxes else near_src_other_ref)[0, j % boxes : j % boxes + 1, :]
        found = lookup(jnp.where(row_at == 0, lane_at, 1), jnp.where((near_at == near + near_shift) & (near >= 0), 1.0, 0.0))
        value = jnp.where(found[1:2] > 0, found[0:1], near_slots)
        near_map = jnp.where(out_row == j, value, near_map)
    near_map_ref[...] = near_map
    fill_operators(half, half + rows_ref.shape[0], used_ref, rows_ref, weighted_ref, rad_ref, t_ref, list_ref)
    for copy in copies:
        copy.wait()


def apply_kernel(places, boxes, halo, first_call, last_call, cls_ref, near_map_ref, t_ref, near_ref, *rest):
    source_refs = rest[: sum(parts for _, _, parts in places)]
    rest = rest[len(source_refs) :]
    if not first_call:
        sum_ref, *rest = rest
    if last_call:
        own_ref, other_ref, *lhs_refs = rest
    else:
        out_ref, *lhs_refs = rest
    me = lax.axis_index("dir")
    region_boxes = boxes * lax.axis_size("dir")
    size = near_ref.shape[2]
    targets = near_ref.shape[0]
    at = 0
    total = None
    for step, (rim, mask, parts) in enumerate(places):
        lhs_ref = lhs_refs[step % len(lhs_refs)]
        owner = me ^ mask
        base = owner * boxes + halo
        if rim:
            base = base + jnp.where(owner * boxes >= halo, -region_boxes, region_boxes)
        for j in range(targets):
            for b in range(boxes):
                block = t_ref[cls_ref[j, base + b]] + near_ref[j, near_map_ref[j, base + b]]
                lhs_ref[j * size : (j + 1) * size, b * size : (b + 1) * size] = block
        values = [ref[...] for ref in source_refs[at : at + parts]]
        at += parts
        rhs = values[0] if parts == 1 else jnp.concatenate(values, 0)
        rhs = rhs.reshape(boxes * size, rhs.shape[-1])
        added = jnp.dot(lhs_ref[...], rhs, preferred_element_type=F32).reshape(targets, size, rhs.shape[-1])
        if step == 0:
            total = added if first_call else sum_ref[...] + added
        else:
            total = (total if last_call else out_ref[...]) + added
        if not last_call:
            out_ref[...] = total
    if last_call:
        own_ref[...] = total[:boxes]
        other_ref[...] = total[boxes:].astype(BF16)


def shards(
    currents,
    radiate,
    receive,
    transfer_table,
    near_blocks,
    dir_offsets,
    trans_src,
    trans_tid,
    near_src,
):
    dir_count = lax.axis_size("dir")
    region_count = lax.axis_size("region")
    own = currents[0]
    boxes, unknowns, incidences = own.shape
    near_slots = near_src.shape[2]
    region_boxes = boxes * dir_count
    halo = region_boxes // 2
    near_halo = region_boxes // 4
    classes, directions = transfer_table.shape
    half = pad_to(classes // 2, 16)
    top = dir_count // 2
    inner = range(2, top, 2)
    split = boxes // 2
    targets = 2 * boxes

    def partner(array, mask):
        return lax.ppermute(array, "dir", [(i, i ^ mask) for i in range(dir_count)])

    along = []
    for i in range(dir_count):
        for z in range(region_count):
            target = z + 1 if i >= top else z - 1
            if 0 <= target < region_count:
                along.append((i * region_count + z, i * region_count + target))

    def beyond(array):
        return lax.ppermute(array, ("dir", "region"), along)

    def pinned(array):
        return pltpu.with_memory_space_constraint(array, pltpu.VMEM)

    def in_hbm(array):
        return pltpu.with_memory_space_constraint(array, pltpu.HBM)

    width = pad_to(region_boxes + 2 * halo, LANES)
    used_width = pad_to(classes, LANES)
    map_shape = (pad_to(targets, ROWS), width)
    table_shape = (classes + 1, unknowns, unknowns)
    low_shape = (half, unknowns, unknowns)
    vmem, smem, hbm = whole(pltpu.VMEM), whole(pltpu.SMEM), whole(pltpu.HBM)
    operator_cost = pl.CostEstimate(
        flops=classes * unknowns * unknowns * directions, bytes_accessed=MIB, transcendentals=0
    )

    field = {0: own}
    rim = {}
    for m in inner:
        field[m] = partner(own, m)
    field[top] = partner(own, top)
    rim[0] = beyond(own)
    near_src_other = partner(near_src, 1)
    near_other = partner(near_blocks, 1)
    table, weighted, rad_here, rows, used, cls = pl.pallas_call(
        functools.partial(first_kernel, half, boxes, halo, region_boxes),
        in_specs=[smem] + [hbm] * 5,
        out_specs=[vmem] * 6,
        out_shape=(
            pltpu.VMEM(low_shape, BF16),
            pltpu.VMEM((unknowns, directions), BF16),
            pltpu.VMEM((directions, unknowns), BF16),
            pltpu.VMEM((classes - half, directions), F32),
            pltpu.VMEM((ROWS, used_width), I32),
            pltpu.VMEM(map_shape, I32),
        ),
        scratch_shapes=[
            pltpu.VMEM(trans_src.shape, I32),
            pltpu.VMEM(trans_tid.shape, I32),
            pltpu.VMEM(transfer_table.shape, BF16),
            pltpu.VMEM(receive.shape, BF16),
            pltpu.VMEM((half, directions), F32),
            pltpu.SMEM((ROWS, used_width), I32),
            pltpu.SMEM((pad_to(classes, 8) + UNROLL,), I32),
            pltpu.SemaphoreType.DMA((6,)),
        ],
        compiler_params=pltpu.CompilerParams(vmem_limit_bytes=8 * MIB),
        cost_estimate=operator_cost,
    )(dir_offsets, *[in_hbm(a) for a in (trans_src, trans_tid, transfer_table, receive, radiate)])

    tied = lax.optimization_barrier((table, [field[m] for m in inner], field[top], rim[0]))
    table, inner_fields, field[top], rim[0] = tied
    for m, value in zip(inner, inner_fields):
        field[m] = value
    for m in inner:
        field[top + m] = partner(field[top], m)
    rim[top] = partner(rim[0], top)
    for m in inner:
        rim[m] = beyond(field[m])

    table, near_here, near_map = pl.pallas_call(
        functools.partial(second_kernel, half, halo - near_halo),
        in_specs=[smem] + [vmem] * 5 + [hbm] * 2 + [vmem],
        out_specs=[vmem] * 3,
        out_shape=(
            pltpu.VMEM(table_shape, BF16),
            pltpu.VMEM((targets, near_slots + 1, unknowns, unknowns), BF16),
            pltpu.VMEM(map_shape, I32),
        ),
        scratch_shapes=[
            pltpu.SMEM((pad_to(classes, 8) + UNROLL,), I32),
            pltpu.SemaphoreType.DMA((targets + 1,)),
        ],
        compiler_params=pltpu.CompilerParams(vmem_limit_bytes=8 * MIB),
        cost_estimate=operator_cost,
    )(used, pinned(rows), pinned(weighted), pinned(rad_here), near_src, near_src_other, in_hbm(near_blocks), near_other, pinned(table))

    def apply(places, total, last):
        if len(places) > GROUP:
            total = apply(places[:GROUP], total, False)
            return apply(places[GROUP:], total, last)
        parts = [part for _, _, group in places for part in group]
        args = [cls, near_map, pinned(table), pinned(near_here)] + [pinned(part) for part in parts]
        args += [] if total is None else [pinned(total)]
        specs = [smem] * 2 + [vmem] * (len(args) - 2)
        layout = [(beyond_it, mask, len(group)) for beyond_it, mask, group in places]
        shape = (boxes, unknowns, incidences)
        whole_shape = (targets, unknowns, incidences)
        return pl.pallas_call(
            functools.partial(apply_kernel, layout, boxes, halo, total is None, last),
            in_specs=specs,
            out_specs=[vmem, vmem] if last else vmem,
            out_shape=(pltpu.VMEM(shape, F32), pltpu.VMEM(shape, BF16)) if last else pltpu.VMEM(whole_shape, F32),
            input_output_aliases={} if last or total is None else {len(args) - 1: 0},
            scratch_shapes=[pltpu.VMEM((targets * unknowns, boxes * unknowns), BF16)] * 2,
            compiler_params=pltpu.CompilerParams(vmem_limit_bytes=14 * MIB),
            cost_estimate=pl.CostEstimate(
                flops=4 * len(places) * (boxes * unknowns) ** 2 * incidences, bytes_accessed=MIB, transcendentals=0
            ),
        )(*args)

    early = [(False, m, [field[m]]) for m in (0, *inner, top)] + [(True, 0, [rim[0]])]
    total = apply(early, None, False)

    tied = lax.optimization_barrier(
        (total, [field[top + m] for m in inner], [rim[m] for m in inner], rim[top])
    )
    total, far_fields, inner_rims, rim[top] = tied
    for m, value, other in zip(inner, far_fields, inner_rims):
        field[top + m], rim[m] = value, other
    last = {m: [partner(rim[top][:split], m), partner(rim[m][split:], top)] for m in inner}
    middle = [(False, top + m, [field[top + m]]) for m in inner]
    middle += [(True, m, [rim[m]]) for m in (*inner, top)]
    total = apply(middle, total, False)
    here, there = apply([(True, top + m, last[m]) for m in inner], total, True)
    return (here + partner(there, 1).astype(F32)).astype(BF16)[None]


def solution(mesh):
    placed = (
        P("region", "dir", None, None),
        P(),
        P(),
        P(),
        P("region", "dir", None, None, None),
        P(),
        P("region", None, None),
        P("region", None, None),
        P("region", "dir", None),
    )
    return jax.shard_map(
        shards,
        mesh=mesh,
        in_specs=placed,
        out_specs=P("region", "dir", None, None),
        check_vma=False,
    )
```

profile of v0, /device:TPU:0, one launch (start us, length us, event | category | flops | bytes accessed | tf_op | source)
XLA Modules:
  0.0 58.5 jit_solution(11064911901001948335)
XLA Ops:
  0.0 0.5 collective-permute-start.1
  0.5 2.5 %collective-permute-start.2 = (bf16[6,128,256]{2,1,0:T(8,128)(2,1)}, bf16[6,128,256]{2,1,0:T(8,128)(2,1)S(1)}, u32[]{:S(2)}, u32[]{:S(2)}) collective-permute-start(bf16[6,128,256]{2,1,0:T(8,128)(2,1)} %bitcast.3), channel_id=1, source_target_pairs={{0,8},{4,12},{8,0},{12,4},{16,24},{20,28},{24,16},{28,20},{1,9},{5... | collective-permute-start | bytes 1179656 | tf_op jit(solution)/shard_map/ppermute | solution.py:255
  2.9 1.5 %collective-permute-start.3 = (bf16[6,128,256]{2,1,0:T(8,128)(2,1)}, bf16[6,128,256]{2,1,0:T(8,128)(2,1)S(1)}, u32[]{:S(2)}, u32[]{:S(2)}) collective-permute-start(bf16[6,128,256]{2,1,0:T(8,128)(2,1)} %bitcast.4), channel_id=1, source_target_pairs={{0,16},{4,20},{8,24},{12,28},{16,0},{20,4},{24,8},{28,12},{1,17},{... | collective-permute-start | bytes 1179656 | tf_op jit(solution)/shard_map/ppermute | solution.py:255
  4.5 1.3 %collective-permute-start.4 = (bf16[6,128,256]{2,1,0:T(8,128)(2,1)}, bf16[6,128,256]{2,1,0:T(8,128)(2,1)S(1)}, u32[]{:S(2)}, u32[]{:S(2)}) collective-permute-start(bf16[6,128,256]{2,1,0:T(8,128)(2,1)} %bitcast.5), channel_id=1, source_target_pairs={{1,0},{2,1},{3,2},{5,4},{6,5},{7,6},{9,8},{10,9},{11,10},{13,12},{... | collective-permute-start | bytes 1179656 | tf_op jit(solution)/shard_map/ppermute | solution.py:265
  5.8 0.7 %copy.12.near_src_ref = s32[1,6,27]{2,1,0:T(8,128)S(1)} copy(s32[1,6,27]{2,0,1:T(1,128)} %param.17) | data formatting | bytes 1296 | tf_op args[8]
  6.4 0.0 collective-permute-start
  6.4 0.0 copy-start.1
  6.4 0.7 %copy-done.1 = s32[9]{0:T(128)S(1)} copy-done((s32[9]{0:T(128)S(1)}, s32[9]{0:T(128)}, u32[]{:S(2)}) %copy-start.1) | copy-done | bytes 60
  7.1 11.9 %shard_map.91 = (bf16[160,128,128]{2,1,0:T(8,128)(2,1)S(1)}, bf16[128,1536]{1,0:T(8,128)(2,1)S(1)}, bf16[1536,128]{1,0:T(8,128)(2,1)S(1)}, f32[156,1536]{1,0:T(8...) custom-call(s32[9]{0:T(128)S(1)} %copy-done.1, s32[1,48,48]{2,1,0:T(8,128)} %src_hbm.1, s32[1,48,48]{2,1,0:T(8,128)} %tid_hbm.1, ...), custom_call_target="tpu_custom_call" | custom-call | flops 7952400384 | bytes 1048576 | tf_op jit(solution)/shard_map/pallas_call | solution.py:291
  19.1 0.0 collective-permute-done.2.rest_1_
  19.1 0.0 collective-permute-done.3.rest_2_
  19.1 0.0 collective-permute-done.4.rest_3_
  19.1 1.8 %collective-permute-start.5 = (bf16[6,128,256]{2,1,0:T(8,128)(2,1)S(1)}, bf16[6,128,256]{2,1,0:T(8,128)(2,1)S(1)}, u32[]{:S(2)}, u32[]{:S(2)}) collective-permute-start(bf16[6,128,256]{2,1,0:T(8,128)(2,1)S(1)} %collective-permute-done.3.rest_2_), channel_id=1, source_target_pairs={{0,8},{4,12},{8,0},{12,4},{16,24},{20,28},{24,16},{28,20},{1,9},{5... | collective-permute-start | bytes 1179656 | tf_op jit(solution)/shard_map/ppermute | solution.py:255
  20.8 1.3 %collective-permute-start.6 = (bf16[6,128,256]{2,1,0:T(8,128)(2,1)S(1)}, bf16[6,128,256]{2,1,0:T(8,128)(2,1)S(1)}, u32[]{:S(2)}, u32[]{:S(2)}) collective-permute-start(bf16[6,128,256]{2,1,0:T(8,128)(2,1)S(1)} %collective-permute-done.2.rest_1_), channel_id=1, source_target_pairs={{1,0},{2,1},{3,2},{5,4},{6,5},{7,6},{9,8},{10,9},{11,10},{13,12},{... | collective-permute-start | bytes 1179656 | tf_op jit(solution)/shard_map/ppermute | solution.py:265
  22.1 5.0 %collective-permute-start.7 = (bf16[6,128,256]{2,1,0:T(8,128)(2,1)S(1)}, bf16[6,128,256]{2,1,0:T(8,128)(2,1)S(1)}, u32[]{:S(2)}, u32[]{:S(2)}) collective-permute-start(bf16[6,128,256]{2,1,0:T(8,128)(2,1)S(1)} %collective-permute-done.4.rest_3_), channel_id=1, source_target_pairs={{0,16},{4,20},{8,24},{12,28},{16,0},{20,4},{24,8},{28,12},{1,17},{... | collective-permute-start | bytes 1179656 | tf_op jit(solution)/shard_map/ppermute | solution.py:255
  27.1 0.0 collective-permute-done.near_src_other_ref
  27.1 0.0 collective-permute-done.1.near_other_hbm
  27.1 13.3 %shard_map.92 = (bf16[317,128,128]{2,1,0:T(8,128)(2,1)S(1)}, bf16[12,28,128,128]{3,2,1,0:T(8,128)(2,1)S(1)}, s32[16,128]{1,0:T(8,128)S(1)}) custom-call(s32[8,384]{1,0:T(8,128)S(1)} %get-tuple-element.25.used_ref, f32[156,1536]{1,0:T(8,128)S(1)} %get-tuple-element.26.rows_ref, bf16[128,1536]{1,0:T(8,128)(2,1)S(1)} %get-tuple-element.27.weighted_ref, ...), custom_call_target="tpu_custom_call" | custom-call | flops 7952400384 | bytes 1048576 | tf_op jit(solution)/shard_map/pallas_call | solution.py:327
  40.4 0.0 copy-done
  40.4 5.4 %shard_map.93.rest_3_ = f32[12,128,256]{2,1,0:T(8,128)S(1)} custom-call(s32[16,128]{1,0:T(8,128)S(1)} %get-tuple-element.24.cls_ref, s32[16,128]{1,0:T(8,128)S(1)} %get-tuple-element.31.near_map_ref, bf16[317,128,128]{2,1,0:T(8,128)(2,1)S(1)} %get-tuple-element.32.t_ref, bf16[12,28,128,128]{3,2,1,0:T(8,128)(2,1)S(1)} %get-tuple-element.33.near_ref, ...), custom_call_target="tpu_custom_call" | custom-call | flops 2415919104 | bytes 1048576 | tf_op jit(solution)/shard_map/pallas_call | solution.py:355
  45.8 0.0 collective-permute-done.5.rest_0_
  45.8 0.0 collective-permute-done.6.rest_1_
  45.8 0.0 collective-permute-done.7.rest_2_
  45.8 1.7 %collective-permute-start.8 = (bf16[3,128,256]{2,1,0:T(8,128)(2,1)S(1)}, bf16[3,128,256]{2,1,0:T(8,128)(2,1)S(1)}, u32[]{:S(2)}, u32[]{:S(2)}) collective-permute-start(bf16[3,128,256]{2,1,0:T(8,128)(2,1)S(1)} %slice.6), channel_id=1, source_target_pairs={{0,8},{4,12},{8,0},{12,4},{16,24},{20,28},{24,16},{28,20},{1,9},{5... | collective-permute-start | bytes 589832 | tf_op jit(solution)/shard_map/ppermute | solution.py:255
  47.5 0.1 collective-permute-start.9
  47.6 4.4 %shard_map.94.rest_2_ = f32[12,128,256]{2,1,0:T(8,128)S(1)} custom-call(s32[16,128]{1,0:T(8,128)S(1)} %get-tuple-element.24.cls_ref, s32[16,128]{1,0:T(8,128)S(1)} %get-tuple-element.31.near_map_ref, bf16[317,128,128]{2,1,0:T(8,128)(2,1)S(1)} %get-tuple-element.32.t_ref, ...), custom_call_target="tpu_custom_call", output_to_operand_aliasing={{}: (7, {})} | custom-call | flops 1811939328 | bytes 1048576 | tf_op jit(solution)/shard_map/pallas_call | solution.py:355
  52.0 0.2 collective-permute-done.8.rest_0_
  52.3 1.5 %collective-permute-done.9.rest_1_ = bf16[3,128,256]{2,1,0:T(8,128)(2,1)S(1)} collective-permute-done((bf16[3,128,256]{2,1,0:T(8,128)(2,1)S(1)}, bf16[3,128,256]{2,1,0:T(8,128)(2,1)S(1)}, u32[]{:S(2)}, u32[]{:S(2)}) %collective-permute-start.9) | collective-permute-done | bytes 196640 | tf_op jit(solution)/shard_map/ppermute | solution.py:255
  53.8 2.0 %shard_map.95 = (f32[6,128,256]{2,1,0:T(8,128)S(1)}, bf16[6,128,256]{2,1,0:T(8,128)(2,1)S(1)}) custom-call(s32[16,128]{1,0:T(8,128)S(1)} %get-tuple-element.24.cls_ref, s32[16,128]{1,0:T(8,128)S(1)} %get-tuple-element.31.near_map_ref, bf16[317,128,128]{2,1,0:T(8,128)(2,1)S(1)} %get-tuple-element.32.t_ref, ...), custom_call_target="tpu_custom_call" | custom-call | flops 603979776 | bytes 1048576 | tf_op jit(solution)/shard_map/pallas_call | solution.py:355
  55.8 0.1 collective-permute-start.10
  55.9 1.7 %collective-permute-done.10 = bf16[6,128,256]{2,1,0:T(8,128)(2,1)S(1)} collective-permute-done((bf16[6,128,256]{2,1,0:T(8,128)(2,1)S(1)}, bf16[6,128,256]{2,1,0:T(8,128)(2,1)S(1)}, u32[]{:S(2)}, u32[]{:S(2)}) %collective-permute-start.10) | collective-permute-done | bytes 393248 | tf_op jit(solution)/shard_map/ppermute | solution.py:255
  57.6 0.8 %fusion = bf16[1,6,128,256]{3,2,1,0:T(8,128)(2,1)} fusion(f32[6,128,256]{2,1,0:T(8,128)S(1)} %get-tuple-element.41, bf16[6,128,256]{2,1,0:T(8,128)(2,1)S(1)} %collective-permute-done.10), kind=kLoop, calls=%fused_computation.1 | loop fusion | flops 589824 | bytes 1572864 | tf_op jit(solution)/shard_map/broadcast_in_dim | solution.py:382
  (3 shorter events, 0.0 us)
Async XLA Ops:
  0.0 27.1 %collective-permute-start.1 = (bf16[1,6,27,128,128]{4,3,2,1,0:T(8,128)(2,1)}, bf16[1,6,27,128,128]{4,3,2,1,0:T(8,128)(2,1)S(1)}, u32[]{:S(2)}, u32[]{:S(2)}) collective-permute-start(bf16[1,6,27,128,128]{4,3,2,1,0:T(8,128)(2,1)} %near_hbm.1), channel_id=1, source_target_pairs={{0,4},{4,0},{8,12},{12,8},{16,20},{20,16},{24,28},{28,24},{1,5},{5... | collective-permute-start | bytes 15925256 | tf_op jit(solution)/shard_map/ppermute | solution.py:255
  0.5 18.6 %collective-permute-start.2 = (bf16[6,128,256]{2,1,0:T(8,128)(2,1)}, bf16[6,128,256]{2,1,0:T(8,128)(2,1)S(1)}, u32[]{:S(2)}, u32[]{:S(2)}) collective-permute-start(bf16[6,128,256]{2,1,0:T(8,128)(2,1)} %bitcast.3), channel_id=1, source_target_pairs={{0,8},{4,12},{8,0},{12,4},{16,24},{20,28},{24,16},{28,20},{1,9},{5... | collective-permute-start | bytes 1179656 | tf_op jit(solution)/shard_map/ppermute | solution.py:255
  2.9 16.1 %collective-permute-start.3 = (bf16[6,128,256]{2,1,0:T(8,128)(2,1)}, bf16[6,128,256]{2,1,0:T(8,128)(2,1)S(1)}, u32[]{:S(2)}, u32[]{:S(2)}) collective-permute-start(bf16[6,128,256]{2,1,0:T(8,128)(2,1)} %bitcast.4), channel_id=1, source_target_pairs={{0,16},{4,20},{8,24},{12,28},{16,0},{20,4},{24,8},{28,12},{1,17},{... | collective-permute-start | bytes 1179656 | tf_op jit(solution)/shard_map/ppermute | solution.py:255
  4.5 14.6 %collective-permute-start.4 = (bf16[6,128,256]{2,1,0:T(8,128)(2,1)}, bf16[6,128,256]{2,1,0:T(8,128)(2,1)S(1)}, u32[]{:S(2)}, u32[]{:S(2)}) collective-permute-start(bf16[6,128,256]{2,1,0:T(8,128)(2,1)} %bitcast.5), channel_id=1, source_target_pairs={{1,0},{2,1},{3,2},{5,4},{6,5},{7,6},{9,8},{10,9},{11,10},{13,12},{... | collective-permute-start | bytes 1179656 | tf_op jit(solution)/shard_map/ppermute | solution.py:265
  6.4 20.7 %collective-permute-start = (s32[1,6,27]{2,1,0:T(8,128)S(1)}, s32[1,6,27]{2,1,0:T(8,128)S(1)}, u32[]{:S(2)}, u32[]{:S(2)}) collective-permute-start(s32[1,6,27]{2,1,0:T(8,128)S(1)} %copy.12.near_src_ref), channel_id=1, source_target_pairs={{0,4},{4,0},{8,12},{12,8},{16,20},{20,16},{24,28},{28,24},{1,5},{5... | collective-permute-start | bytes 1952 | tf_op jit(solution)/shard_map/ppermute | solution.py:255
  6.4 0.7 %copy-start.1 = (s32[9]{0:T(128)S(1)}, s32[9]{0:T(128)}, u32[]{:S(2)}) copy-start(s32[9]{0:T(128)} %off_ref.1) | copy-start | bytes 112
  19.1 26.7 %collective-permute-start.5 = (bf16[6,128,256]{2,1,0:T(8,128)(2,1)S(1)}, bf16[6,128,256]{2,1,0:T(8,128)(2,1)S(1)}, u32[]{:S(2)}, u32[]{:S(2)}) collective-permute-start(bf16[6,128,256]{2,1,0:T(8,128)(2,1)S(1)} %collective-permute-done.3.rest_2_), channel_id=1, source_target_pairs={{0,8},{4,12},{8,0},{12,4},{16,24},{20,28},{24,16},{28,20},{1,9},{5... | collective-permute-start | bytes 1179656 | tf_op jit(solution)/shard_map/ppermute | solution.py:255
  20.8 24.9 %collective-permute-start.6 = (bf16[6,128,256]{2,1,0:T(8,128)(2,1)S(1)}, bf16[6,128,256]{2,1,0:T(8,128)(2,1)S(1)}, u32[]{:S(2)}, u32[]{:S(2)}) collective-permute-start(bf16[6,128,256]{2,1,0:T(8,128)(2,1)S(1)} %collective-permute-done.2.rest_1_), channel_id=1, source_target_pairs={{1,0},{2,1},{3,2},{5,4},{6,5},{7,6},{9,8},{10,9},{11,10},{13,12},{... | collective-permute-start | bytes 1179656 | tf_op jit(solution)/shard_map/ppermute | solution.py:265
  22.1 23.7 %collective-permute-start.7 = (bf16[6,128,256]{2,1,0:T(8,128)(2,1)S(1)}, bf16[6,128,256]{2,1,0:T(8,128)(2,1)S(1)}, u32[]{:S(2)}, u32[]{:S(2)}) collective-permute-start(bf16[6,128,256]{2,1,0:T(8,128)(2,1)S(1)} %collective-permute-done.4.rest_3_), channel_id=1, source_target_pairs={{0,16},{4,20},{8,24},{12,28},{16,0},{20,4},{24,8},{28,12},{1,17},{... | collective-permute-start | bytes 1179656 | tf_op jit(solution)/shard_map/ppermute | solution.py:255
  27.1 13.3 %copy-start = (bf16[1,6,128,256]{3,2,1,0:T(8,128)(2,1)S(1)}, bf16[1,6,128,256]{3,2,1,0:T(8,128)(2,1)}, u32[]{:S(2)}) copy-start(bf16[1,6,128,256]{3,2,1,0:T(8,128)(2,1)} %param.9) | copy-start | bytes 1179652
  45.8 6.4 %collective-permute-start.8 = (bf16[3,128,256]{2,1,0:T(8,128)(2,1)S(1)}, bf16[3,128,256]{2,1,0:T(8,128)(2,1)S(1)}, u32[]{:S(2)}, u32[]{:S(2)}) collective-permute-start(bf16[3,128,256]{2,1,0:T(8,128)(2,1)S(1)} %slice.6), channel_id=1, source_target_pairs={{0,8},{4,12},{8,0},{12,4},{16,24},{20,28},{24,16},{28,20},{1,9},{5... | collective-permute-start | bytes 589832 | tf_op jit(solution)/shard_map/ppermute | solution.py:255
  47.5 6.3 %collective-permute-start.9 = (bf16[3,128,256]{2,1,0:T(8,128)(2,1)S(1)}, bf16[3,128,256]{2,1,0:T(8,128)(2,1)S(1)}, u32[]{:S(2)}, u32[]{:S(2)}) collective-permute-start(bf16[3,128,256]{2,1,0:T(8,128)(2,1)S(1)} %slice.7), channel_id=1, source_target_pairs={{0,16},{4,20},{8,24},{12,28},{16,0},{20,4},{24,8},{28,12},{1,17},{... | collective-permute-start | bytes 589832 | tf_op jit(solution)/shard_map/ppermute | solution.py:255
  55.8 1.8 %collective-permute-start.10 = (bf16[6,128,256]{2,1,0:T(8,128)(2,1)S(1)}, bf16[6,128,256]{2,1,0:T(8,128)(2,1)S(1)}, u32[]{:S(2)}, u32[]{:S(2)}) collective-permute-start(bf16[6,128,256]{2,1,0:T(8,128)(2,1)S(1)} %get-tuple-element.42), channel_id=1, source_target_pairs={{0,4},{4,0},{8,12},{12,8},{16,20},{20,16},{24,28},{28,24},{1,5},{5... | collective-permute-start | bytes 1179656 | tf_op jit(solution)/shard_map/ppermute | solution.py:255
where the time goes:
time: 59 us; the launch traced here: 58.5 us
  Pallas kernels  37 us (63%)
  starting transfers between devices  15.6 us (26%)
  waiting for transfers between devices  3.52 us (6%)
  local copies, waits for them, and re-layouts  1.37 us (2%)
  other arithmetic  0.83 us (1%)
    pallas_call x1, Pallas kernels, shards(): pl.pallas_call(functools.partial(second_kernel, half, halo - near_halo),...  13.3 us
    ppermute x9, starting transfers between devices, partner(): return lax.ppermute(array, 'dir', [(i, i ^ mask) for i in range(dir_count)])  13 us
    pallas_call x1, Pallas kernels, shards(): pl.pallas_call(functools.partial(first_kernel, half, boxes, halo, region_...  11.9 us
    pallas_call x3, Pallas kernels, apply(): pl.pallas_call(functools.partial(apply_kernel, layout, boxes, halo, total...  11.8 us
    ppermute x9, waiting for transfers between devices, partner(): return lax.ppermute(array, 'dir', [(i, i ^ mask) for i in range(dir_count)])  3.51 us
    ppermute x2, starting transfers between devices, beyond(): return lax.ppermute(array, ('dir', 'region'), along)  2.56 us
    unnamed x5, local copies, waits for them, and re-layouts  1.35 us
  transfers between devices with their start and end apart: 11, of which 3 were waited for; matrix products, arithmetic and copies ran while one was open for 1% of the time, Pallas kernels for 60%

commit v1 on v0

v1 whole, which is shorter than its diff:
```python
import functools

import jax
import jax.numpy as jnp
from jax import lax
from jax.experimental import pallas as pl
from jax.experimental.pallas import tpu as pltpu
from jax.sharding import PartitionSpec as P

BF16, F32, I32 = jnp.bfloat16, jnp.float32, jnp.int32
NT_DIMS = (((1,), (1,)), ((), ()))
LANES = 128
ROWS = 8
UNROLL = 16
TAIL = 4
GROUP = 8
MIB = 2**20


def pad_to(size, tile):
    return -(-size // tile) * tile


def whole(memory_space):
    return pl.BlockSpec(memory_space=memory_space)


def lookup(parts, hot):
    return lax.dot_general(parts.astype(F32).astype(BF16), hot.astype(BF16), NT_DIMS, preferred_element_type=F32).astype(I32)


def fill_operators(begin, end, list_ref, rows_ref, weighted_ref, rad_ref, out_ref):
    def step(at, wide):
        for u in range(wide):
            place = jnp.minimum(at + u, end - 1)
            row = rows_ref[pl.ds(list_ref[0, place], 1), :].astype(BF16)
            product = weighted_ref[...] * row
            out_ref[place] = jnp.dot(product, rad_ref[...], preferred_element_type=F32).astype(BF16)

    def main_step(i, carry):
        step(begin + i * UNROLL, UNROLL)
        return carry

    def tail_step(i, carry):
        step(begin + main * UNROLL + i * TAIL, TAIL)
        return carry

    count = jnp.maximum(end - begin, 0)
    main = count // UNROLL
    lax.fori_loop(0, main, main_step, 0)
    lax.fori_loop(0, (count - main * UNROLL + TAIL - 1) // TAIL, tail_step, 0)


def first_kernel(
    first_count,
    boxes,
    halo,
    region_boxes,
    off_hbm,
    src_hbm,
    tid_hbm,
    near_src_hbm,
    table_hbm,
    recv_hbm,
    rad_hbm,
    t_ref,
    weighted_ref,
    rad_ref,
    rows_ref,
    cls_ref,
    near_src_ref,
    list_ref,
    off_ref,
    src_ref,
    tid_ref,
    table_ref,
    recv_ref,
    used_ref,
    used_smem,
    sems,
):
    pairs = [
        (src_hbm, src_ref),
        (tid_hbm, tid_ref),
        (off_hbm, off_ref),
        (recv_hbm, recv_ref),
        (table_hbm, table_ref),
        (rad_hbm, rad_ref),
        (near_src_hbm, near_src_ref),
    ]
    copies = [pltpu.make_async_copy(a, b, sems.at[i]) for i, (a, b) in enumerate(pairs)]
    for copy in copies:
        copy.start()
    classes = table_ref.shape[0]
    directions = recv_ref.shape[1]
    me = lax.axis_index("dir")
    dir_count = region_boxes // boxes
    top = dir_count // 2
    slots = src_ref.shape[2]
    width = cls_ref.shape[1]
    used_width = used_ref.shape[1]
    ext_at = lax.broadcasted_iota(I32, (width, slots), 0)
    class_at = lax.broadcasted_iota(I32, (used_width, slots), 0)
    row_at = lax.broadcasted_iota(I32, (ROWS, slots), 0)
    out_row = lax.broadcasted_iota(I32, cls_ref.shape, 0)
    seen = jnp.zeros((used_width, slots), F32)
    cls = jnp.full(cls_ref.shape, classes, I32)
    copies[0].wait()
    copies[1].wait()
    for j in range(2 * boxes):
        target = (me if j < boxes else me ^ 1) * boxes + j % boxes
        src = src_ref[0, pl.ds(target, 1), :]
        tid = tid_ref[0, pl.ds(target, 1), :]
        mask = (((src - halo + region_boxes) // boxes) % dir_count) ^ me
        beyond = (src < halo) | (src >= halo + region_boxes)
        late = beyond & ((mask & top) != 0) & ((mask & (top - 2)) != 0)
        even = (mask & 1) == 0
        here = (src >= 0) & ((even | late) if j < boxes else (even & ~late))
        seen = jnp.where((class_at == tid) & here, 1.0, seen)
        parts = jnp.where(row_at == 0, tid // 16, jnp.where(row_at == 1, tid % 16, 1))
        found = lookup(parts, jnp.where(ext_at == src, 1.0, 0.0))
        value = jnp.where(found[2:3] > 0, found[0:1] * 16 + found[1:2], classes)
        cls = jnp.where(out_row == j, value, cls)
    used_ref[...] = lookup(jnp.ones((ROWS, slots), I32), seen)
    cls_ref[...] = cls
    to_smem = pltpu.make_async_copy(used_ref, used_smem, sems.at[len(pairs)])
    to_smem.start()
    copies[2].wait()
    position = lax.broadcasted_iota(I32, (1, directions), 1)
    band_size = jnp.ones((1, directions), I32)
    bands = off_ref.shape[0] - 1
    for d in range(bands):
        start, end = off_ref[d], off_ref[d + 1]
        band_size = jnp.where((position >= start) & (position < end), end - start, band_size)
    weight = directions / (bands * band_size.astype(F32))
    copies[3].wait()
    weighted_ref[...] = (recv_ref[...].astype(F32) * weight).astype(BF16)
    copies[4].wait()
    rows_ref[...] = table_ref[...].astype(F32)
    to_smem.wait()

    def note(n, count):
        list_ref[0, count] = n
        list_ref[1, n] = count
        return count + (used_smem[0, n] > 0).astype(I32)

    count = lax.fori_loop(0, classes, note, 0, unroll=8)
    list_ref[1, classes] = classes
    list_ref[0, classes + 1] = count
    copies[5].wait()
    copies[6].wait()
    fill_operators(0, jnp.minimum(count, first_count), list_ref, rows_ref, weighted_ref, rad_ref, t_ref)


def second_kernel(
    near_shift,
    list_ref,
    rows_ref,
    weighted_ref,
    rad_ref,
    near_src_ref,
    near_src_other_ref,
    near_hbm,
    near_other_hbm,
    low_ref,
    t_ref,
    near_ref,
    near_map_ref,
    sems,
):
    boxes, near_slots = near_hbm.shape[1:3]
    copies = []
    for i, array in enumerate((near_hbm, near_other_hbm)):
        for j in range(boxes):
            row = i * boxes + j
            copies.append(
                pltpu.make_async_copy(array.at[0, j], near_ref.at[row, pl.ds(0, near_slots)], sems.at[row])
            )
            copies[-1].start()
    first_count = low_ref.shape[0]
    classes = rows_ref.shape[0]
    copies.append(pltpu.make_async_copy(low_ref, t_ref.at[pl.ds(0, first_count)], sems.at[2 * boxes]))
    copies[-1].start()
    t_ref[t_ref.shape[0] - 1] = jnp.zeros(t_ref.shape[1:], BF16)
    for row in range(2 * boxes):
        near_ref[row, near_slots] = jnp.zeros(near_ref.shape[2:], BF16)
    width = near_map_ref.shape[1]
    near_at = lax.broadcasted_iota(I32, (width, near_slots), 0)
    row_at = lax.broadcasted_iota(I32, (ROWS, near_slots), 0)
    lane_at = lax.broadcasted_iota(I32, (ROWS, near_slots), 1)
    out_row = lax.broadcasted_iota(I32, near_map_ref.shape, 0)
    near_map = jnp.full(near_map_ref.shape, near_slots, I32)
    for j in range(2 * boxes):
        near = (near_src_ref if j < boxes else near_src_other_ref)[0, j % boxes : j % boxes + 1, :]
        found = lookup(jnp.where(row_at == 0, lane_at, 1), jnp.where((near_at == near + near_shift) & (near >= 0), 1.0, 0.0))
        value = jnp.where(found[1:2] > 0, found[0:1], near_slots)
        near_map = jnp.where(out_row == j, value, near_map)
    near_map_ref[...] = near_map
    fill_operators(first_count, list_ref[0, classes + 1], list_ref, rows_ref, weighted_ref, rad_ref, t_ref)
    for copy in copies:
        copy.wait()


def apply_kernel(
    places, first_row, boxes, halo, with_total, with_other, dtype, cls_ref, near_map_ref, list_ref, t_ref, near_ref, *rest
):
    source_refs, rest = rest[: sum(parts for _, _, parts in places)], rest[sum(parts for _, _, parts in places) :]
    if with_total:
        sum_ref, *rest = rest
    if with_other:
        other_ref, *rest = rest
    out_ref, total_ref, *lhs_refs = rest
    me = lax.axis_index("dir")
    region_boxes = boxes * lax.axis_size("dir")
    size = near_ref.shape[2]
    at = 0
    for step, (rim, mask, parts) in enumerate(places):
        lhs_ref = lhs_refs[step % len(lhs_refs)]
        owner = me ^ mask
        base = owner * boxes + halo
        if rim:
            base = base + jnp.where(owner * boxes >= halo, -region_boxes, region_boxes)
        for j in range(boxes):
            row = first_row + j
            for b in range(boxes):
                block = t_ref[list_ref[1, cls_ref[row, base + b]]] + near_ref[row, near_map_ref[row, base + b]]
                lhs_ref[j * size : (j + 1) * size, b * size : (b + 1) * size] = block
        values = [ref[...] for ref in source_refs[at : at + parts]]
        at += parts
        rhs = values[0] if parts == 1 else jnp.concatenate(values, 0)
        rhs = rhs.reshape(boxes * size, rhs.shape[-1])
        added = jnp.dot(lhs_ref[...], rhs, preferred_element_type=F32).reshape(total_ref.shape)
        if step == 0:
            total = sum_ref[...] + added if with_total else added
            total = total + other_ref[...].astype(F32) if with_other else total
        else:
            total = total_ref[...] + added
        if step == len(places) - 1:
            out_ref[...] = total.astype(dtype).reshape(out_ref.shape)
        else:
            total_ref[...] = total


def shards(
    currents,
    radiate,
    receive,
    transfer_table,
    near_blocks,
    dir_offsets,
    trans_src,
    trans_tid,
    near_src,
):
    dir_count = lax.axis_size("dir")
    region_count = lax.axis_size("region")
    own = currents[0]
    boxes, unknowns, incidences = own.shape
    near_slots = near_src.shape[2]
    region_boxes = boxes * dir_count
    halo = region_boxes // 2
    near_halo = region_boxes // 4
    classes, directions = transfer_table.shape
    first_count = pad_to(classes // 4, UNROLL)
    top = dir_count // 2
    inner = range(2, top, 2)
    split = boxes // 2
    targets = 2 * boxes

    def partner(array, mask):
        return lax.ppermute(array, "dir", [(i, i ^ mask) for i in range(dir_count)])

    along = []
    for i in range(dir_count):
        for z in range(region_count):
            target = z + 1 if i >= top else z - 1
            if 0 <= target < region_count:
                along.append((i * region_count + z, i * region_count + target))

    def beyond(array):
        return lax.ppermute(array, ("dir", "region"), along)

    def pinned(array):
        return pltpu.with_memory_space_constraint(array, pltpu.VMEM)

    def in_hbm(array):
        return pltpu.with_memory_space_constraint(array, pltpu.HBM)

    width = pad_to(region_boxes + 2 * halo, LANES)
    used_width = pad_to(classes, LANES)
    map_shape = (pad_to(targets, ROWS), width)
    table_shape = (classes + 1, unknowns, unknowns)
    low_shape = (first_count, unknowns, unknowns)
    list_shape = (2, pad_to(classes + 2, LANES))
    vmem, smem, hbm = whole(pltpu.VMEM), whole(pltpu.SMEM), whole(pltpu.HBM)
    operator_cost = pl.CostEstimate(
        flops=classes * unknowns * unknowns * directions, bytes_accessed=MIB, transcendentals=0
    )

    field = {0: own}
    rim = {}
    for m in inner:
        field[m] = partner(own, m)
    field[top] = partner(own, top)
    rim[0] = beyond(own)
    near_other = partner(near_blocks, 1)
    low, weighted, rad_here, rows, cls, near_src_here, listed = pl.pallas_call(
        functools.partial(first_kernel, first_count, boxes, halo, region_boxes),
        in_specs=[hbm] * 7,
        out_specs=[vmem] * 6 + [smem],
        out_shape=(
            pltpu.VMEM(low_shape, BF16),
            pltpu.VMEM((unknowns, directions), BF16),
            pltpu.VMEM((directions, unknowns), BF16),
            pltpu.VMEM((classes, directions), F32),
            pltpu.VMEM(map_shape, I32),
            pltpu.VMEM(near_src.shape, I32),
            jax.ShapeDtypeStruct(list_shape, I32),
        ),
        scratch_shapes=[
            pltpu.SMEM(dir_offsets.shape, I32),
            pltpu.VMEM(trans_src.shape, I32),
            pltpu.VMEM(trans_tid.shape, I32),
            pltpu.VMEM(transfer_table.shape, BF16),
            pltpu.VMEM(receive.shape, BF16),
            pltpu.VMEM((ROWS, used_width), I32),
            pltpu.SMEM((ROWS, used_width), I32),
            pltpu.SemaphoreType.DMA((8,)),
        ],
        compiler_params=pltpu.CompilerParams(vmem_limit_bytes=8 * MIB),
        cost_estimate=operator_cost,
    )(*[in_hbm(a) for a in (dir_offsets, trans_src, trans_tid, near_src, transfer_table, receive, radiate)])

    tied = lax.optimization_barrier((low, [field[m] for m in inner], field[top], rim[0]))
    low, inner_fields, field[top], rim[0] = tied
    near_src_other = partner(near_src_here, 1)
    for m, value in zip(inner, inner_fields):
        field[m] = value
    for m in inner:
        field[top + m] = partner(field[top], m)
    rim[top] = partner(rim[0], top)
    for m in inner:
        rim[m] = beyond(field[m])

    table, near_here, near_map = pl.pallas_call(
        functools.partial(second_kernel, halo - near_halo),
        in_specs=[smem] + [vmem] * 5 + [hbm] * 2 + [vmem],
        out_specs=[vmem] * 3,
        out_shape=(
            pltpu.VMEM(table_shape, BF16),
            pltpu.VMEM((targets, near_slots + 1, unknowns, unknowns), BF16),
            pltpu.VMEM(map_shape, I32),
        ),
        scratch_shapes=[pltpu.SemaphoreType.DMA((targets + 1,))],
        compiler_params=pltpu.CompilerParams(vmem_limit_bytes=8 * MIB),
        cost_estimate=operator_cost,
    )(
        listed,
        pinned(rows),
        pinned(weighted),
        pinned(rad_here),
        pinned(near_src_here),
        near_src_other,
        in_hbm(near_blocks),
        near_other,
        pinned(low),
    )

    def apply(places, first_row, total, other, dtype, shape):
        full = (boxes, unknowns, incidences)
        if len(places) > GROUP:
            total = apply(places[:GROUP], first_row, total, None, F32, full)
            return apply(places[GROUP:], first_row, total, other, dtype, shape)
        parts = [part for _, _, group in places for part in group]
        args = [cls, near_map, listed, pinned(table), pinned(near_here)] + [pinned(part) for part in parts]
        args += [pinned(extra) for extra in (total, other) if extra is not None]
        specs = [smem] * 3 + [vmem] * (len(args) - 3)
        layout = [(outside, mask, len(group)) for outside, mask, group in places]
        kernel = functools.partial(
            apply_kernel, layout, first_row, boxes, halo, total is not None, other is not None, dtype
        )
        return pl.pallas_call(
            kernel,
            in_specs=specs,
            out_specs=vmem,
            out_shape=pltpu.VMEM(shape, dtype) if len(shape) == 3 else jax.ShapeDtypeStruct(shape, dtype),
            scratch_shapes=[pltpu.VMEM(full, F32)]
            + [pltpu.VMEM((boxes * unknowns, boxes * unknowns), BF16)] * 2,
            compiler_params=pltpu.CompilerParams(vmem_limit_bytes=14 * MIB),
            cost_estimate=pl.CostEstimate(
                flops=2 * len(places) * (boxes * unknowns) ** 2 * incidences, bytes_accessed=MIB, transcendentals=0
            ),
        )(*args)

    tied = lax.optimization_barrier(
        (table, [field[top + m] for m in inner], [rim[m] for m in inner], rim[top])
    )
    table, far_fields, inner_rims, rim[top] = tied
    for m, value, other in zip(inner, far_fields, inner_rims):
        field[top + m], rim[m] = value, other
    last = {m: [partner(rim[top][:split], m), partner(rim[m][split:], top)] for m in inner}

    full = (boxes, unknowns, incidences)
    early = [(False, m, [field[m]]) for m in (0, *inner, top)] + [(True, 0, [rim[0]])]
    middle = [(False, top + m, [field[top + m]]) for m in inner]
    middle += [(True, m, [rim[m]]) for m in (*inner, top)]
    for_other = apply(early + middle, boxes, None, None, BF16, full)

    for_other, last = lax.optimization_barrier((for_other, last))
    late = [(True, top + m, last[m]) for m in inner]
    late += [(True, top + m + 1, [partner(part, 1) for part in last[m]]) for m in inner]
    from_other = partner(for_other, 1)
    total = apply(early, 0, None, None, F32, full)
    return apply(middle + late, 0, total, from_other, BF16, currents.shape)


def solution(mesh):
    placed = (
        P("region", "dir", None, None),
        P(),
        P(),
        P(),
        P("region", "dir", None, None, None),
        P(),
        P("region", None, None),
        P("region", None, None),
        P("region", "dir", None),
    )
    return jax.shard_map(
        shards,
        mesh=mesh,
        in_specs=placed,
        out_specs=P("region", "dir", None, None),
        check_vma=False,
    )
```

time: 59 us -> 56.9 us (0.964)
  waiting for transfers between devices: 3.52 us -> 0.99 us
  Pallas kernels: 37 us -> 39.5 us
  other arithmetic: 0.83 us -> 0 us
  starting transfers between devices: 15.6 us -> 14.9 us
    ppermute x9 -> x11, waiting for transfers between devices: 3.51 us -> 0.99 us  [partner(): return lax.ppermute(array, 'dir', [(i, i ^ mask) for i in range(dir_count)])]
    pallas_call x5, Pallas kernels: 37 us -> 39.5 us  [the longest x3 13.8 us: apply(): pl.pallas_call(kernel, in_specs=specs, out_specs=vmem, out_shape=pltpu.VM...]
    broadcast_in_dim x1 -> x0, other arithmetic: 0.83 us -> none  [shards(): return (here + partner(there, 1).astype(F32)).astype(BF16)[None]]
    ppermute x9 -> x11, starting transfers between devices: 13 us -> 12.4 us  [partner(): return lax.ppermute(array, 'dir', [(i, i ^ mask) for i in range(dir_count)])]
    unnamed x5 -> x3, local copies, waits for them, and re-layouts: 1.35 us -> 1.28 us
  transfers between devices with their start and end apart: 11 -> 13, of which waited for: 3 -> 1; matrix products, arithmetic and copies ran while one was open for 1% -> 2% of each run, Pallas kernels for 60% -> 61%
where the time goes in v1:
time: 56.9 us
  Pallas kernels  39.5 us (69%)
  starting transfers between devices  14.9 us (26%)
  local copies, waits for them, and re-layouts  1.31 us (2%)
  waiting for transfers between devices  0.99 us (2%)
    pallas_call x3, Pallas kernels, apply(): pl.pallas_call(kernel, in_specs=specs, out_specs=vmem, out_shape=pltpu.VM...  13.8 us
    pallas_call x1, Pallas kernels, shards(): pl.pallas_call(functools.partial(first_kernel, first_count, boxes, halo,...  13.7 us
    ppermute x11, starting transfers between devices, partner(): return lax.ppermute(array, 'dir', [(i, i ^ mask) for i in range(dir_count)])  12.4 us
    pallas_call x1, Pallas kernels, shards(): pl.pallas_call(functools.partial(second_kernel, halo - near_halo), in_spe...  11.9 us
    ppermute x2, starting transfers between devices, beyond(): return lax.ppermute(array, ('dir', 'region'), along)  2.56 us
    unnamed x3, local copies, waits for them, and re-layouts  1.28 us
  transfers between devices with their start and end apart: 13, of which 1 were waited for; matrix products, arithmetic and copies ran while one was open for 2% of the time, Pallas kernels for 61%

profile of v1, /device:TPU:0, one launch (start us, length us, event | category | flops | bytes accessed | tf_op | source)
XLA Modules:
  0.0 56.9 jit_solution(10090542256462753857)
XLA Ops:
  0.0 0.5 collective-permute-start.1
  0.5 2.5 %collective-permute-start.2 = (bf16[6,128,256]{2,1,0:T(8,128)(2,1)}, bf16[6,128,256]{2,1,0:T(8,128)(2,1)S(1)}, u32[]{:S(2)}, u32[]{:S(2)}) collective-permute-start(bf16[6,128,256]{2,1,0:T(8,128)(2,1)} %bitcast.1), channel_id=1, source_target_pairs={{0,8},{4,12},{8,0},{12,4},{16,24},{20,28},{24,16},{28,20},{1,9},{5... | collective-permute-start | bytes 1179656 | tf_op jit(solution)/shard_map/ppermute | solution.py:271
  2.9 1.5 %collective-permute-start.3 = (bf16[6,128,256]{2,1,0:T(8,128)(2,1)}, bf16[6,128,256]{2,1,0:T(8,128)(2,1)S(1)}, u32[]{:S(2)}, u32[]{:S(2)}) collective-permute-start(bf16[6,128,256]{2,1,0:T(8,128)(2,1)} %bitcast.2), channel_id=1, source_target_pairs={{0,16},{4,20},{8,24},{12,28},{16,0},{20,4},{24,8},{28,12},{1,17},{... | collective-permute-start | bytes 1179656 | tf_op jit(solution)/shard_map/ppermute | solution.py:271
  4.5 1.3 %collective-permute-start.4 = (bf16[6,128,256]{2,1,0:T(8,128)(2,1)}, bf16[6,128,256]{2,1,0:T(8,128)(2,1)S(1)}, u32[]{:S(2)}, u32[]{:S(2)}) collective-permute-start(bf16[6,128,256]{2,1,0:T(8,128)(2,1)} %bitcast.3), channel_id=1, source_target_pairs={{1,0},{2,1},{3,2},{5,4},{6,5},{7,6},{9,8},{10,9},{11,10},{13,12},{... | collective-permute-start | bytes 1179656 | tf_op jit(solution)/shard_map/ppermute | solution.py:281
  5.8 1.3 %copy.10.near_src_hbm = s32[1,6,27]{2,1,0:T(8,128)} copy(s32[1,6,27]{2,0,1:T(1,128)} %param.17) | data formatting | bytes 1296 | tf_op args[8]
  7.0 13.7 %shard_map.91 = (bf16[80,128,128]{2,1,0:T(8,128)(2,1)S(1)}, bf16[128,1536]{1,0:T(8,128)(2,1)S(1)}, bf16[1536,128]{1,0:T(8,128)(2,1)S(1)}, f32[316,1536]{1,0:T(8,...) custom-call(s32[9]{0:T(128)} %off_hbm.1, s32[1,48,48]{2,1,0:T(8,128)} %src_hbm.1, ...), custom_call_target="tpu_custom_call" | custom-call | flops 7952400384 | bytes 1048576 | tf_op jit(solution)/shard_map/pallas_call | solution.py:307
  20.8 0.1 collective-permute-start
  20.8 0.0 collective-permute-done.2.rest_1_
  20.9 0.0 collective-permute-done.3.rest_2_
  20.9 0.0 collective-permute-done.4.rest_3_
  20.9 0.6 %collective-permute-start.5 = (bf16[6,128,256]{2,1,0:T(8,128)(2,1)S(1)}, bf16[6,128,256]{2,1,0:T(8,128)(2,1)S(1)}, u32[]{:S(2)}, u32[]{:S(2)}) collective-permute-start(bf16[6,128,256]{2,1,0:T(8,128)(2,1)S(1)} %collective-permute-done.3.rest_2_), channel_id=1, source_target_pairs={{0,8},{4,12},{8,0},{12,4},{16,24},{20,28},{24,16},{28,20},{1,9},{5... | collective-permute-start | bytes 1179656 | tf_op jit(solution)/shard_map/ppermute | solution.py:271
  21.5 1.3 %collective-permute-start.6 = (bf16[6,128,256]{2,1,0:T(8,128)(2,1)S(1)}, bf16[6,128,256]{2,1,0:T(8,128)(2,1)S(1)}, u32[]{:S(2)}, u32[]{:S(2)}) collective-permute-start(bf16[6,128,256]{2,1,0:T(8,128)(2,1)S(1)} %collective-permute-done.2.rest_1_), channel_id=1, source_target_pairs={{1,0},{2,1},{3,2},{5,4},{6,5},{7,6},{9,8},{10,9},{11,10},{13,12},{... | collective-permute-start | bytes 1179656 | tf_op jit(solution)/shard_map/ppermute | solution.py:281
  22.8 5.0 %collective-permute-start.7 = (bf16[6,128,256]{2,1,0:T(8,128)(2,1)S(1)}, bf16[6,128,256]{2,1,0:T(8,128)(2,1)S(1)}, u32[]{:S(2)}, u32[]{:S(2)}) collective-permute-start(bf16[6,128,256]{2,1,0:T(8,128)(2,1)S(1)} %collective-permute-done.4.rest_3_), channel_id=1, source_target_pairs={{0,16},{4,20},{8,24},{12,28},{16,0},{20,4},{24,8},{28,12},{1,17},{... | collective-permute-start | bytes 1179656 | tf_op jit(solution)/shard_map/ppermute | solution.py:271
  27.7 0.0 collective-permute-done.near_src_other_ref
  27.8 0.0 collective-permute-done.1.near_other_hbm
  27.8 11.9 %shard_map.92 = (bf16[317,128,128]{2,1,0:T(8,128)(2,1)S(1)}, bf16[12,28,128,128]{3,2,1,0:T(8,128)(2,1)S(1)}, s32[16,128]{1,0:T(8,128)S(1)}) custom-call(s32[2,384]{1,0:T(2,128)S(1)} %get-tuple-element.27.list_ref, f32[316,1536]{1,0:T(8,128)S(1)} %get-tuple-element.28.rows_ref, bf16[128,1536]{1,0:T(8,128)(2,1)S(1)} %get-tuple-element.29.weighted_ref, ...), custom_call_target="tpu_custom_call" | custom-call | flops 7952400384 | bytes 1048576 | tf_op jit(solution)/shard_map/pallas_call | solution.py:345
  39.7 0.0 collective-permute-done.5.rest_4_.rest_0_
  39.7 0.0 collective-permute-done.6.rest_5_.rest_1_
  39.7 0.0 collective-permute-done.7.rest_6_.rest_2_
  39.8 1.6 %collective-permute-start.8 = (bf16[3,128,256]{2,1,0:T(8,128)(2,1)S(1)}, bf16[3,128,256]{2,1,0:T(8,128)(2,1)S(1)}, u32[]{:S(2)}, u32[]{:S(2)}) collective-permute-start(bf16[3,128,256]{2,1,0:T(8,128)(2,1)S(1)} %slice.6), channel_id=1, source_target_pairs={{0,8},{4,12},{8,0},{12,4},{16,24},{20,28},{24,16},{28,20},{1,9},{5... | collective-permute-start | bytes 589832 | tf_op jit(solution)/shard_map/ppermute | solution.py:271
  41.4 0.1 collective-permute-start.9
  41.5 5.7 %shard_map.93 = bf16[6,128,256]{2,1,0:T(8,128)(2,1)S(1)} custom-call(s32[16,128]{1,0:T(8,128)S(1)} %get-tuple-element.26.cls_ref, s32[16,128]{1,0:T(8,128)S(1)} %get-tuple-element.34.near_map_ref, s32[2,384]{1,0:T(2,128)S(1)} %get-tuple-element.27.list_ref, bf16[317,128,128]{2,1,0:T(8,128)(2,1)S(1)} %get-tuple-element.39.t_ref, ...), custom_call_target="tpu_custom_call" | custom-call | flops 2113929216 | bytes 1048576 | tf_op jit(solution)/shard_map/pallas_call | solution.py:382
  47.2 0.0 collective-permute-done.8.rest_3_
  47.2 1.0 %collective-permute-done.9.rest_4_ = bf16[3,128,256]{2,1,0:T(8,128)(2,1)S(1)} collective-permute-done((bf16[3,128,256]{2,1,0:T(8,128)(2,1)S(1)}, bf16[3,128,256]{2,1,0:T(8,128)(2,1)S(1)}, u32[]{:S(2)}, u32[]{:S(2)}) %collective-permute-start.9) | collective-permute-done | bytes 196640 | tf_op jit(solution)/shard_map/ppermute | solution.py:271
  48.2 0.0 collective-permute-start.12
  48.2 0.5 collective-permute-start.10
  48.7 0.0 collective-permute-start.11
  48.7 3.2 %shard_map.94.rest_7_ = f32[6,128,256]{2,1,0:T(8,128)S(1)} custom-call(s32[16,128]{1,0:T(8,128)S(1)} %get-tuple-element.26.cls_ref, s32[16,128]{1,0:T(8,128)S(1)} %get-tuple-element.34.near_map_ref, s32[2,384]{1,0:T(2,128)S(1)} %get-tuple-element.27.list_ref, bf16[317,128,128]{2,1,0:T(8,128)(2,1)S(1)} %get-tuple-element.39.t_ref, ...), custom_call_target="tpu_custom_call" | custom-call | flops 1207959552 | bytes 1048576 | tf_op jit(solution)/shard_map/pallas_call | solution.py:382
  51.8 0.0 collective-permute-done.10.rest_5_
  51.8 0.0 collective-permute-done.11.rest_6_
  51.9 0.0 collective-permute-done.12.rest_8_
  51.9 5.0 %shard_map.95 = bf16[1,6,128,256]{3,2,1,0:T(8,128)(2,1)} custom-call(s32[16,128]{1,0:T(8,128)S(1)} %get-tuple-element.26.cls_ref, s32[16,128]{1,0:T(8,128)S(1)} %get-tuple-element.34.near_map_ref, s32[2,384]{1,0:T(2,128)S(1)} %get-tuple-element.27.list_ref, bf16[317,128,128]{2,1,0:T(8,128)(2,1)S(1)} %get-tuple-element.39.t_ref, ...), custom_call_target="tpu_custom_call" | custom-call | flops 1509949440 | bytes 1048576 | tf_op jit(solution)/shard_map/pallas_call | solution.py:382
  (4 shorter events, 0.0 us)
Async XLA Ops:
  0.0 27.8 %collective-permute-start.1 = (bf16[1,6,27,128,128]{4,3,2,1,0:T(8,128)(2,1)}, bf16[1,6,27,128,128]{4,3,2,1,0:T(8,128)(2,1)S(1)}, u32[]{:S(2)}, u32[]{:S(2)}) collective-permute-start(bf16[1,6,27,128,128]{4,3,2,1,0:T(8,128)(2,1)} %near_hbm.1), channel_id=1, source_target_pairs={{0,4},{4,0},{8,12},{12,8},{16,20},{20,16},{24,28},{28,24},{1,5},{5... | collective-permute-start | bytes 15925256 | tf_op jit(solution)/shard_map/ppermute | solution.py:271
  0.5 20.4 %collective-permute-start.2 = (bf16[6,128,256]{2,1,0:T(8,128)(2,1)}, bf16[6,128,256]{2,1,0:T(8,128)(2,1)S(1)}, u32[]{:S(2)}, u32[]{:S(2)}) collective-permute-start(bf16[6,128,256]{2,1,0:T(8,128)(2,1)} %bitcast.1), channel_id=1, source_target_pairs={{0,8},{4,12},{8,0},{12,4},{16,24},{20,28},{24,16},{28,20},{1,9},{5... | collective-permute-start | bytes 1179656 | tf_op jit(solution)/shard_map/ppermute | solution.py:271
  2.9 17.9 %collective-permute-start.3 = (bf16[6,128,256]{2,1,0:T(8,128)(2,1)}, bf16[6,128,256]{2,1,0:T(8,128)(2,1)S(1)}, u32[]{:S(2)}, u32[]{:S(2)}) collective-permute-start(bf16[6,128,256]{2,1,0:T(8,128)(2,1)} %bitcast.2), channel_id=1, source_target_pairs={{0,16},{4,20},{8,24},{12,28},{16,0},{20,4},{24,8},{28,12},{1,17},{... | collective-permute-start | bytes 1179656 | tf_op jit(solution)/shard_map/ppermute | solution.py:271
  4.5 16.4 %collective-permute-start.4 = (bf16[6,128,256]{2,1,0:T(8,128)(2,1)}, bf16[6,128,256]{2,1,0:T(8,128)(2,1)S(1)}, u32[]{:S(2)}, u32[]{:S(2)}) collective-permute-start(bf16[6,128,256]{2,1,0:T(8,128)(2,1)} %bitcast.3), channel_id=1, source_target_pairs={{1,0},{2,1},{3,2},{5,4},{6,5},{7,6},{9,8},{10,9},{11,10},{13,12},{... | collective-permute-start | bytes 1179656 | tf_op jit(solution)/shard_map/ppermute | solution.py:281
  20.8 7.0 %collective-permute-start = (s32[1,6,27]{2,1,0:T(8,128)S(1)}, s32[1,6,27]{2,1,0:T(8,128)S(1)}, u32[]{:S(2)}, u32[]{:S(2)}) collective-permute-start(s32[1,6,27]{2,1,0:T(8,128)S(1)} %get-tuple-element.31.near_src_ref), channel_id=1, source_target_pairs={{0,4},{4,0},{8,12},{12,8},{16,20},{20,16},{24,28},{28,24},{1,5},{5... | collective-permute-start | bytes 1952 | tf_op jit(solution)/shard_map/ppermute | solution.py:271
  20.9 18.8 %collective-permute-start.5 = (bf16[6,128,256]{2,1,0:T(8,128)(2,1)S(1)}, bf16[6,128,256]{2,1,0:T(8,128)(2,1)S(1)}, u32[]{:S(2)}, u32[]{:S(2)}) collective-permute-start(bf16[6,128,256]{2,1,0:T(8,128)(2,1)S(1)} %collective-permute-done.3.rest_2_), channel_id=1, source_target_pairs={{0,8},{4,12},{8,0},{12,4},{16,24},{20,28},{24,16},{28,20},{1,9},{5... | collective-permute-start | bytes 1179656 | tf_op jit(solution)/shard_map/ppermute | solution.py:271
  21.5 18.2 %collective-permute-start.6 = (bf16[6,128,256]{2,1,0:T(8,128)(2,1)S(1)}, bf16[6,128,256]{2,1,0:T(8,128)(2,1)S(1)}, u32[]{:S(2)}, u32[]{:S(2)}) collective-permute-start(bf16[6,128,256]{2,1,0:T(8,128)(2,1)S(1)} %collective-permute-done.2.rest_1_), channel_id=1, source_target_pairs={{1,0},{2,1},{3,2},{5,4},{6,5},{7,6},{9,8},{10,9},{11,10},{13,12},{... | collective-permute-start | bytes 1179656 | tf_op jit(solution)/shard_map/ppermute | solution.py:281
  22.8 17.0 %collective-permute-start.7 = (bf16[6,128,256]{2,1,0:T(8,128)(2,1)S(1)}, bf16[6,128,256]{2,1,0:T(8,128)(2,1)S(1)}, u32[]{:S(2)}, u32[]{:S(2)}) collective-permute-start(bf16[6,128,256]{2,1,0:T(8,128)(2,1)S(1)} %collective-permute-done.4.rest_3_), channel_id=1, source_target_pairs={{0,16},{4,20},{8,24},{12,28},{16,0},{20,4},{24,8},{28,12},{1,17},{... | collective-permute-start | bytes 1179656 | tf_op jit(solution)/shard_map/ppermute | solution.py:271
  27.8 13.8 %copy-start = (bf16[1,6,128,256]{3,2,1,0:T(8,128)(2,1)S(1)}, bf16[1,6,128,256]{3,2,1,0:T(8,128)(2,1)}, u32[]{:S(2)}) copy-start(bf16[1,6,128,256]{3,2,1,0:T(8,128)(2,1)} %param.9) | copy-start | bytes 1179652
  39.8 7.5 %collective-permute-start.8 = (bf16[3,128,256]{2,1,0:T(8,128)(2,1)S(1)}, bf16[3,128,256]{2,1,0:T(8,128)(2,1)S(1)}, u32[]{:S(2)}, u32[]{:S(2)}) collective-permute-start(bf16[3,128,256]{2,1,0:T(8,128)(2,1)S(1)} %slice.6), channel_id=1, source_target_pairs={{0,8},{4,12},{8,0},{12,4},{16,24},{20,28},{24,16},{28,20},{1,9},{5... | collective-permute-start | bytes 589832 | tf_op jit(solution)/shard_map/ppermute | solution.py:271
  41.4 6.7 %collective-permute-start.9 = (bf16[3,128,256]{2,1,0:T(8,128)(2,1)S(1)}, bf16[3,128,256]{2,1,0:T(8,128)(2,1)S(1)}, u32[]{:S(2)}, u32[]{:S(2)}) collective-permute-start(bf16[3,128,256]{2,1,0:T(8,128)(2,1)S(1)} %slice.7), channel_id=1, source_target_pairs={{0,16},{4,20},{8,24},{12,28},{16,0},{20,4},{24,8},{28,12},{1,17},{... | collective-permute-start | bytes 589832 | tf_op jit(solution)/shard_map/ppermute | solution.py:271
  48.2 3.7 %collective-permute-start.12 = (bf16[6,128,256]{2,1,0:T(8,128)(2,1)S(1)}, bf16[6,128,256]{2,1,0:T(8,128)(2,1)S(1)}, u32[]{:S(2)}, u32[]{:S(2)}) collective-permute-start(bf16[6,128,256]{2,1,0:T(8,128)(2,1)S(1)} %shard_map.93), channel_id=1, source_target_pairs={{0,4},{4,0},{8,12},{12,8},{16,20},{20,16},{24,28},{28,24},{1,5},{5... | collective-permute-start | bytes 1179656 | tf_op jit(solution)/shard_map/ppermute | solution.py:271
  48.2 3.7 %collective-permute-start.10 = (bf16[3,128,256]{2,1,0:T(8,128)(2,1)S(1)}, bf16[3,128,256]{2,1,0:T(8,128)(2,1)S(1)}, u32[]{:S(2)}, u32[]{:S(2)}) collective-permute-start(bf16[3,128,256]{2,1,0:T(8,128)(2,1)S(1)} %collective-permute-done.8.rest_3_), channel_id=1, source_target_pairs={{0,4},{4,0},{8,12},{12,8},{16,20},{20,16},{24,28},{28,24},{1,5},{5... | collective-permute-start | bytes 589832 | tf_op jit(solution)/shard_map/ppermute | solution.py:271
  48.7 3.2 %collective-permute-start.11 = (bf16[3,128,256]{2,1,0:T(8,128)(2,1)S(1)}, bf16[3,128,256]{2,1,0:T(8,128)(2,1)S(1)}, u32[]{:S(2)}, u32[]{:S(2)}) collective-permute-start(bf16[3,128,256]{2,1,0:T(8,128)(2,1)S(1)} %collective-permute-done.9.rest_4_), channel_id=1, source_target_pairs={{0,4},{4,0},{8,12},{12,8},{16,20},{20,16},{24,28},{28,24},{1,5},{5... | collective-permute-start | bytes 589832 | tf_op jit(solution)/shard_map/ppermute | solution.py:271

commit v2 on v1

--- a/solution.py
+++ b/solution.py
@@ -69,14 +69,13 @@
     rows_ref,
     cls_ref,
     near_src_ref,
-    list_ref,
+    listed_ref,
     off_ref,
     src_ref,
     tid_ref,
     table_ref,
     recv_ref,
-    used_ref,
-    used_smem,
+    list_ref,
     sems,
 ):
     pairs = [
@@ -98,7 +97,7 @@
     top = dir_count // 2
     slots = src_ref.shape[2]
     width = cls_ref.shape[1]
-    used_width = used_ref.shape[1]
+    used_width = listed_ref.shape[1]
     ext_at = lax.broadcasted_iota(I32, (width, slots), 0)
     class_at = lax.broadcasted_iota(I32, (used_width, slots), 0)
     row_at = lax.broadcasted_iota(I32, (ROWS, slots), 0)
@@ -121,9 +120,21 @@
         found = lookup(parts, jnp.where(ext_at == src, 1.0, 0.0))
         value = jnp.where(found[2:3] > 0, found[0:1] * 16 + found[1:2], classes)
         cls = jnp.where(out_row == j, value, cls)
-    used_ref[...] = lookup(jnp.ones((ROWS, slots), I32), seen)
     cls_ref[...] = cls
-    to_smem = pltpu.make_async_copy(used_ref, used_smem, sems.at[len(pairs)])
+    is_used = jnp.minimum(lookup(jnp.ones((ROWS, slots), I32), seen), 1)
+    down = lax.broadcasted_iota(I32, (used_width, used_width), 0)
+    across = lax.broadcasted_iota(I32, (used_width, used_width), 1)
+    rank = lookup(is_used, jnp.where(across < down, 1.0, 0.0))
+    here = (down == rank[0:1]) & (is_used[0:1] > 0)
+    lane = lax.broadcasted_iota(I32, (ROWS, used_width), 1)
+    list_row = lax.broadcasted_iota(I32, (ROWS, used_width), 0)
+    found = lookup(jnp.where(list_row == 0, lane // 16, lane % 16), jnp.where(here, 1.0, 0.0))
+    ordered = found[0:1] * 16 + found[1:2]
+    rank = jnp.where(lane == classes, classes, rank)
+    count = jnp.sum(is_used[0:1].astype(F32), axis=1, keepdims=True).astype(I32)
+    listed = jnp.where(list_row == 0, ordered, jnp.where(list_row == 1, rank, count))
+    listed_ref[...] = listed
+    to_smem = pltpu.make_async_copy(listed_ref, list_ref, sems.at[len(pairs)])
     to_smem.start()
     copies[2].wait()
     position = lax.broadcasted_iota(I32, (1, directions), 1)
@@ -138,15 +149,7 @@
     copies[4].wait()
     rows_ref[...] = table_ref[...].astype(F32)
     to_smem.wait()
-
-    def note(n, count):
-        list_ref[0, count] = n
-        list_ref[1, n] = count
-        return count + (used_smem[0, n] > 0).astype(I32)
-
-    count = lax.fori_loop(0, classes, note, 0, unroll=8)
-    list_ref[1, classes] = classes
-    list_ref[0, classes + 1] = count
+    count = list_ref[2, 0]
     copies[5].wait()
     copies[6].wait()
     fill_operators(0, jnp.minimum(count, first_count), list_ref, rows_ref, weighted_ref, rad_ref, t_ref)
@@ -178,7 +181,6 @@
             )
             copies[-1].start()
     first_count = low_ref.shape[0]
-    classes = rows_ref.shape[0]
     copies.append(pltpu.make_async_copy(low_ref, t_ref.at[pl.ds(0, first_count)], sems.at[2 * boxes]))
     copies[-1].start()
     t_ref[t_ref.shape[0] - 1] = jnp.zeros(t_ref.shape[1:], BF16)
@@ -191,12 +193,12 @@
     out_row = lax.broadcasted_iota(I32, near_map_ref.shape, 0)
     near_map = jnp.full(near_map_ref.shape, near_slots, I32)
     for j in range(2 * boxes):
-        near = (near_src_ref if j < boxes else near_src_other_ref)[0, j % boxes : j % boxes + 1, :]
+        near = (near_src_ref if j < boxes else near_src_other_ref)[j % boxes]
         found = lookup(jnp.where(row_at == 0, lane_at, 1), jnp.where((near_at == near + near_shift) & (near >= 0), 1.0, 0.0))
         value = jnp.where(found[1:2] > 0, found[0:1], near_slots)
         near_map = jnp.where(out_row == j, value, near_map)
     near_map_ref[...] = near_map
-    fill_operators(first_count, list_ref[0, classes + 1], list_ref, rows_ref, weighted_ref, rad_ref, t_ref)
+    fill_operators(first_count, list_ref[2, 0], list_ref, rows_ref, weighted_ref, rad_ref, t_ref)
     for copy in copies:
         copy.wait()
 
@@ -209,36 +211,37 @@
         sum_ref, *rest = rest
     if with_other:
         other_ref, *rest = rest
-    out_ref, total_ref, *lhs_refs = rest
+    (out_ref,) = rest
     me = lax.axis_index("dir")
     region_boxes = boxes * lax.axis_size("dir")
-    size = near_ref.shape[2]
+    groups = []
     at = 0
-    for step, (rim, mask, parts) in enumerate(places):
-        lhs_ref = lhs_refs[step % len(lhs_refs)]
+    for rim, mask, parts in places:
         owner = me ^ mask
         base = owner * boxes + halo
         if rim:
             base = base + jnp.where(owner * boxes >= halo, -region_boxes, region_boxes)
-        for j in range(boxes):
-            row = first_row + j
+        groups.append((base, source_refs[at : at + parts]))
+        at += parts
+    for j in range(boxes):
+        row = first_row + j
+        total = sum_ref[j] if with_total else None
+        if with_other:
+            other = other_ref[j].astype(F32)
+            total = other if total is None else total + other
+        for base, refs in groups:
+            blocks = []
             for b in range(boxes):
-                block = t_ref[list_ref[1, cls_ref[row, base + b]]] + near_ref[row, near_map_ref[row, base + b]]
-                lhs_ref[j * size : (j + 1) * size, b * size : (b + 1) * size] = block
-        values = [ref[...] for ref in source_refs[at : at + parts]]
-        at += parts
-        rhs = values[0] if parts == 1 else jnp.concatenate(values, 0)
-        rhs = rhs.reshape(boxes * size, rhs.shape[-1])
-        added = jnp.dot(lhs_ref[...], rhs, preferred_element_type=F32).reshape(total_ref.shape)
-        if step == 0:
-            total = sum_ref[...] + added if with_total else added
-            total = total + other_ref[...].astype(F32) if with_other else total
+                n = list_ref[1, cls_ref[row, base + b]]
+                blocks.append(t_ref[n] + near_ref[row, near_map_ref[row, base + b]])
+            values = [ref[...].reshape(-1, ref.shape[-1]) for ref in refs]
+            rhs = values[0] if len(values) == 1 else jnp.concatenate(values, 0)
+            added = jnp.dot(jnp.concatenate(blocks, 1), rhs, preferred_element_type=F32)
+            total = added if total is None else total + added
+        if len(out_ref.shape) == 4:
+            out_ref[0, j] = total.astype(dtype)
         else:
-            total = total_ref[...] + added
-        if step == len(places) - 1:
-            out_ref[...] = total.astype(dtype).reshape(out_ref.shape)
-        else:
-            total_ref[...] = total
+            out_ref[j] = total.astype(dtype)
 
 
 def shards(
@@ -257,6 +260,7 @@
     own = currents[0]
     boxes, unknowns, incidences = own.shape
     near_slots = near_src.shape[2]
+    near_src = near_src.reshape(boxes, 1, near_slots)
     region_boxes = boxes * dir_count
     halo = region_boxes // 2
     near_halo = region_boxes // 4
@@ -287,11 +291,10 @@
         return pltpu.with_memory_space_constraint(array, pltpu.HBM)
 
     width = pad_to(region_boxes + 2 * halo, LANES)
-    used_width = pad_to(classes, LANES)
     map_shape = (pad_to(targets, ROWS), width)
     table_shape = (classes + 1, unknowns, unknowns)
     low_shape = (first_count, unknowns, unknowns)
-    list_shape = (2, pad_to(classes + 2, LANES))
+    list_shape = (ROWS, pad_to(classes + 1, LANES))
     vmem, smem, hbm = whole(pltpu.VMEM), whole(pltpu.SMEM), whole(pltpu.HBM)
     operator_cost = pl.CostEstimate(
         flops=classes * unknowns * unknowns * directions, bytes_accessed=MIB, transcendentals=0
@@ -307,7 +310,7 @@
     low, weighted, rad_here, rows, cls, near_src_here, listed = pl.pallas_call(
         functools.partial(first_kernel, first_count, boxes, halo, region_boxes),
         in_specs=[hbm] * 7,
-        out_specs=[vmem] * 6 + [smem],
+        out_specs=[vmem] * 7,
         out_shape=(
             pltpu.VMEM(low_shape, BF16),
             pltpu.VMEM((unknowns, directions), BF16),
@@ -315,7 +318,7 @@
             pltpu.VMEM((classes, directions), F32),
             pltpu.VMEM(map_shape, I32),
             pltpu.VMEM(near_src.shape, I32),
-            jax.ShapeDtypeStruct(list_shape, I32),
+            pltpu.VMEM(list_shape, I32),
         ),
         scratch_shapes=[
             pltpu.SMEM(dir_offsets.shape, I32),
@@ -323,8 +326,7 @@
             pltpu.VMEM(trans_tid.shape, I32),
             pltpu.VMEM(transfer_table.shape, BF16),
             pltpu.VMEM(receive.shape, BF16),
-            pltpu.VMEM((ROWS, used_width), I32),
-            pltpu.SMEM((ROWS, used_width), I32),
+            pltpu.SMEM(list_shape, I32),
             pltpu.SemaphoreType.DMA((8,)),
         ],
         compiler_params=pltpu.CompilerParams(vmem_limit_bytes=8 * MIB),
@@ -384,9 +386,7 @@
             in_specs=specs,
             out_specs=vmem,
             out_shape=pltpu.VMEM(shape, dtype) if len(shape) == 3 else jax.ShapeDtypeStruct(shape, dtype),
-            scratch_shapes=[pltpu.VMEM(full, F32)]
-            + [pltpu.VMEM((boxes * unknowns, boxes * unknowns), BF16)] * 2,
-            compiler_params=pltpu.CompilerParams(vmem_limit_bytes=14 * MIB),
+            compiler_params=pltpu.CompilerParams(vmem_limit_bytes=12 * MIB),
             cost_estimate=pl.CostEstimate(
                 flops=2 * len(places) * (boxes * unknowns) ** 2 * incidences, bytes_accessed=MIB, transcendentals=0
             ),

time: 56.9 us -> 51.2 us (0.90); the launches traced: 56.9 us -> 50.6 us
  Pallas kernels: 39.5 us -> 32.9 us
  local copies, waits for them, and re-layouts: 1.31 us -> 0.03 us
  waiting for transfers between devices: 0.99 us -> 2.04 us
  starting transfers between devices: 14.9 us -> 15.5 us
    pallas_call x3, Pallas kernels: 13.8 us -> 9.8 us  [apply(): pl.pallas_call(kernel, in_specs=specs, out_specs=vmem, out_shape=pltpu.VM...]
    pallas_call x1, Pallas kernels: 13.7 us -> 11.5 us  [shards(): pl.pallas_call(functools.partial(first_kernel, first_count, boxes, halo,...]
    unnamed x3 -> x2, local copies, waits for them, and re-layouts: 1.28 us -> 0.01 us
    ppermute x11, waiting for transfers between devices: 0.99 us -> 1.9 us  [partner(): return lax.ppermute(array, 'dir', [(i, i ^ mask) for i in range(dir_count)])]
  transfers between devices with their start and end apart: 13 -> 13, of which waited for: 1 -> 3; matrix products, arithmetic and copies ran while one was open for 2% -> 0% of each run, Pallas kernels for 61% -> 58%
where the time goes in v2:
time: 51.2 us; the launch traced here: 50.6 us
  Pallas kernels  32.9 us (64%)
  starting transfers between devices  15.5 us (30%)
  waiting for transfers between devices  2.04 us (4%)
    ppermute x11, starting transfers between devices, partner(): return lax.ppermute(array, 'dir', [(i, i ^ mask) for i in range(dir_count)])  12.9 us
    pallas_call x1, Pallas kernels, shards(): pl.pallas_call(functools.partial(first_kernel, first_count, boxes, halo,...  11.5 us
    pallas_call x1, Pallas kernels, shards(): pl.pallas_call(functools.partial(second_kernel, halo - near_halo), in_spe...  11.5 us
    pallas_call x3, Pallas kernels, apply(): pl.pallas_call(kernel, in_specs=specs, out_specs=vmem, out_shape=pltpu.VM...  9.8 us
    ppermute x2, starting transfers between devices, beyond(): return lax.ppermute(array, ('dir', 'region'), along)  2.56 us
    ppermute x11, waiting for transfers between devices, partner(): return lax.ppermute(array, 'dir', [(i, i ^ mask) for i in range(dir_count)])  1.9 us
  transfers between devices with their start and end apart: 13, of which 3 were waited for; matrix products, arithmetic and copies ran while one was open for 0% of the time, Pallas kernels for 58%

profile of v2, /device:TPU:0, one launch (start us, length us, event | category | flops | bytes accessed | tf_op | source)
XLA Modules:
  0.0 50.6 jit_solution(7019427181704929484)
XLA Ops:
  0.0 0.5 collective-permute-start.1
  0.5 2.5 %collective-permute-start.2 = (bf16[6,128,256]{2,1,0:T(8,128)(2,1)}, bf16[6,128,256]{2,1,0:T(8,128)(2,1)S(1)}, u32[]{:S(2)}, u32[]{:S(2)}) collective-permute-start(bf16[6,128,256]{2,1,0:T(8,128)(2,1)} %bitcast.2), channel_id=1, source_target_pairs={{0,8},{4,12},{8,0},{12,4},{16,24},{20,28},{24,16},{28,20},{1,9},{5... | collective-permute-start | bytes 1179656 | tf_op jit(solution)/shard_map/ppermute | solution.py:275
  2.9 1.5 %collective-permute-start.3 = (bf16[6,128,256]{2,1,0:T(8,128)(2,1)}, bf16[6,128,256]{2,1,0:T(8,128)(2,1)S(1)}, u32[]{:S(2)}, u32[]{:S(2)}) collective-permute-start(bf16[6,128,256]{2,1,0:T(8,128)(2,1)} %bitcast.3), channel_id=1, source_target_pairs={{0,16},{4,20},{8,24},{12,28},{16,0},{20,4},{24,8},{28,12},{1,17},{... | collective-permute-start | bytes 1179656 | tf_op jit(solution)/shard_map/ppermute | solution.py:275
  4.5 1.3 %collective-permute-start.4 = (bf16[6,128,256]{2,1,0:T(8,128)(2,1)}, bf16[6,128,256]{2,1,0:T(8,128)(2,1)S(1)}, u32[]{:S(2)}, u32[]{:S(2)}) collective-permute-start(bf16[6,128,256]{2,1,0:T(8,128)(2,1)} %bitcast.4), channel_id=1, source_target_pairs={{1,0},{2,1},{3,2},{5,4},{6,5},{7,6},{9,8},{10,9},{11,10},{13,12},{... | collective-permute-start | bytes 1179656 | tf_op jit(solution)/shard_map/ppermute | solution.py:285
  5.8 11.5 %shard_map.91 = (bf16[80,128,128]{2,1,0:T(8,128)(2,1)S(1)}, bf16[128,1536]{1,0:T(8,128)(2,1)S(1)}, bf16[1536,128]{1,0:T(8,128)(2,1)S(1)}, f32[316,1536]{1,0:T(8,...) custom-call(s32[9]{0:T(128)} %off_hbm.1, s32[1,48,48]{2,1,0:T(8,128)} %src_hbm.1, ...), custom_call_target="tpu_custom_call" | custom-call | flops 7952400384 | bytes 1048576 | tf_op jit(solution)/shard_map/pallas_call | solution.py:310
  17.3 0.1 collective-permute-start
  17.4 0.0 collective-permute-done.2.rest_1_
  17.4 0.0 collective-permute-done.3.rest_2_
  17.4 0.1 collective-permute-done.4.rest_3_
  17.5 0.5 %collective-permute-start.5 = (bf16[6,128,256]{2,1,0:T(8,128)(2,1)S(1)}, bf16[6,128,256]{2,1,0:T(8,128)(2,1)S(1)}, u32[]{:S(2)}, u32[]{:S(2)}) collective-permute-start(bf16[6,128,256]{2,1,0:T(8,128)(2,1)S(1)} %collective-permute-done.3.rest_2_), channel_id=1, source_target_pairs={{0,8},{4,12},{8,0},{12,4},{16,24},{20,28},{24,16},{28,20},{1,9},{5... | collective-permute-start | bytes 1179656 | tf_op jit(solution)/shard_map/ppermute | solution.py:275
  18.1 1.3 %collective-permute-start.6 = (bf16[6,128,256]{2,1,0:T(8,128)(2,1)S(1)}, bf16[6,128,256]{2,1,0:T(8,128)(2,1)S(1)}, u32[]{:S(2)}, u32[]{:S(2)}) collective-permute-start(bf16[6,128,256]{2,1,0:T(8,128)(2,1)S(1)} %collective-permute-done.2.rest_1_), channel_id=1, source_target_pairs={{1,0},{2,1},{3,2},{5,4},{6,5},{7,6},{9,8},{10,9},{11,10},{13,12},{... | collective-permute-start | bytes 1179656 | tf_op jit(solution)/shard_map/ppermute | solution.py:285
  19.3 4.9 %collective-permute-start.7 = (bf16[6,128,256]{2,1,0:T(8,128)(2,1)S(1)}, bf16[6,128,256]{2,1,0:T(8,128)(2,1)S(1)}, u32[]{:S(2)}, u32[]{:S(2)}) collective-permute-start(bf16[6,128,256]{2,1,0:T(8,128)(2,1)S(1)} %collective-permute-done.4.rest_3_), channel_id=1, source_target_pairs={{0,16},{4,20},{8,24},{12,28},{16,0},{20,4},{24,8},{28,12},{1,17},{... | collective-permute-start | bytes 1179656 | tf_op jit(solution)/shard_map/ppermute | solution.py:275
  24.3 0.0 collective-permute-done.near_src_other_ref
  24.3 0.0 collective-permute-done.1.near_other_hbm
  24.3 11.5 %shard_map.92 = (bf16[317,128,128]{2,1,0:T(8,128)(2,1)S(1)}, bf16[12,28,128,128]{3,2,1,0:T(8,128)(2,1)S(1)}, s32[16,128]{1,0:T(8,128)S(1)}) custom-call(s32[8,384]{1,0:T(8,128)S(1)} %get-tuple-element.27.list_ref, f32[316,1536]{1,0:T(8,128)S(1)} %get-tuple-element.28.rows_ref, bf16[128,1536]{1,0:T(8,128)(2,1)S(1)} %get-tuple-element.29.weighted_ref, ...), custom_call_target="tpu_custom_call" | custom-call | flops 7952400384 | bytes 1048576 | tf_op jit(solution)/shard_map/pallas_call | solution.py:347
  35.8 0.0 collective-permute-done.5.rest_4_.rest_0_
  35.8 0.0 collective-permute-done.6.rest_5_.rest_1_
  35.8 0.0 collective-permute-done.7.rest_6_.rest_2_
  35.9 0.1 collective-permute-start.8
  36.0 2.2 %collective-permute-start.9 = (bf16[3,128,256]{2,1,0:T(8,128)(2,1)S(1)}, bf16[3,128,256]{2,1,0:T(8,128)(2,1)S(1)}, u32[]{:S(2)}, u32[]{:S(2)}) collective-permute-start(bf16[3,128,256]{2,1,0:T(8,128)(2,1)S(1)} %slice.7), channel_id=1, source_target_pairs={{0,16},{4,20},{8,24},{12,28},{16,0},{20,4},{24,8},{28,12},{1,17},{... | collective-permute-start | bytes 589832 | tf_op jit(solution)/shard_map/ppermute | solution.py:275
  38.2 0.0 copy-done
  38.2 3.6 %shard_map.93 = bf16[6,128,256]{2,1,0:T(8,128)(2,1)S(1)} custom-call(s32[16,128]{1,0:T(8,128)S(1)} %get-tuple-element.26.cls_ref, s32[16,128]{1,0:T(8,128)S(1)} %get-tuple-element.34.near_map_ref, s32[8,384]{1,0:T(8,128)S(1)} %get-tuple-element.27.list_ref, bf16[317,128,128]{2,1,0:T(8,128)(2,1)S(1)} %get-tuple-element.39.t_ref, ...), custom_call_target="tpu_custom_call" | custom-call | flops 2113929216 | bytes 1048576 | tf_op jit(solution)/shard_map/pallas_call | solution.py:384
  41.8 1.5 %collective-permute-done.8.rest_3_ = bf16[3,128,256]{2,1,0:T(8,128)(2,1)S(1)} collective-permute-done((bf16[3,128,256]{2,1,0:T(8,128)(2,1)S(1)}, bf16[3,128,256]{2,1,0:T(8,128)(2,1)S(1)}, u32[]{:S(2)}, u32[]{:S(2)}) %collective-permute-start.8) | collective-permute-done | bytes 196640 | tf_op jit(solution)/shard_map/ppermute | solution.py:275
  43.3 0.3 collective-permute-done.9.rest_4_
  43.6 0.1 collective-permute-start.12
  43.8 0.4 collective-permute-start.10
  44.2 0.1 collective-permute-start.11
  44.3 2.6 %shard_map.94.rest_7_ = f32[6,128,256]{2,1,0:T(8,128)S(1)} custom-call(s32[16,128]{1,0:T(8,128)S(1)} %get-tuple-element.26.cls_ref, s32[16,128]{1,0:T(8,128)S(1)} %get-tuple-element.34.near_map_ref, s32[8,384]{1,0:T(8,128)S(1)} %get-tuple-element.27.list_ref, bf16[317,128,128]{2,1,0:T(8,128)(2,1)S(1)} %get-tuple-element.39.t_ref, ...), custom_call_target="tpu_custom_call" | custom-call | flops 1207959552 | bytes 1048576 | tf_op jit(solution)/shard_map/pallas_call | solution.py:384
  46.8 0.0 collective-permute-done.10.rest_5_
  46.9 0.0 collective-permute-done.11.rest_6_
  46.9 0.0 collective-permute-done.12.rest_8_
  46.9 3.7 %shard_map.95 = bf16[1,6,128,256]{3,2,1,0:T(8,128)(2,1)} custom-call(s32[16,128]{1,0:T(8,128)S(1)} %get-tuple-element.26.cls_ref, s32[16,128]{1,0:T(8,128)S(1)} %get-tuple-element.34.near_map_ref, s32[8,384]{1,0:T(8,128)S(1)} %get-tuple-element.27.list_ref, bf16[317,128,128]{2,1,0:T(8,128)(2,1)S(1)} %get-tuple-element.39.t_ref, ...), custom_call_target="tpu_custom_call" | custom-call | flops 1509949440 | bytes 1048576 | tf_op jit(solution)/shard_map/pallas_call | solution.py:384
  (3 shorter events, 0.0 us)
Async XLA Ops:
  0.0 24.3 %collective-permute-start.1 = (bf16[1,6,27,128,128]{4,3,2,1,0:T(8,128)(2,1)}, bf16[1,6,27,128,128]{4,3,2,1,0:T(8,128)(2,1)S(1)}, u32[]{:S(2)}, u32[]{:S(2)}) collective-permute-start(bf16[1,6,27,128,128]{4,3,2,1,0:T(8,128)(2,1)} %near_hbm.1), channel_id=1, source_target_pairs={{0,4},{4,0},{8,12},{12,8},{16,20},{20,16},{24,28},{28,24},{1,5},{5... | collective-permute-start | bytes 15925256 | tf_op jit(solution)/shard_map/ppermute | solution.py:275
  0.5 16.9 %collective-permute-start.2 = (bf16[6,128,256]{2,1,0:T(8,128)(2,1)}, bf16[6,128,256]{2,1,0:T(8,128)(2,1)S(1)}, u32[]{:S(2)}, u32[]{:S(2)}) collective-permute-start(bf16[6,128,256]{2,1,0:T(8,128)(2,1)} %bitcast.2), channel_id=1, source_target_pairs={{0,8},{4,12},{8,0},{12,4},{16,24},{20,28},{24,16},{28,20},{1,9},{5... | collective-permute-start | bytes 1179656 | tf_op jit(solution)/shard_map/ppermute | solution.py:275
  2.9 14.4 %collective-permute-start.3 = (bf16[6,128,256]{2,1,0:T(8,128)(2,1)}, bf16[6,128,256]{2,1,0:T(8,128)(2,1)S(1)}, u32[]{:S(2)}, u32[]{:S(2)}) collective-permute-start(bf16[6,128,256]{2,1,0:T(8,128)(2,1)} %bitcast.3), channel_id=1, source_target_pairs={{0,16},{4,20},{8,24},{12,28},{16,0},{20,4},{24,8},{28,12},{1,17},{... | collective-permute-start | bytes 1179656 | tf_op jit(solution)/shard_map/ppermute | solution.py:275
  4.5 13.1 %collective-permute-start.4 = (bf16[6,128,256]{2,1,0:T(8,128)(2,1)}, bf16[6,128,256]{2,1,0:T(8,128)(2,1)S(1)}, u32[]{:S(2)}, u32[]{:S(2)}) collective-permute-start(bf16[6,128,256]{2,1,0:T(8,128)(2,1)} %bitcast.4), channel_id=1, source_target_pairs={{1,0},{2,1},{3,2},{5,4},{6,5},{7,6},{9,8},{10,9},{11,10},{13,12},{... | collective-permute-start | bytes 1179656 | tf_op jit(solution)/shard_map/ppermute | solution.py:285
  17.3 7.0 %collective-permute-start = (s32[6,1,27]{2,1,0:T(1,128)S(1)}, s32[6,1,27]{2,1,0:T(1,128)S(1)}, u32[]{:S(2)}, u32[]{:S(2)}) collective-permute-start(s32[6,1,27]{2,1,0:T(1,128)S(1)} %get-tuple-element.31.near_src_ref), channel_id=1, source_target_pairs={{0,4},{4,0},{8,12},{12,8},{16,20},{20,16},{24,28},{28,24},{1,5},{5... | collective-permute-start | bytes 1952 | tf_op jit(solution)/shard_map/ppermute | solution.py:275
  17.5 18.3 %collective-permute-start.5 = (bf16[6,128,256]{2,1,0:T(8,128)(2,1)S(1)}, bf16[6,128,256]{2,1,0:T(8,128)(2,1)S(1)}, u32[]{:S(2)}, u32[]{:S(2)}) collective-permute-start(bf16[6,128,256]{2,1,0:T(8,128)(2,1)S(1)} %collective-permute-done.3.rest_2_), channel_id=1, source_target_pairs={{0,8},{4,12},{8,0},{12,4},{16,24},{20,28},{24,16},{28,20},{1,9},{5... | collective-permute-start | bytes 1179656 | tf_op jit(solution)/shard_map/ppermute | solution.py:275
  18.1 17.8 %collective-permute-start.6 = (bf16[6,128,256]{2,1,0:T(8,128)(2,1)S(1)}, bf16[6,128,256]{2,1,0:T(8,128)(2,1)S(1)}, u32[]{:S(2)}, u32[]{:S(2)}) collective-permute-start(bf16[6,128,256]{2,1,0:T(8,128)(2,1)S(1)} %collective-permute-done.2.rest_1_), channel_id=1, source_target_pairs={{1,0},{2,1},{3,2},{5,4},{6,5},{7,6},{9,8},{10,9},{11,10},{13,12},{... | collective-permute-start | bytes 1179656 | tf_op jit(solution)/shard_map/ppermute | solution.py:285
  19.3 16.5 %collective-permute-start.7 = (bf16[6,128,256]{2,1,0:T(8,128)(2,1)S(1)}, bf16[6,128,256]{2,1,0:T(8,128)(2,1)S(1)}, u32[]{:S(2)}, u32[]{:S(2)}) collective-permute-start(bf16[6,128,256]{2,1,0:T(8,128)(2,1)S(1)} %collective-permute-done.4.rest_3_), channel_id=1, source_target_pairs={{0,16},{4,20},{8,24},{12,28},{16,0},{20,4},{24,8},{28,12},{1,17},{... | collective-permute-start | bytes 1179656 | tf_op jit(solution)/shard_map/ppermute | solution.py:275
  24.3 13.9 %copy-start = (bf16[1,6,128,256]{3,2,1,0:T(8,128)(2,1)S(1)}, bf16[1,6,128,256]{3,2,1,0:T(8,128)(2,1)}, u32[]{:S(2)}) copy-start(bf16[1,6,128,256]{3,2,1,0:T(8,128)(2,1)} %param.9) | copy-start | bytes 1179652
  35.9 7.5 %collective-permute-start.8 = (bf16[3,128,256]{2,1,0:T(8,128)(2,1)S(1)}, bf16[3,128,256]{2,1,0:T(8,128)(2,1)S(1)}, u32[]{:S(2)}, u32[]{:S(2)}) collective-permute-start(bf16[3,128,256]{2,1,0:T(8,128)(2,1)S(1)} %slice.6), channel_id=1, source_target_pairs={{0,8},{4,12},{8,0},{12,4},{16,24},{20,28},{24,16},{28,20},{1,9},{5... | collective-permute-start | bytes 589832 | tf_op jit(solution)/shard_map/ppermute | solution.py:275
  36.0 7.7 %collective-permute-start.9 = (bf16[3,128,256]{2,1,0:T(8,128)(2,1)S(1)}, bf16[3,128,256]{2,1,0:T(8,128)(2,1)S(1)}, u32[]{:S(2)}, u32[]{:S(2)}) collective-permute-start(bf16[3,128,256]{2,1,0:T(8,128)(2,1)S(1)} %slice.7), channel_id=1, source_target_pairs={{0,16},{4,20},{8,24},{12,28},{16,0},{20,4},{24,8},{28,12},{1,17},{... | collective-permute-start | bytes 589832 | tf_op jit(solution)/shard_map/ppermute | solution.py:275
  43.6 3.2 %collective-permute-start.12 = (bf16[6,128,256]{2,1,0:T(8,128)(2,1)S(1)}, bf16[6,128,256]{2,1,0:T(8,128)(2,1)S(1)}, u32[]{:S(2)}, u32[]{:S(2)}) collective-permute-start(bf16[6,128,256]{2,1,0:T(8,128)(2,1)S(1)} %shard_map.93), channel_id=1, source_target_pairs={{0,4},{4,0},{8,12},{12,8},{16,20},{20,16},{24,28},{28,24},{1,5},{5... | collective-permute-start | bytes 1179656 | tf_op jit(solution)/shard_map/ppermute | solution.py:275
  43.8 3.1 %collective-permute-start.10 = (bf16[3,128,256]{2,1,0:T(8,128)(2,1)S(1)}, bf16[3,128,256]{2,1,0:T(8,128)(2,1)S(1)}, u32[]{:S(2)}, u32[]{:S(2)}) collective-permute-start(bf16[3,128,256]{2,1,0:T(8,128)(2,1)S(1)} %collective-permute-done.8.rest_3_), channel_id=1, source_target_pairs={{0,4},{4,0},{8,12},{12,8},{16,20},{20,16},{24,28},{28,24},{1,5},{5... | collective-permute-start | bytes 589832 | tf_op jit(solution)/shard_map/ppermute | solution.py:275
  44.2 2.7 %collective-permute-start.11 = (bf16[3,128,256]{2,1,0:T(8,128)(2,1)S(1)}, bf16[3,128,256]{2,1,0:T(8,128)(2,1)S(1)}, u32[]{:S(2)}, u32[]{:S(2)}) collective-permute-start(bf16[3,128,256]{2,1,0:T(8,128)(2,1)S(1)} %collective-permute-done.9.rest_4_), channel_id=1, source_target_pairs={{0,4},{4,0},{8,12},{12,8},{16,20},{20,16},{24,28},{28,24},{1,5},{5... | collective-permute-start | bytes 589832 | tf_op jit(solution)/shard_map/ppermute | solution.py:275

commit v3 on v2

--- a/solution.py
+++ b/solution.py
@@ -59,7 +59,6 @@
     off_hbm,
     src_hbm,
     tid_hbm,
-    near_src_hbm,
     table_hbm,
     recv_hbm,
     rad_hbm,
@@ -68,7 +67,6 @@
     rad_ref,
     rows_ref,
     cls_ref,
-    near_src_ref,
     listed_ref,
     off_ref,
     src_ref,
@@ -85,7 +83,6 @@
         (recv_hbm, recv_ref),
         (table_hbm, table_ref),
         (rad_hbm, rad_ref),
-        (near_src_hbm, near_src_ref),
     ]
     copies = [pltpu.make_async_copy(a, b, sems.at[i]) for i, (a, b) in enumerate(pairs)]
     for copy in copies:
@@ -151,7 +148,6 @@
     to_smem.wait()
     count = list_ref[2, 0]
     copies[5].wait()
-    copies[6].wait()
     fill_operators(0, jnp.minimum(count, first_count), list_ref, rows_ref, weighted_ref, rad_ref, t_ref)
 
 
@@ -307,17 +303,17 @@
     field[top] = partner(own, top)
     rim[0] = beyond(own)
     near_other = partner(near_blocks, 1)
-    low, weighted, rad_here, rows, cls, near_src_here, listed = pl.pallas_call(
+    near_src_other = partner(near_src, 1)
+    low, weighted, rad_here, rows, cls, listed = pl.pallas_call(
         functools.partial(first_kernel, first_count, boxes, halo, region_boxes),
-        in_specs=[hbm] * 7,
-        out_specs=[vmem] * 7,
+        in_specs=[hbm] * 6,
+        out_specs=[vmem] * 6,
         out_shape=(
             pltpu.VMEM(low_shape, BF16),
             pltpu.VMEM((unknowns, directions), BF16),
             pltpu.VMEM((directions, unknowns), BF16),
             pltpu.VMEM((classes, directions), F32),
             pltpu.VMEM(map_shape, I32),
-            pltpu.VMEM(near_src.shape, I32),
             pltpu.VMEM(list_shape, I32),
         ),
         scratch_shapes=[
@@ -327,15 +323,14 @@
             pltpu.VMEM(transfer_table.shape, BF16),
             pltpu.VMEM(receive.shape, BF16),
             pltpu.SMEM(list_shape, I32),
-            pltpu.SemaphoreType.DMA((8,)),
+            pltpu.SemaphoreType.DMA((7,)),
         ],
         compiler_params=pltpu.CompilerParams(vmem_limit_bytes=8 * MIB),
         cost_estimate=operator_cost,
-    )(*[in_hbm(a) for a in (dir_offsets, trans_src, trans_tid, near_src, transfer_table, receive, radiate)])
+    )(*[in_hbm(a) for a in (dir_offsets, trans_src, trans_tid, transfer_table, receive, radiate)])
 
     tied = lax.optimization_barrier((low, [field[m] for m in inner], field[top], rim[0]))
     low, inner_fields, field[top], rim[0] = tied
-    near_src_other = partner(near_src_here, 1)
     for m, value in zip(inner, inner_fields):
         field[m] = value
     for m in inner:
@@ -361,7 +356,7 @@
         pinned(rows),
         pinned(weighted),
         pinned(rad_here),
-        pinned(near_src_here),
+        near_src,
         near_src_other,
         in_hbm(near_blocks),
         near_other,
@@ -406,12 +401,14 @@
     middle += [(True, m, [rim[m]]) for m in (*inner, top)]
     for_other = apply(early + middle, boxes, None, None, BF16, full)
 
-    for_other, last = lax.optimization_barrier((for_other, last))
-    late = [(True, top + m, last[m]) for m in inner]
-    late += [(True, top + m + 1, [partner(part, 1) for part in last[m]]) for m in inner]
     from_other = partner(for_other, 1)
     total = apply(early, 0, None, None, F32, full)
-    return apply(middle + late, 0, total, from_other, BF16, currents.shape)
+
+    total, last = lax.optimization_barrier((total, last))
+    turned = {m: [partner(part, 1) for part in last[m]] for m in inner}
+    total = apply(middle, 0, total, from_other, F32, full)
+    late = [(True, top + m, last[m]) for m in inner] + [(True, top + m + 1, turned[m]) for m in inner]
+    return apply(late, 0, total, None, BF16, currents.shape)
 
 
 def solution(mesh):

time: 51.2 us -> 54.6 us (1.066)
  waiting for transfers between devices: 2.04 us -> 4.2 us
  Pallas kernels: 32.9 us -> 34.2 us
    ppermute x11, waiting for transfers between devices: 1.9 us -> 4.07 us  [partner(): return lax.ppermute(array, 'dir', [(i, i ^ mask) for i in range(dir_count)])]
    pallas_call x3 -> x4, Pallas kernels: 9.8 us -> 11 us  [apply(): pl.pallas_call(kernel, in_specs=specs, out_specs=vmem, out_shape=pltpu.VM...]
  transfers between devices with their start and end apart: 13 -> 13, of which waited for: 3 -> 3; matrix products, arithmetic and copies ran while one was open for 0% -> 0% of each run, Pallas kernels for 58% -> 52%
where the time goes in v3:
time: 54.6 us; the launch traced here: 54.1 us
  Pallas kernels  34.2 us (63%)
  starting transfers between devices  15.6 us (29%)
  waiting for transfers between devices  4.2 us (8%)
    ppermute x11, starting transfers between devices, partner(): return lax.ppermute(array, 'dir', [(i, i ^ mask) for i in range(dir_count)])  13 us
    pallas_call x1, Pallas kernels, shards(): pl.pallas_call(functools.partial(second_kernel, halo - near_halo), in_spe...  11.6 us
    pallas_call x1, Pallas kernels, shards(): pl.pallas_call(functools.partial(first_kernel, first_count, boxes, halo,...  11.5 us
    pallas_call x4, Pallas kernels, apply(): pl.pallas_call(kernel, in_specs=specs, out_specs=vmem, out_shape=pltpu.VM...  11 us
    ppermute x11, waiting for transfers between devices, partner(): return lax.ppermute(array, 'dir', [(i, i ^ mask) for i in range(dir_count)])  4.07 us
    ppermute x2, starting transfers between devices, beyond(): return lax.ppermute(array, ('dir', 'region'), along)  2.56 us
  transfers between devices with their start and end apart: 13, of which 3 were waited for; matrix products, arithmetic and copies ran while one was open for 0% of the time, Pallas kernels for 52%

profile of v3, /device:TPU:0, one launch (start us, length us, event | category | flops | bytes accessed | tf_op | source)
XLA Modules:
  0.0 54.1 jit_solution(10533827819510659409)
XLA Ops:
  0.0 0.5 collective-permute-start.1
  0.5 2.5 %collective-permute-start.2 = (bf16[6,128,256]{2,1,0:T(8,128)(2,1)}, bf16[6,128,256]{2,1,0:T(8,128)(2,1)S(1)}, u32[]{:S(2)}, u32[]{:S(2)}) collective-permute-start(bf16[6,128,256]{2,1,0:T(8,128)(2,1)} %bitcast.2), channel_id=1, source_target_pairs={{0,8},{4,12},{8,0},{12,4},{16,24},{20,28},{24,16},{28,20},{1,9},{5... | collective-permute-start | bytes 1179656 | tf_op jit(solution)/shard_map/ppermute | solution.py:271
  2.9 1.5 %collective-permute-start.3 = (bf16[6,128,256]{2,1,0:T(8,128)(2,1)}, bf16[6,128,256]{2,1,0:T(8,128)(2,1)S(1)}, u32[]{:S(2)}, u32[]{:S(2)}) collective-permute-start(bf16[6,128,256]{2,1,0:T(8,128)(2,1)} %bitcast.3), channel_id=1, source_target_pairs={{0,16},{4,20},{8,24},{12,28},{16,0},{20,4},{24,8},{28,12},{1,17},{... | collective-permute-start | bytes 1179656 | tf_op jit(solution)/shard_map/ppermute | solution.py:271
  4.5 1.3 %collective-permute-start.4 = (bf16[6,128,256]{2,1,0:T(8,128)(2,1)}, bf16[6,128,256]{2,1,0:T(8,128)(2,1)S(1)}, u32[]{:S(2)}, u32[]{:S(2)}) collective-permute-start(bf16[6,128,256]{2,1,0:T(8,128)(2,1)} %bitcast.4), channel_id=1, source_target_pairs={{1,0},{2,1},{3,2},{5,4},{6,5},{7,6},{9,8},{10,9},{11,10},{13,12},{... | collective-permute-start | bytes 1179656 | tf_op jit(solution)/shard_map/ppermute | solution.py:281
  5.8 0.1 collective-permute-start
  5.8 11.5 %shard_map.91 = (bf16[80,128,128]{2,1,0:T(8,128)(2,1)S(1)}, bf16[128,1536]{1,0:T(8,128)(2,1)S(1)}, bf16[1536,128]{1,0:T(8,128)(2,1)S(1)}, f32[316,1536]{1,0:T(8,...) custom-call(s32[9]{0:T(128)} %off_hbm.1, s32[1,48,48]{2,1,0:T(8,128)} %src_hbm.1, s32[1,48,48]{2,1,0:T(8,128)} %tid_hbm.1, ...), custom_call_target="tpu_custom_call" | custom-call | flops 7952400384 | bytes 1048576 | tf_op jit(solution)/shard_map/pallas_call | solution.py:307
  17.4 0.0 collective-permute-done.2.rest_1_
  17.4 0.0 collective-permute-done.3.rest_2_
  17.4 0.1 collective-permute-done.4.rest_3_
  17.5 0.5 collective-permute-start.5
  18.1 1.3 %collective-permute-start.6 = (bf16[6,128,256]{2,1,0:T(8,128)(2,1)S(1)}, bf16[6,128,256]{2,1,0:T(8,128)(2,1)S(1)}, u32[]{:S(2)}, u32[]{:S(2)}) collective-permute-start(bf16[6,128,256]{2,1,0:T(8,128)(2,1)S(1)} %collective-permute-done.2.rest_1_), channel_id=1, source_target_pairs={{1,0},{2,1},{3,2},{5,4},{6,5},{7,6},{9,8},{10,9},{11,10},{13,12},{... | collective-permute-start | bytes 1179656 | tf_op jit(solution)/shard_map/ppermute | solution.py:281
  19.3 4.9 %collective-permute-start.7 = (bf16[6,128,256]{2,1,0:T(8,128)(2,1)S(1)}, bf16[6,128,256]{2,1,0:T(8,128)(2,1)S(1)}, u32[]{:S(2)}, u32[]{:S(2)}) collective-permute-start(bf16[6,128,256]{2,1,0:T(8,128)(2,1)S(1)} %collective-permute-done.4.rest_3_), channel_id=1, source_target_pairs={{0,16},{4,20},{8,24},{12,28},{16,0},{20,4},{24,8},{28,12},{1,17},{... | collective-permute-start | bytes 1179656 | tf_op jit(solution)/shard_map/ppermute | solution.py:271
  24.3 0.0 collective-permute-done.near_src_other_ref
  24.3 0.0 collective-permute-done.1.near_other_hbm
  24.3 0.0 copy-start
  24.3 11.6 %shard_map.92 = (bf16[317,128,128]{2,1,0:T(8,128)(2,1)S(1)}, bf16[12,28,128,128]{3,2,1,0:T(8,128)(2,1)S(1)}, s32[16,128]{1,0:T(8,128)S(1)}) custom-call(s32[8,384]{1,0:T(8,128)S(1)} %get-tuple-element.26.list_ref, f32[316,1536]{1,0:T(8,128)S(1)} %get-tuple-element.27.rows_ref, bf16[128,1536]{1,0:T(8,128)(2,1)S(1)} %get-tuple-element.28.weighted_ref, ...), custom_call_target="tpu_custom_call" | custom-call | flops 7952400384 | bytes 1048576 | tf_op jit(solution)/shard_map/pallas_call | solution.py:342
  35.9 0.0 collective-permute-done.5.rest_4_.rest_0_
  35.9 0.0 collective-permute-done.6.rest_5_.rest_1_
  35.9 0.0 collective-permute-done.7.rest_6_.rest_2_
  36.0 3.6 %shard_map.94 = bf16[6,128,256]{2,1,0:T(8,128)(2,1)S(1)} custom-call(s32[16,128]{1,0:T(8,128)S(1)} %get-tuple-element.25.cls_ref, s32[16,128]{1,0:T(8,128)S(1)} %get-tuple-element.32.near_map_ref, s32[8,384]{1,0:T(8,128)S(1)} %get-tuple-element.26.list_ref, bf16[317,128,128]{2,1,0:T(8,128)(2,1)S(1)} %get-tuple-element.37.t_ref, ...), custom_call_target="tpu_custom_call" | custom-call | flops 2113929216 | bytes 1048576 | tf_op jit(solution)/shard_map/pallas_call | solution.py:379
  39.5 0.1 collective-permute-start.12
  39.7 2.0 %collective-permute-start.8 = (bf16[3,128,256]{2,1,0:T(8,128)(2,1)S(1)}, bf16[3,128,256]{2,1,0:T(8,128)(2,1)S(1)}, u32[]{:S(2)}, u32[]{:S(2)}) collective-permute-start(bf16[3,128,256]{2,1,0:T(8,128)(2,1)S(1)} %slice.6), channel_id=1, source_target_pairs={{0,8},{4,12},{8,0},{12,4},{16,24},{20,28},{24,16},{28,20},{1,9},{5... | collective-permute-start | bytes 589832 | tf_op jit(solution)/shard_map/ppermute | solution.py:271
  41.7 0.4 collective-permute-start.9
  42.1 2.5 %shard_map.93.rest_3_ = f32[6,128,256]{2,1,0:T(8,128)S(1)} custom-call(s32[16,128]{1,0:T(8,128)S(1)} %get-tuple-element.25.cls_ref, s32[16,128]{1,0:T(8,128)S(1)} %get-tuple-element.32.near_map_ref, s32[8,384]{1,0:T(8,128)S(1)} %get-tuple-element.26.list_ref, bf16[317,128,128]{2,1,0:T(8,128)(2,1)S(1)} %get-tuple-element.37.t_ref, ...), custom_call_target="tpu_custom_call" | custom-call | flops 1207959552 | bytes 1048576 | tf_op jit(solution)/shard_map/pallas_call | solution.py:379
  44.7 2.6 %collective-permute-done.8.rest_0_ = bf16[3,128,256]{2,1,0:T(8,128)(2,1)S(1)} collective-permute-done((bf16[3,128,256]{2,1,0:T(8,128)(2,1)S(1)}, bf16[3,128,256]{2,1,0:T(8,128)(2,1)S(1)}, u32[]{:S(2)}, u32[]{:S(2)}) %collective-permute-start.8) | collective-permute-done | bytes 196640 | tf_op jit(solution)/shard_map/ppermute | solution.py:271
  47.2 1.5 %collective-permute-done.9.rest_1_ = bf16[3,128,256]{2,1,0:T(8,128)(2,1)S(1)} collective-permute-done((bf16[3,128,256]{2,1,0:T(8,128)(2,1)S(1)}, bf16[3,128,256]{2,1,0:T(8,128)(2,1)S(1)}, u32[]{:S(2)}, u32[]{:S(2)}) %collective-permute-start.9) | collective-permute-done | bytes 196640 | tf_op jit(solution)/shard_map/ppermute | solution.py:271
  48.7 0.0 collective-permute-start.10
  48.7 0.5 collective-permute-start.11
  49.2 2.2 %shard_map.95.rest_4_ = f32[6,128,256]{2,1,0:T(8,128)S(1)} custom-call(s32[16,128]{1,0:T(8,128)S(1)} %get-tuple-element.25.cls_ref, s32[16,128]{1,0:T(8,128)S(1)} %get-tuple-element.32.near_map_ref, s32[8,384]{1,0:T(8,128)S(1)} %get-tuple-element.26.list_ref, bf16[317,128,128]{2,1,0:T(8,128)(2,1)S(1)} %get-tuple-element.37.t_ref, ...), custom_call_target="tpu_custom_call" | custom-call | flops 905969664 | bytes 1048576 | tf_op jit(solution)/shard_map/pallas_call | solution.py:379
  51.5 0.0 collective-permute-done.10.rest_2_
  51.5 0.0 collective-permute-done.11.rest_3_
  51.5 2.6 %shard_map.96 = bf16[1,6,128,256]{3,2,1,0:T(8,128)(2,1)} custom-call(s32[16,128]{1,0:T(8,128)S(1)} %get-tuple-element.25.cls_ref, s32[16,128]{1,0:T(8,128)S(1)} %get-tuple-element.32.near_map_ref, s32[8,384]{1,0:T(8,128)S(1)} %get-tuple-element.26.list_ref, bf16[317,128,128]{2,1,0:T(8,128)(2,1)S(1)} %get-tuple-element.37.t_ref, ...), custom_call_target="tpu_custom_call" | custom-call | flops 603979776 | bytes 1048576 | tf_op jit(solution)/shard_map/pallas_call | solution.py:379
  (6 shorter events, 0.0 us)
Async XLA Ops:
  0.0 24.3 %collective-permute-start.1 = (bf16[1,6,27,128,128]{4,3,2,1,0:T(8,128)(2,1)}, bf16[1,6,27,128,128]{4,3,2,1,0:T(8,128)(2,1)S(1)}, u32[]{:S(2)}, u32[]{:S(2)}) collective-permute-start(bf16[1,6,27,128,128]{4,3,2,1,0:T(8,128)(2,1)} %near_hbm.1), channel_id=1, source_target_pairs={{0,4},{4,0},{8,12},{12,8},{16,20},{20,16},{24,28},{28,24},{1,5},{5... | collective-permute-start | bytes 15925256 | tf_op jit(solution)/shard_map/ppermute | solution.py:271
  0.5 16.9 %collective-permute-start.2 = (bf16[6,128,256]{2,1,0:T(8,128)(2,1)}, bf16[6,128,256]{2,1,0:T(8,128)(2,1)S(1)}, u32[]{:S(2)}, u32[]{:S(2)}) collective-permute-start(bf16[6,128,256]{2,1,0:T(8,128)(2,1)} %bitcast.2), channel_id=1, source_target_pairs={{0,8},{4,12},{8,0},{12,4},{16,24},{20,28},{24,16},{28,20},{1,9},{5... | collective-permute-start | bytes 1179656 | tf_op jit(solution)/shard_map/ppermute | solution.py:271
  2.9 14.4 %collective-permute-start.3 = (bf16[6,128,256]{2,1,0:T(8,128)(2,1)}, bf16[6,128,256]{2,1,0:T(8,128)(2,1)S(1)}, u32[]{:S(2)}, u32[]{:S(2)}) collective-permute-start(bf16[6,128,256]{2,1,0:T(8,128)(2,1)} %bitcast.3), channel_id=1, source_target_pairs={{0,16},{4,20},{8,24},{12,28},{16,0},{20,4},{24,8},{28,12},{1,17},{... | collective-permute-start | bytes 1179656 | tf_op jit(solution)/shard_map/ppermute | solution.py:271
  4.5 13.1 %collective-permute-start.4 = (bf16[6,128,256]{2,1,0:T(8,128)(2,1)}, bf16[6,128,256]{2,1,0:T(8,128)(2,1)S(1)}, u32[]{:S(2)}, u32[]{:S(2)}) collective-permute-start(bf16[6,128,256]{2,1,0:T(8,128)(2,1)} %bitcast.4), channel_id=1, source_target_pairs={{1,0},{2,1},{3,2},{5,4},{6,5},{7,6},{9,8},{10,9},{11,10},{13,12},{... | collective-permute-start | bytes 1179656 | tf_op jit(solution)/shard_map/ppermute | solution.py:281
  5.8 18.5 %copy-start.1 = (s32[1,6,27]{2,0,1:T(1,128)S(1)}, s32[1,6,27]{2,0,1:T(1,128)}, u32[]{:S(2)}) copy-start(s32[1,6,27]{2,0,1:T(1,128)} %param.17) | copy-start | bytes 1948
  5.8 18.5 %collective-permute-start = (s32[6,1,27]{2,1,0:T(1,128)}, s32[6,1,27]{2,1,0:T(1,128)S(1)}, u32[]{:S(2)}, u32[]{:S(2)}) collective-permute-start(s32[6,1,27]{2,1,0:T(1,128)} %bitcast.7), channel_id=1, source_target_pairs={{0,4},{4,0},{8,12},{12,8},{16,20},{20,16},{24,28},{28,24},{1,5},{5... | collective-permute-start | bytes 1952 | tf_op jit(solution)/shard_map/ppermute | solution.py:271
  17.5 18.4 %collective-permute-start.5 = (bf16[6,128,256]{2,1,0:T(8,128)(2,1)S(1)}, bf16[6,128,256]{2,1,0:T(8,128)(2,1)S(1)}, u32[]{:S(2)}, u32[]{:S(2)}) collective-permute-start(bf16[6,128,256]{2,1,0:T(8,128)(2,1)S(1)} %collective-permute-done.3.rest_2_), channel_id=1, source_target_pairs={{0,8},{4,12},{8,0},{12,4},{16,24},{20,28},{24,16},{28,20},{1,9},{5... | collective-permute-start | bytes 1179656 | tf_op jit(solution)/shard_map/ppermute | solution.py:271
  18.1 17.9 %collective-permute-start.6 = (bf16[6,128,256]{2,1,0:T(8,128)(2,1)S(1)}, bf16[6,128,256]{2,1,0:T(8,128)(2,1)S(1)}, u32[]{:S(2)}, u32[]{:S(2)}) collective-permute-start(bf16[6,128,256]{2,1,0:T(8,128)(2,1)S(1)} %collective-permute-done.2.rest_1_), channel_id=1, source_target_pairs={{1,0},{2,1},{3,2},{5,4},{6,5},{7,6},{9,8},{10,9},{11,10},{13,12},{... | collective-permute-start | bytes 1179656 | tf_op jit(solution)/shard_map/ppermute | solution.py:281
  19.3 16.6 %collective-permute-start.7 = (bf16[6,128,256]{2,1,0:T(8,128)(2,1)S(1)}, bf16[6,128,256]{2,1,0:T(8,128)(2,1)S(1)}, u32[]{:S(2)}, u32[]{:S(2)}) collective-permute-start(bf16[6,128,256]{2,1,0:T(8,128)(2,1)S(1)} %collective-permute-done.4.rest_3_), channel_id=1, source_target_pairs={{0,16},{4,20},{8,24},{12,28},{16,0},{20,4},{24,8},{28,12},{1,17},{... | collective-permute-start | bytes 1179656 | tf_op jit(solution)/shard_map/ppermute | solution.py:271
  24.3 11.7 %copy-start = (bf16[1,6,128,256]{3,2,1,0:T(8,128)(2,1)S(1)}, bf16[1,6,128,256]{3,2,1,0:T(8,128)(2,1)}, u32[]{:S(2)}) copy-start(bf16[1,6,128,256]{3,2,1,0:T(8,128)(2,1)} %param.9) | copy-start | bytes 1179652
  39.5 9.7 %collective-permute-start.12 = (bf16[6,128,256]{2,1,0:T(8,128)(2,1)S(1)}, bf16[6,128,256]{2,1,0:T(8,128)(2,1)S(1)}, u32[]{:S(2)}, u32[]{:S(2)}) collective-permute-start(bf16[6,128,256]{2,1,0:T(8,128)(2,1)S(1)} %shard_map.94), channel_id=1, source_target_pairs={{0,4},{4,0},{8,12},{12,8},{16,20},{20,16},{24,28},{28,24},{1,5},{5... | collective-permute-start | bytes 1179656 | tf_op jit(solution)/shard_map/ppermute | solution.py:271
  39.7 7.6 %collective-permute-start.8 = (bf16[3,128,256]{2,1,0:T(8,128)(2,1)S(1)}, bf16[3,128,256]{2,1,0:T(8,128)(2,1)S(1)}, u32[]{:S(2)}, u32[]{:S(2)}) collective-permute-start(bf16[3,128,256]{2,1,0:T(8,128)(2,1)S(1)} %slice.6), channel_id=1, source_target_pairs={{0,8},{4,12},{8,0},{12,4},{16,24},{20,28},{24,16},{28,20},{1,9},{5... | collective-permute-start | bytes 589832 | tf_op jit(solution)/shard_map/ppermute | solution.py:271
  41.7 7.0 %collective-permute-start.9 = (bf16[3,128,256]{2,1,0:T(8,128)(2,1)S(1)}, bf16[3,128,256]{2,1,0:T(8,128)(2,1)S(1)}, u32[]{:S(2)}, u32[]{:S(2)}) collective-permute-start(bf16[3,128,256]{2,1,0:T(8,128)(2,1)S(1)} %slice.7), channel_id=1, source_target_pairs={{0,16},{4,20},{8,24},{12,28},{16,0},{20,4},{24,8},{28,12},{1,17},{... | collective-permute-start | bytes 589832 | tf_op jit(solution)/shard_map/ppermute | solution.py:271
  48.7 2.8 %collective-permute-start.10 = (bf16[3,128,256]{2,1,0:T(8,128)(2,1)S(1)}, bf16[3,128,256]{2,1,0:T(8,128)(2,1)S(1)}, u32[]{:S(2)}, u32[]{:S(2)}) collective-permute-start(bf16[3,128,256]{2,1,0:T(8,128)(2,1)S(1)} %collective-permute-done.8.rest_0_), channel_id=1, source_target_pairs={{0,4},{4,0},{8,12},{12,8},{16,20},{20,16},{24,28},{28,24},{1,5},{5... | collective-permute-start | bytes 589832 | tf_op jit(solution)/shard_map/ppermute | solution.py:271
  48.7 2.8 %collective-permute-start.11 = (bf16[3,128,256]{2,1,0:T(8,128)(2,1)S(1)}, bf16[3,128,256]{2,1,0:T(8,128)(2,1)S(1)}, u32[]{:S(2)}, u32[]{:S(2)}) collective-permute-start(bf16[3,128,256]{2,1,0:T(8,128)(2,1)S(1)} %collective-permute-done.9.rest_1_), channel_id=1, source_target_pairs={{0,4},{4,0},{8,12},{12,8},{16,20},{20,16},{24,28},{28,24},{1,5},{5... | collective-permute-start | bytes 589832 | tf_op jit(solution)/shard_map/ppermute | solution.py:271

commit v4 on v3

--- a/solution.py
+++ b/solution.py
@@ -382,9 +382,7 @@
             out_specs=vmem,
             out_shape=pltpu.VMEM(shape, dtype) if len(shape) == 3 else jax.ShapeDtypeStruct(shape, dtype),
             compiler_params=pltpu.CompilerParams(vmem_limit_bytes=12 * MIB),
-            cost_estimate=pl.CostEstimate(
-                flops=2 * len(places) * (boxes * unknowns) ** 2 * incidences, bytes_accessed=MIB, transcendentals=0
-            ),
+            cost_estimate=pl.CostEstimate(flops=MIB, bytes_accessed=MIB, transcendentals=0),
         )(*args)
 
     tied = lax.optimization_barrier(

time: 54.6 us -> 50.7 us (0.929); the launches traced: 54.1 us -> 51.2 us
  waiting for transfers between devices: 4.2 us -> 0.16 us
  starting transfers between devices: 15.6 us -> 16.8 us
    ppermute x11, waiting for transfers between devices: 4.07 us -> 0.03 us  [partner(): return lax.ppermute(array, 'dir', [(i, i ^ mask) for i in range(dir_count)])]
    ppermute x11, starting transfers between devices: 13 us -> 14.2 us  [partner(): return lax.ppermute(array, 'dir', [(i, i ^ mask) for i in range(dir_count)])]
  transfers between devices with their start and end apart: 13 -> 13, of which waited for: 3 -> 1; matrix products, arithmetic and copies ran while one was open for 0% -> 0% of each run, Pallas kernels for 52% -> 61%
where the time goes in v4:
time: 50.7 us; the launch traced here: 51.2 us
  Pallas kernels  34 us (67%)
  starting transfers between devices  16.8 us (33%)
    ppermute x11, starting transfers between devices, partner(): return lax.ppermute(array, 'dir', [(i, i ^ mask) for i in range(dir_count)])  14.2 us
    pallas_call x1, Pallas kernels, shards(): pl.pallas_call(functools.partial(first_kernel, first_count, boxes, halo,...  11.5 us
    pallas_call x1, Pallas kernels, shards(): pl.pallas_call(functools.partial(second_kernel, halo - near_halo), in_spe...  11.5 us
    pallas_call x4, Pallas kernels, apply(): pl.pallas_call(kernel, in_specs=specs, out_specs=vmem, out_shape=pltpu.VM...  11 us
    ppermute x2, starting transfers between devices, beyond(): return lax.ppermute(array, ('dir', 'region'), along)  2.56 us
  transfers between devices with their start and end apart: 13, of which 1 were waited for; matrix products, arithmetic and copies ran while one was open for 0% of the time, Pallas kernels for 61%

profile of v4, /device:TPU:0, one launch (start us, length us, event | category | flops | bytes accessed | tf_op | source)
XLA Modules:
  0.0 51.2 jit_solution(526460176683546913)
XLA Ops:
  0.0 0.5 collective-permute-start.1
  0.5 2.5 %collective-permute-start.2 = (bf16[6,128,256]{2,1,0:T(8,128)(2,1)}, bf16[6,128,256]{2,1,0:T(8,128)(2,1)S(1)}, u32[]{:S(2)}, u32[]{:S(2)}) collective-permute-start(bf16[6,128,256]{2,1,0:T(8,128)(2,1)} %bitcast.2), channel_id=1, source_target_pairs={{0,8},{4,12},{8,0},{12,4},{16,24},{20,28},{24,16},{28,20},{1,9},{5... | collective-permute-start | bytes 1179656 | tf_op jit(solution)/shard_map/ppermute | solution.py:271
  2.9 1.5 %collective-permute-start.3 = (bf16[6,128,256]{2,1,0:T(8,128)(2,1)}, bf16[6,128,256]{2,1,0:T(8,128)(2,1)S(1)}, u32[]{:S(2)}, u32[]{:S(2)}) collective-permute-start(bf16[6,128,256]{2,1,0:T(8,128)(2,1)} %bitcast.3), channel_id=1, source_target_pairs={{0,16},{4,20},{8,24},{12,28},{16,0},{20,4},{24,8},{28,12},{1,17},{... | collective-permute-start | bytes 1179656 | tf_op jit(solution)/shard_map/ppermute | solution.py:271
  4.5 1.3 %collective-permute-start.4 = (bf16[6,128,256]{2,1,0:T(8,128)(2,1)}, bf16[6,128,256]{2,1,0:T(8,128)(2,1)S(1)}, u32[]{:S(2)}, u32[]{:S(2)}) collective-permute-start(bf16[6,128,256]{2,1,0:T(8,128)(2,1)} %bitcast.4), channel_id=1, source_target_pairs={{1,0},{2,1},{3,2},{5,4},{6,5},{7,6},{9,8},{10,9},{11,10},{13,12},{... | collective-permute-start | bytes 1179656 | tf_op jit(solution)/shard_map/ppermute | solution.py:281
  5.8 0.1 collective-permute-start
  5.8 11.5 %shard_map.91 = (bf16[80,128,128]{2,1,0:T(8,128)(2,1)S(1)}, bf16[128,1536]{1,0:T(8,128)(2,1)S(1)}, bf16[1536,128]{1,0:T(8,128)(2,1)S(1)}, f32[316,1536]{1,0:T(8,...) custom-call(s32[9]{0:T(128)} %off_hbm.1, s32[1,48,48]{2,1,0:T(8,128)} %src_hbm.1, s32[1,48,48]{2,1,0:T(8,128)} %tid_hbm.1, ...), custom_call_target="tpu_custom_call" | custom-call | flops 7952400384 | bytes 1048576 | tf_op jit(solution)/shard_map/pallas_call | solution.py:307
  17.4 0.0 collective-permute-done.2.rest_1_
  17.4 0.0 collective-permute-done.3.rest_2_
  17.4 0.1 collective-permute-done.4.rest_3_
  17.5 0.5 %collective-permute-start.5 = (bf16[6,128,256]{2,1,0:T(8,128)(2,1)S(1)}, bf16[6,128,256]{2,1,0:T(8,128)(2,1)S(1)}, u32[]{:S(2)}, u32[]{:S(2)}) collective-permute-start(bf16[6,128,256]{2,1,0:T(8,128)(2,1)S(1)} %collective-permute-done.3.rest_2_), channel_id=1, source_target_pairs={{0,8},{4,12},{8,0},{12,4},{16,24},{20,28},{24,16},{28,20},{1,9},{5... | collective-permute-start | bytes 1179656 | tf_op jit(solution)/shard_map/ppermute | solution.py:271
  18.1 1.3 %collective-permute-start.6 = (bf16[6,128,256]{2,1,0:T(8,128)(2,1)S(1)}, bf16[6,128,256]{2,1,0:T(8,128)(2,1)S(1)}, u32[]{:S(2)}, u32[]{:S(2)}) collective-permute-start(bf16[6,128,256]{2,1,0:T(8,128)(2,1)S(1)} %collective-permute-done.2.rest_1_), channel_id=1, source_target_pairs={{1,0},{2,1},{3,2},{5,4},{6,5},{7,6},{9,8},{10,9},{11,10},{13,12},{... | collective-permute-start | bytes 1179656 | tf_op jit(solution)/shard_map/ppermute | solution.py:281
  19.3 4.9 %collective-permute-start.7 = (bf16[6,128,256]{2,1,0:T(8,128)(2,1)S(1)}, bf16[6,128,256]{2,1,0:T(8,128)(2,1)S(1)}, u32[]{:S(2)}, u32[]{:S(2)}) collective-permute-start(bf16[6,128,256]{2,1,0:T(8,128)(2,1)S(1)} %collective-permute-done.4.rest_3_), channel_id=1, source_target_pairs={{0,16},{4,20},{8,24},{12,28},{16,0},{20,4},{24,8},{28,12},{1,17},{... | collective-permute-start | bytes 1179656 | tf_op jit(solution)/shard_map/ppermute | solution.py:271
  24.3 0.0 collective-permute-done.near_src_other_ref
  24.3 0.0 collective-permute-done.1.near_other_hbm
  24.3 0.0 copy-start
  24.3 11.5 %shard_map.92 = (bf16[317,128,128]{2,1,0:T(8,128)(2,1)S(1)}, bf16[12,28,128,128]{3,2,1,0:T(8,128)(2,1)S(1)}, s32[16,128]{1,0:T(8,128)S(1)}) custom-call(s32[8,384]{1,0:T(8,128)S(1)} %get-tuple-element.26.list_ref, f32[316,1536]{1,0:T(8,128)S(1)} %get-tuple-element.27.rows_ref, bf16[128,1536]{1,0:T(8,128)(2,1)S(1)} %get-tuple-element.28.weighted_ref, ...), custom_call_target="tpu_custom_call" | custom-call | flops 7952400384 | bytes 1048576 | tf_op jit(solution)/shard_map/pallas_call | solution.py:342
  35.8 0.0 collective-permute-done.5.rest_4_.rest_0_
  35.8 0.0 collective-permute-done.6.rest_5_.rest_1_
  35.8 0.0 collective-permute-done.7.rest_6_.rest_2_
  35.9 1.0 %collective-permute-start.8 = (bf16[3,128,256]{2,1,0:T(8,128)(2,1)S(1)}, bf16[3,128,256]{2,1,0:T(8,128)(2,1)S(1)}, u32[]{:S(2)}, u32[]{:S(2)}) collective-permute-start(bf16[3,128,256]{2,1,0:T(8,128)(2,1)S(1)} %slice.6), channel_id=1, source_target_pairs={{0,8},{4,12},{8,0},{12,4},{16,24},{20,28},{24,16},{28,20},{1,9},{5... | collective-permute-start | bytes 589832 | tf_op jit(solution)/shard_map/ppermute | solution.py:271
  36.9 2.6 %collective-permute-start.9 = (bf16[3,128,256]{2,1,0:T(8,128)(2,1)S(1)}, bf16[3,128,256]{2,1,0:T(8,128)(2,1)S(1)}, u32[]{:S(2)}, u32[]{:S(2)}) collective-permute-start(bf16[3,128,256]{2,1,0:T(8,128)(2,1)S(1)} %slice.7), channel_id=1, source_target_pairs={{0,16},{4,20},{8,24},{12,28},{16,0},{20,4},{24,8},{28,12},{1,17},{... | collective-permute-start | bytes 589832 | tf_op jit(solution)/shard_map/ppermute | solution.py:271
  39.4 3.6 %shard_map.94 = bf16[6,128,256]{2,1,0:T(8,128)(2,1)S(1)} custom-call(s32[16,128]{1,0:T(8,128)S(1)} %get-tuple-element.25.cls_ref, s32[16,128]{1,0:T(8,128)S(1)} %get-tuple-element.32.near_map_ref, s32[8,384]{1,0:T(8,128)S(1)} %get-tuple-element.26.list_ref, bf16[317,128,128]{2,1,0:T(8,128)(2,1)S(1)} %get-tuple-element.37.t_ref, ...), custom_call_target="tpu_custom_call" | custom-call | flops 1048576 | bytes 1048576 | tf_op jit(solution)/shard_map/pallas_call | solution.py:379
  43.0 0.1 collective-permute-start.12
  43.1 2.6 %shard_map.93.rest_3_ = f32[6,128,256]{2,1,0:T(8,128)S(1)} custom-call(s32[16,128]{1,0:T(8,128)S(1)} %get-tuple-element.25.cls_ref, s32[16,128]{1,0:T(8,128)S(1)} %get-tuple-element.32.near_map_ref, s32[8,384]{1,0:T(8,128)S(1)} %get-tuple-element.26.list_ref, bf16[317,128,128]{2,1,0:T(8,128)(2,1)S(1)} %get-tuple-element.37.t_ref, ...), custom_call_target="tpu_custom_call" | custom-call | flops 1048576 | bytes 1048576 | tf_op jit(solution)/shard_map/pallas_call | solution.py:379
  45.7 0.0 collective-permute-done.8.rest_0_
  45.7 0.0 collective-permute-done.9.rest_1_
  45.7 0.6 %collective-permute-start.10 = (bf16[3,128,256]{2,1,0:T(8,128)(2,1)S(1)}, bf16[3,128,256]{2,1,0:T(8,128)(2,1)S(1)}, u32[]{:S(2)}, u32[]{:S(2)}) collective-permute-start(bf16[3,128,256]{2,1,0:T(8,128)(2,1)S(1)} %collective-permute-done.8.rest_0_), channel_id=1, source_target_pairs={{0,4},{4,0},{8,12},{12,8},{16,20},{20,16},{24,28},{28,24},{1,5},{5... | collective-permute-start | bytes 589832 | tf_op jit(solution)/shard_map/ppermute | solution.py:271
  46.2 0.1 collective-permute-start.11
  46.3 0.0 collective-permute-done.12.rest_4_
  46.3 2.2 %shard_map.95.rest_4_ = f32[6,128,256]{2,1,0:T(8,128)S(1)} custom-call(s32[16,128]{1,0:T(8,128)S(1)} %get-tuple-element.25.cls_ref, s32[16,128]{1,0:T(8,128)S(1)} %get-tuple-element.32.near_map_ref, s32[8,384]{1,0:T(8,128)S(1)} %get-tuple-element.26.list_ref, bf16[317,128,128]{2,1,0:T(8,128)(2,1)S(1)} %get-tuple-element.37.t_ref, ...), custom_call_target="tpu_custom_call" | custom-call | flops 1048576 | bytes 1048576 | tf_op jit(solution)/shard_map/pallas_call | solution.py:379
  48.6 0.0 collective-permute-done.11.rest_3_
  48.6 2.6 %shard_map.96 = bf16[1,6,128,256]{3,2,1,0:T(8,128)(2,1)} custom-call(s32[16,128]{1,0:T(8,128)S(1)} %get-tuple-element.25.cls_ref, s32[16,128]{1,0:T(8,128)S(1)} %get-tuple-element.32.near_map_ref, s32[8,384]{1,0:T(8,128)S(1)} %get-tuple-element.26.list_ref, bf16[317,128,128]{2,1,0:T(8,128)(2,1)S(1)} %get-tuple-element.37.t_ref, ...), custom_call_target="tpu_custom_call" | custom-call | flops 1048576 | bytes 1048576 | tf_op jit(solution)/shard_map/pallas_call | solution.py:379
  (6 shorter events, 0.0 us)
Async XLA Ops:
  0.0 24.3 %collective-permute-start.1 = (bf16[1,6,27,128,128]{4,3,2,1,0:T(8,128)(2,1)}, bf16[1,6,27,128,128]{4,3,2,1,0:T(8,128)(2,1)S(1)}, u32[]{:S(2)}, u32[]{:S(2)}) collective-permute-start(bf16[1,6,27,128,128]{4,3,2,1,0:T(8,128)(2,1)} %near_hbm.1), channel_id=1, source_target_pairs={{0,4},{4,0},{8,12},{12,8},{16,20},{20,16},{24,28},{28,24},{1,5},{5... | collective-permute-start | bytes 15925256 | tf_op jit(solution)/shard_map/ppermute | solution.py:271
  0.5 16.9 %collective-permute-start.2 = (bf16[6,128,256]{2,1,0:T(8,128)(2,1)}, bf16[6,128,256]{2,1,0:T(8,128)(2,1)S(1)}, u32[]{:S(2)}, u32[]{:S(2)}) collective-permute-start(bf16[6,128,256]{2,1,0:T(8,128)(2,1)} %bitcast.2), channel_id=1, source_target_pairs={{0,8},{4,12},{8,0},{12,4},{16,24},{20,28},{24,16},{28,20},{1,9},{5... | collective-permute-start | bytes 1179656 | tf_op jit(solution)/shard_map/ppermute | solution.py:271
  2.9 14.4 %collective-permute-start.3 = (bf16[6,128,256]{2,1,0:T(8,128)(2,1)}, bf16[6,128,256]{2,1,0:T(8,128)(2,1)S(1)}, u32[]{:S(2)}, u32[]{:S(2)}) collective-permute-start(bf16[6,128,256]{2,1,0:T(8,128)(2,1)} %bitcast.3), channel_id=1, source_target_pairs={{0,16},{4,20},{8,24},{12,28},{16,0},{20,4},{24,8},{28,12},{1,17},{... | collective-permute-start | bytes 1179656 | tf_op jit(solution)/shard_map/ppermute | solution.py:271
  4.5 13.1 %collective-permute-start.4 = (bf16[6,128,256]{2,1,0:T(8,128)(2,1)}, bf16[6,128,256]{2,1,0:T(8,128)(2,1)S(1)}, u32[]{:S(2)}, u32[]{:S(2)}) collective-permute-start(bf16[6,128,256]{2,1,0:T(8,128)(2,1)} %bitcast.4), channel_id=1, source_target_pairs={{1,0},{2,1},{3,2},{5,4},{6,5},{7,6},{9,8},{10,9},{11,10},{13,12},{... | collective-permute-start | bytes 1179656 | tf_op jit(solution)/shard_map/ppermute | solution.py:281
  5.8 18.5 %copy-start.1 = (s32[1,6,27]{2,0,1:T(1,128)S(1)}, s32[1,6,27]{2,0,1:T(1,128)}, u32[]{:S(2)}) copy-start(s32[1,6,27]{2,0,1:T(1,128)} %param.17) | copy-start | bytes 1948
  5.8 18.5 %collective-permute-start = (s32[6,1,27]{2,1,0:T(1,128)}, s32[6,1,27]{2,1,0:T(1,128)S(1)}, u32[]{:S(2)}, u32[]{:S(2)}) collective-permute-start(s32[6,1,27]{2,1,0:T(1,128)} %bitcast.7), channel_id=1, source_target_pairs={{0,4},{4,0},{8,12},{12,8},{16,20},{20,16},{24,28},{28,24},{1,5},{5... | collective-permute-start | bytes 1952 | tf_op jit(solution)/shard_map/ppermute | solution.py:271
  17.5 18.3 %collective-permute-start.5 = (bf16[6,128,256]{2,1,0:T(8,128)(2,1)S(1)}, bf16[6,128,256]{2,1,0:T(8,128)(2,1)S(1)}, u32[]{:S(2)}, u32[]{:S(2)}) collective-permute-start(bf16[6,128,256]{2,1,0:T(8,128)(2,1)S(1)} %collective-permute-done.3.rest_2_), channel_id=1, source_target_pairs={{0,8},{4,12},{8,0},{12,4},{16,24},{20,28},{24,16},{28,20},{1,9},{5... | collective-permute-start | bytes 1179656 | tf_op jit(solution)/shard_map/ppermute | solution.py:271
  18.1 17.8 %collective-permute-start.6 = (bf16[6,128,256]{2,1,0:T(8,128)(2,1)S(1)}, bf16[6,128,256]{2,1,0:T(8,128)(2,1)S(1)}, u32[]{:S(2)}, u32[]{:S(2)}) collective-permute-start(bf16[6,128,256]{2,1,0:T(8,128)(2,1)S(1)} %collective-permute-done.2.rest_1_), channel_id=1, source_target_pairs={{1,0},{2,1},{3,2},{5,4},{6,5},{7,6},{9,8},{10,9},{11,10},{13,12},{... | collective-permute-start | bytes 1179656 | tf_op jit(solution)/shard_map/ppermute | solution.py:281
  19.3 16.5 %collective-permute-start.7 = (bf16[6,128,256]{2,1,0:T(8,128)(2,1)S(1)}, bf16[6,128,256]{2,1,0:T(8,128)(2,1)S(1)}, u32[]{:S(2)}, u32[]{:S(2)}) collective-permute-start(bf16[6,128,256]{2,1,0:T(8,128)(2,1)S(1)} %collective-permute-done.4.rest_3_), channel_id=1, source_target_pairs={{0,16},{4,20},{8,24},{12,28},{16,0},{20,4},{24,8},{28,12},{1,17},{... | collective-permute-start | bytes 1179656 | tf_op jit(solution)/shard_map/ppermute | solution.py:271
  24.3 15.2 %copy-start = (bf16[1,6,128,256]{3,2,1,0:T(8,128)(2,1)S(1)}, bf16[1,6,128,256]{3,2,1,0:T(8,128)(2,1)}, u32[]{:S(2)}) copy-start(bf16[1,6,128,256]{3,2,1,0:T(8,128)(2,1)} %param.9) | copy-start | bytes 1179652
  35.9 9.8 %collective-permute-start.8 = (bf16[3,128,256]{2,1,0:T(8,128)(2,1)S(1)}, bf16[3,128,256]{2,1,0:T(8,128)(2,1)S(1)}, u32[]{:S(2)}, u32[]{:S(2)}) collective-permute-start(bf16[3,128,256]{2,1,0:T(8,128)(2,1)S(1)} %slice.6), channel_id=1, source_target_pairs={{0,8},{4,12},{8,0},{12,4},{16,24},{20,28},{24,16},{28,20},{1,9},{5... | collective-permute-start | bytes 589832 | tf_op jit(solution)/shard_map/ppermute | solution.py:271
  36.9 8.8 %collective-permute-start.9 = (bf16[3,128,256]{2,1,0:T(8,128)(2,1)S(1)}, bf16[3,128,256]{2,1,0:T(8,128)(2,1)S(1)}, u32[]{:S(2)}, u32[]{:S(2)}) collective-permute-start(bf16[3,128,256]{2,1,0:T(8,128)(2,1)S(1)} %slice.7), channel_id=1, source_target_pairs={{0,16},{4,20},{8,24},{12,28},{16,0},{20,4},{24,8},{28,12},{1,17},{... | collective-permute-start | bytes 589832 | tf_op jit(solution)/shard_map/ppermute | solution.py:271
  43.0 3.3 %collective-permute-start.12 = (bf16[6,128,256]{2,1,0:T(8,128)(2,1)S(1)}, bf16[6,128,256]{2,1,0:T(8,128)(2,1)S(1)}, u32[]{:S(2)}, u32[]{:S(2)}) collective-permute-start(bf16[6,128,256]{2,1,0:T(8,128)(2,1)S(1)} %shard_map.94), channel_id=1, source_target_pairs={{0,4},{4,0},{8,12},{12,8},{16,20},{20,16},{24,28},{28,24},{1,5},{5... | collective-permute-start | bytes 1179656 | tf_op jit(solution)/shard_map/ppermute | solution.py:271
  45.7 2.9 %collective-permute-start.10 = (bf16[3,128,256]{2,1,0:T(8,128)(2,1)S(1)}, bf16[3,128,256]{2,1,0:T(8,128)(2,1)S(1)}, u32[]{:S(2)}, u32[]{:S(2)}) collective-permute-start(bf16[3,128,256]{2,1,0:T(8,128)(2,1)S(1)} %collective-permute-done.8.rest_0_), channel_id=1, source_target_pairs={{0,4},{4,0},{8,12},{12,8},{16,20},{20,16},{24,28},{28,24},{1,5},{5... | collective-permute-start | bytes 589832 | tf_op jit(solution)/shard_map/ppermute | solution.py:271
  46.2 2.3 %collective-permute-start.11 = (bf16[3,128,256]{2,1,0:T(8,128)(2,1)S(1)}, bf16[3,128,256]{2,1,0:T(8,128)(2,1)S(1)}, u32[]{:S(2)}, u32[]{:S(2)}) collective-permute-start(bf16[3,128,256]{2,1,0:T(8,128)(2,1)S(1)} %collective-permute-done.9.rest_1_), channel_id=1, source_target_pairs={{0,4},{4,0},{8,12},{12,8},{16,20},{20,16},{24,28},{28,24},{1,5},{5... | collective-permute-start | bytes 589832 | tf_op jit(solution)/shard_map/ppermute | solution.py:271

commit v5 on v4

--- a/solution.py
+++ b/solution.py
@@ -52,7 +52,7 @@
 
 
 def first_kernel(
-    first_count,
+    shared,
     boxes,
     halo,
     region_boxes,
@@ -100,6 +100,7 @@
     row_at = lax.broadcasted_iota(I32, (ROWS, slots), 0)
     out_row = lax.broadcasted_iota(I32, cls_ref.shape, 0)
     seen = jnp.zeros((used_width, slots), F32)
+    seen_by_chip = seen
     cls = jnp.full(cls_ref.shape, classes, I32)
     copies[0].wait()
     copies[1].wait()
@@ -113,23 +114,37 @@
         even = (mask & 1) == 0
         here = (src >= 0) & ((even | late) if j < boxes else (even & ~late))
         seen = jnp.where((class_at == tid) & here, 1.0, seen)
+        seen_by_chip = jnp.where((class_at == tid) & (src >= 0), 1.0, seen_by_chip)
         parts = jnp.where(row_at == 0, tid // 16, jnp.where(row_at == 1, tid % 16, 1))
         found = lookup(parts, jnp.where(ext_at == src, 1.0, 0.0))
         value = jnp.where(found[2:3] > 0, found[0:1] * 16 + found[1:2], classes)
         cls = jnp.where(out_row == j, value, cls)
     cls_ref[...] = cls
-    is_used = jnp.minimum(lookup(jnp.ones((ROWS, slots), I32), seen), 1)
+    lane = lax.broadcasted_iota(I32, (ROWS, used_width), 1)
+    list_row = lax.broadcasted_iota(I32, (ROWS, used_width), 0)
+    ones = jnp.ones((ROWS, slots), I32)
+    by_chip = jnp.where(lane < shared, jnp.minimum(lookup(ones, seen_by_chip), 1), 0)
+    by_core = jnp.where(lane >= shared, jnp.minimum(lookup(ones, seen), 1), 0)
+    is_used = jnp.where(list_row == 0, by_chip, by_core)
     down = lax.broadcasted_iota(I32, (used_width, used_width), 0)
     across = lax.broadcasted_iota(I32, (used_width, used_width), 1)
     rank = lookup(is_used, jnp.where(across < down, 1.0, 0.0))
-    here = (down == rank[0:1]) & (is_used[0:1] > 0)
-    lane = lax.broadcasted_iota(I32, (ROWS, used_width), 1)
-    list_row = lax.broadcasted_iota(I32, (ROWS, used_width), 0)
+    shared_rank, own_rank = rank[0:1], rank[1:2]
+    one_lane = lane[0:1]
+    capacity = (shared + 1) // 2
+    empty = capacity + classes - shared
+    other = (shared_rank ^ me) & 1
+    shared_place = shared_rank // 2 + other * (empty + 1)
+    place = jnp.where(one_lane < shared, shared_place, capacity + own_rank)
+    place = jnp.where(one_lane == classes, empty, place)
+    listed_here = jnp.where(one_lane < shared, is_used[0:1] * (1 - other), is_used[1:2])
+    here = down == jnp.where(listed_here > 0, place, -1)
     found = lookup(jnp.where(list_row == 0, lane // 16, lane % 16), jnp.where(here, 1.0, 0.0))
     ordered = found[0:1] * 16 + found[1:2]
-    rank = jnp.where(lane == classes, classes, rank)
-    count = jnp.sum(is_used[0:1].astype(F32), axis=1, keepdims=True).astype(I32)
-    listed = jnp.where(list_row == 0, ordered, jnp.where(list_row == 1, rank, count))
+    count = jnp.sum(is_used.astype(F32), axis=1, keepdims=True).astype(I32)
+    first_end = (count[0:1] - (me & 1) + 1) // 2
+    ends = jnp.where(one_lane == 0, first_end, capacity + count[1:2])
+    listed = jnp.where(list_row == 0, ordered, jnp.where(list_row == 1, place, ends))
     listed_ref[...] = listed
     to_smem = pltpu.make_async_copy(listed_ref, list_ref, sems.at[len(pairs)])
     to_smem.start()
@@ -146,9 +161,8 @@
     copies[4].wait()
     rows_ref[...] = table_ref[...].astype(F32)
     to_smem.wait()
-    count = list_ref[2, 0]
     copies[5].wait()
-    fill_operators(0, jnp.minimum(count, first_count), list_ref, rows_ref, weighted_ref, rad_ref, t_ref)
+    fill_operators(0, list_ref[2, 0], list_ref, rows_ref, weighted_ref, rad_ref, t_ref)
 
 
 def second_kernel(
@@ -194,13 +208,13 @@
         value = jnp.where(found[1:2] > 0, found[0:1], near_slots)
         near_map = jnp.where(out_row == j, value, near_map)
     near_map_ref[...] = near_map
-    fill_operators(first_count, list_ref[2, 0], list_ref, rows_ref, weighted_ref, rad_ref, t_ref)
+    fill_operators(first_count, list_ref[2, 1], list_ref, rows_ref, weighted_ref, rad_ref, t_ref)
     for copy in copies:
         copy.wait()
 
 
 def apply_kernel(
-    places, first_row, boxes, halo, with_total, with_other, dtype, cls_ref, near_map_ref, list_ref, t_ref, near_ref, *rest
+    places, first_row, boxes, halo, with_total, with_other, dtype, cls_ref, near_map_ref, list_ref, t_ref, low_ref, near_ref, *rest
 ):
     source_refs, rest = rest[: sum(parts for _, _, parts in places)], rest[sum(parts for _, _, parts in places) :]
     if with_total:
@@ -210,6 +224,7 @@
     (out_ref,) = rest
     me = lax.axis_index("dir")
     region_boxes = boxes * lax.axis_size("dir")
+    empty = t_ref.shape[0] - 1
     groups = []
     at = 0
     for rim, mask, parts in places:
@@ -229,7 +244,10 @@
             blocks = []
             for b in range(boxes):
                 n = list_ref[1, cls_ref[row, base + b]]
-                blocks.append(t_ref[n] + near_ref[row, near_map_ref[row, base + b]])
+                here = t_ref[jnp.minimum(n, empty)]
+                there = low_ref[jnp.maximum(n - empty - 1, 0)]
+                block = jnp.where(n > empty, there, here)
+                blocks.append(block + near_ref[row, near_map_ref[row, base + b]])
             values = [ref[...].reshape(-1, ref.shape[-1]) for ref in refs]
             rhs = values[0] if len(values) == 1 else jnp.concatenate(values, 0)
             added = jnp.dot(jnp.concatenate(blocks, 1), rhs, preferred_element_type=F32)
@@ -261,7 +279,8 @@
     halo = region_boxes // 2
     near_halo = region_boxes // 4
     classes, directions = transfer_table.shape
-    first_count = pad_to(classes // 4, UNROLL)
+    shared = classes * 5 // 8
+    capacity = (shared + 1) // 2
     top = dir_count // 2
     inner = range(2, top, 2)
     split = boxes // 2
@@ -288,8 +307,8 @@
 
     width = pad_to(region_boxes + 2 * halo, LANES)
     map_shape = (pad_to(targets, ROWS), width)
-    table_shape = (classes + 1, unknowns, unknowns)
-    low_shape = (first_count, unknowns, unknowns)
+    table_shape = (capacity + classes - shared + 1, unknowns, unknowns)
+    low_shape = (capacity, unknowns, unknowns)
     list_shape = (ROWS, pad_to(classes + 1, LANES))
     vmem, smem, hbm = whole(pltpu.VMEM), whole(pltpu.SMEM), whole(pltpu.HBM)
     operator_cost = pl.CostEstimate(
@@ -305,7 +324,7 @@
     near_other = partner(near_blocks, 1)
     near_src_other = partner(near_src, 1)
     low, weighted, rad_here, rows, cls, listed = pl.pallas_call(
-        functools.partial(first_kernel, first_count, boxes, halo, region_boxes),
+        functools.partial(first_kernel, shared, boxes, halo, region_boxes),
         in_specs=[hbm] * 6,
         out_specs=[vmem] * 6,
         out_shape=(
@@ -333,6 +352,7 @@
     low, inner_fields, field[top], rim[0] = tied
     for m, value in zip(inner, inner_fields):
         field[m] = value
+    low_other = partner(low, 1)
     for m in inner:
         field[top + m] = partner(field[top], m)
     rim[top] = partner(rim[0], top)
@@ -369,7 +389,7 @@
             total = apply(places[:GROUP], first_row, total, None, F32, full)
             return apply(places[GROUP:], first_row, total, other, dtype, shape)
         parts = [part for _, _, group in places for part in group]
-        args = [cls, near_map, listed, pinned(table), pinned(near_here)] + [pinned(part) for part in parts]
+        args = [cls, near_map, listed, pinned(table), pinned(low_other), pinned(near_here)] + [pinned(part) for part in parts]
         args += [pinned(extra) for extra in (total, other) if extra is not None]
         specs = [smem] * 3 + [vmem] * (len(args) - 3)
         layout = [(outside, mask, len(group)) for outside, mask, group in places]

time: 50.7 us -> 54.8 us (1.081); the launches traced: 51.2 us -> 54.6 us
  Pallas kernels: 34 us -> 37.7 us
  starting transfers between devices: 16.8 us -> 13.7 us
  waiting for transfers between devices: 0.16 us -> 3.02 us
    pallas_call x4, Pallas kernels: 11 us -> 15.2 us  [apply(): pl.pallas_call(kernel, in_specs=specs, out_specs=vmem, out_shape=pltpu.VM...]
    ppermute x11 -> x12, starting transfers between devices: 14.2 us -> 11.1 us  [partner(): return lax.ppermute(array, 'dir', [(i, i ^ mask) for i in range(dir_count)])]
    ppermute x11 -> x12, waiting for transfers between devices: 0.03 us -> 2.93 us  [partner(): return lax.ppermute(array, 'dir', [(i, i ^ mask) for i in range(dir_count)])]
    pallas_call x1, Pallas kernels: 11.5 us -> 10.8 us  [shards(): pl.pallas_call(functools.partial(second_kernel, halo - near_halo), in_spe...]
  transfers between devices with their start and end apart: 13 -> 14, of which waited for: 1 -> 2; matrix products, arithmetic and copies ran while one was open for 0% -> 0% of each run, Pallas kernels for 61% -> 63%
where the time goes in v5:
time: 54.8 us; the launch traced here: 54.6 us
  Pallas kernels  37.7 us (69%)
  starting transfers between devices  13.7 us (25%)
  waiting for transfers between devices  3.02 us (6%)
    pallas_call x4, Pallas kernels, apply(): pl.pallas_call(kernel, in_specs=specs, out_specs=vmem, out_shape=pltpu.VM...  15.2 us
    pallas_call x1, Pallas kernels, shards(): pl.pallas_call(functools.partial(first_kernel, shared, boxes, halo, regio...  11.6 us
    ppermute x12, starting transfers between devices, partner(): return lax.ppermute(array, 'dir', [(i, i ^ mask) for i in range(dir_count)])  11.1 us
    pallas_call x1, Pallas kernels, shards(): pl.pallas_call(functools.partial(second_kernel, halo - near_halo), in_spe...  10.8 us
    ppermute x12, waiting for transfers between devices, partner(): return lax.ppermute(array, 'dir', [(i, i ^ mask) for i in range(dir_count)])  2.93 us
    ppermute x2, starting transfers between devices, beyond(): return lax.ppermute(array, ('dir', 'region'), along)  2.56 us
  transfers between devices with their start and end apart: 14, of which 2 were waited for; matrix products, arithmetic and copies ran while one was open for 0% of the time, Pallas kernels for 63%

profile of v5, /device:TPU:0, one launch (start us, length us, event | category | flops | bytes accessed | tf_op | source)
XLA Modules:
  0.0 54.6 jit_solution(1374264703829976763)
XLA Ops:
  0.0 0.5 collective-permute-start.1
  0.5 2.5 %collective-permute-start.2 = (bf16[6,128,256]{2,1,0:T(8,128)(2,1)}, bf16[6,128,256]{2,1,0:T(8,128)(2,1)S(1)}, u32[]{:S(2)}, u32[]{:S(2)}) collective-permute-start(bf16[6,128,256]{2,1,0:T(8,128)(2,1)} %bitcast.2), channel_id=1, source_target_pairs={{0,8},{4,12},{8,0},{12,4},{16,24},{20,28},{24,16},{28,20},{1,9},{5... | collective-permute-start | bytes 1179656 | tf_op jit(solution)/shard_map/ppermute | solution.py:290
  3.0 1.5 %collective-permute-start.3 = (bf16[6,128,256]{2,1,0:T(8,128)(2,1)}, bf16[6,128,256]{2,1,0:T(8,128)(2,1)S(1)}, u32[]{:S(2)}, u32[]{:S(2)}) collective-permute-start(bf16[6,128,256]{2,1,0:T(8,128)(2,1)} %bitcast.3), channel_id=1, source_target_pairs={{0,16},{4,20},{8,24},{12,28},{16,0},{20,4},{24,8},{28,12},{1,17},{... | collective-permute-start | bytes 1179656 | tf_op jit(solution)/shard_map/ppermute | solution.py:290
  4.5 1.3 %collective-permute-start.4 = (bf16[6,128,256]{2,1,0:T(8,128)(2,1)}, bf16[6,128,256]{2,1,0:T(8,128)(2,1)S(1)}, u32[]{:S(2)}, u32[]{:S(2)}) collective-permute-start(bf16[6,128,256]{2,1,0:T(8,128)(2,1)} %bitcast.4), channel_id=1, source_target_pairs={{1,0},{2,1},{3,2},{5,4},{6,5},{7,6},{9,8},{10,9},{11,10},{13,12},{... | collective-permute-start | bytes 1179656 | tf_op jit(solution)/shard_map/ppermute | solution.py:300
  5.8 11.6 %shard_map.91 = (bf16[99,128,128]{2,1,0:T(8,128)(2,1)S(1)}, bf16[128,1536]{1,0:T(8,128)(2,1)S(1)}, bf16[1536,128]{1,0:T(8,128)(2,1)S(1)}, f32[316,1536]{1,0:T(8,...) custom-call(s32[9]{0:T(128)} %off_hbm.1, s32[1,48,48]{2,1,0:T(8,128)} %src_hbm.1, s32[1,48,48]{2,1,0:T(8,128)} %tid_hbm.1, ...), custom_call_target="tpu_custom_call" | custom-call | flops 7952400384 | bytes 1048576 | tf_op jit(solution)/shard_map/pallas_call | solution.py:326
  17.4 0.0 collective-permute-done.2.rest_1_
  17.4 0.0 collective-permute-done.3.rest_2_
  17.4 0.1 collective-permute-done.4.rest_3_
  17.5 0.0 collective-permute-start.8
  17.5 0.5 collective-permute-start
  18.0 1.1 %collective-permute-start.5 = (bf16[6,128,256]{2,1,0:T(8,128)(2,1)S(1)}, bf16[6,128,256]{2,1,0:T(8,128)(2,1)S(1)}, u32[]{:S(2)}, u32[]{:S(2)}) collective-permute-start(bf16[6,128,256]{2,1,0:T(8,128)(2,1)S(1)} %collective-permute-done.3.rest_2_), channel_id=1, source_target_pairs={{0,8},{4,12},{8,0},{12,4},{16,24},{20,28},{24,16},{28,20},{1,9},{5... | collective-permute-start | bytes 1179656 | tf_op jit(solution)/shard_map/ppermute | solution.py:290
  19.1 1.3 %collective-permute-start.6 = (bf16[6,128,256]{2,1,0:T(8,128)(2,1)S(1)}, bf16[6,128,256]{2,1,0:T(8,128)(2,1)S(1)}, u32[]{:S(2)}, u32[]{:S(2)}) collective-permute-start(bf16[6,128,256]{2,1,0:T(8,128)(2,1)S(1)} %collective-permute-done.2.rest_1_), channel_id=1, source_target_pairs={{1,0},{2,1},{3,2},{5,4},{6,5},{7,6},{9,8},{10,9},{11,10},{13,12},{... | collective-permute-start | bytes 1179656 | tf_op jit(solution)/shard_map/ppermute | solution.py:300
  20.4 2.9 %collective-permute-done.near_src_other_ref = s32[6,1,27]{2,1,0:T(1,128)S(1)} collective-permute-done((s32[6,1,27]{2,1,0:T(1,128)S(1)}, s32[6,1,27]{2,1,0:T(1,128)S(1)}, u32[]{:S(2)}, u32[]{:S(2)}) %collective-permute-start) | collective-permute-done | bytes 680 | tf_op jit(solution)/shard_map/ppermute | solution.py:290
  23.3 3.3 %collective-permute-start.7 = (bf16[6,128,256]{2,1,0:T(8,128)(2,1)S(1)}, bf16[6,128,256]{2,1,0:T(8,128)(2,1)S(1)}, u32[]{:S(2)}, u32[]{:S(2)}) collective-permute-start(bf16[6,128,256]{2,1,0:T(8,128)(2,1)S(1)} %collective-permute-done.4.rest_3_), channel_id=1, source_target_pairs={{0,16},{4,20},{8,24},{12,28},{16,0},{20,4},{24,8},{28,12},{1,17},{... | collective-permute-start | bytes 1179656 | tf_op jit(solution)/shard_map/ppermute | solution.py:290
  26.6 0.0 collective-permute-done.1.near_other_hbm
  26.6 10.8 %shard_map.92 = (bf16[219,128,128]{2,1,0:T(8,128)(2,1)S(1)}, bf16[12,28,128,128]{3,2,1,0:T(8,128)(2,1)S(1)}, s32[16,128]{1,0:T(8,128)S(1)}) custom-call(s32[8,384]{1,0:T(8,128)S(1)} %get-tuple-element.26.list_ref, f32[316,1536]{1,0:T(8,128)S(1)} %get-tuple-element.27.rows_ref, bf16[128,1536]{1,0:T(8,128)(2,1)S(1)} %get-tuple-element.28.weighted_ref, ...), custom_call_target="tpu_custom_call" | custom-call | flops 7952400384 | bytes 1048576 | tf_op jit(solution)/shard_map/pallas_call | solution.py:362
  37.5 0.0 collective-permute-done.5.rest_4_.rest_0_
  37.5 0.0 collective-permute-done.6.rest_5_.rest_1_
  37.5 0.0 collective-permute-done.7.rest_6_.rest_2_
  37.5 1.0 %collective-permute-start.9 = (bf16[3,128,256]{2,1,0:T(8,128)(2,1)S(1)}, bf16[3,128,256]{2,1,0:T(8,128)(2,1)S(1)}, u32[]{:S(2)}, u32[]{:S(2)}) collective-permute-start(bf16[3,128,256]{2,1,0:T(8,128)(2,1)S(1)} %slice.6), channel_id=1, source_target_pairs={{0,8},{4,12},{8,0},{12,4},{16,24},{20,28},{24,16},{28,20},{1,9},{5... | collective-permute-start | bytes 589832 | tf_op jit(solution)/shard_map/ppermute | solution.py:290
  38.5 0.1 collective-permute-start.10
  38.6 0.0 collective-permute-done.8.low_ref
  38.6 5.6 %shard_map.94 = bf16[6,128,256]{2,1,0:T(8,128)(2,1)S(1)} custom-call(s32[16,128]{1,0:T(8,128)S(1)} %get-tuple-element.25.cls_ref, s32[16,128]{1,0:T(8,128)S(1)} %get-tuple-element.32.near_map_ref, s32[8,384]{1,0:T(8,128)S(1)} %get-tuple-element.26.list_ref, bf16[219,128,128]{2,1,0:T(8,128)(2,1)S(1)} %get-tuple-element.37.t_ref, ...), custom_call_target="tpu_custom_call" | custom-call | flops 1048576 | bytes 1048576 | tf_op jit(solution)/shard_map/pallas_call | solution.py:399
  44.2 0.1 collective-permute-start.13
  44.3 3.5 %shard_map.93.rest_3_ = f32[6,128,256]{2,1,0:T(8,128)S(1)} custom-call(s32[16,128]{1,0:T(8,128)S(1)} %get-tuple-element.25.cls_ref, s32[16,128]{1,0:T(8,128)S(1)} %get-tuple-element.32.near_map_ref, s32[8,384]{1,0:T(8,128)S(1)} %get-tuple-element.26.list_ref, bf16[219,128,128]{2,1,0:T(8,128)(2,1)S(1)} %get-tuple-element.37.t_ref, ...), custom_call_target="tpu_custom_call" | custom-call | flops 1048576 | bytes 1048576 | tf_op jit(solution)/shard_map/pallas_call | solution.py:399
  47.8 0.0 collective-permute-done.10.rest_1_
  47.8 0.5 collective-permute-start.11
  48.4 0.1 collective-permute-start.12
  48.5 0.0 collective-permute-done.13.rest_4_
  48.5 3.0 %shard_map.95.rest_4_ = f32[6,128,256]{2,1,0:T(8,128)S(1)} custom-call(s32[16,128]{1,0:T(8,128)S(1)} %get-tuple-element.25.cls_ref, s32[16,128]{1,0:T(8,128)S(1)} %get-tuple-element.32.near_map_ref, s32[8,384]{1,0:T(8,128)S(1)} %get-tuple-element.26.list_ref, bf16[219,128,128]{2,1,0:T(8,128)(2,1)S(1)} %get-tuple-element.37.t_ref, ...), custom_call_target="tpu_custom_call" | custom-call | flops 1048576 | bytes 1048576 | tf_op jit(solution)/shard_map/pallas_call | solution.py:399
  51.5 0.0 collective-permute-done.12.rest_3_
  51.5 3.1 %shard_map.96 = bf16[1,6,128,256]{3,2,1,0:T(8,128)(2,1)} custom-call(s32[16,128]{1,0:T(8,128)S(1)} %get-tuple-element.25.cls_ref, s32[16,128]{1,0:T(8,128)S(1)} %get-tuple-element.32.near_map_ref, s32[8,384]{1,0:T(8,128)S(1)} %get-tuple-element.26.list_ref, bf16[219,128,128]{2,1,0:T(8,128)(2,1)S(1)} %get-tuple-element.37.t_ref, ...), custom_call_target="tpu_custom_call" | custom-call | flops 1048576 | bytes 1048576 | tf_op jit(solution)/shard_map/pallas_call | solution.py:399
  (8 shorter events, 0.0 us)
Async XLA Ops:
  0.0 26.6 %collective-permute-start.1 = (bf16[1,6,27,128,128]{4,3,2,1,0:T(8,128)(2,1)}, bf16[1,6,27,128,128]{4,3,2,1,0:T(8,128)(2,1)S(1)}, u32[]{:S(2)}, u32[]{:S(2)}) collective-permute-start(bf16[1,6,27,128,128]{4,3,2,1,0:T(8,128)(2,1)} %near_hbm.1), channel_id=1, source_target_pairs={{0,4},{4,0},{8,12},{12,8},{16,20},{20,16},{24,28},{28,24},{1,5},{5... | collective-permute-start | bytes 15925256 | tf_op jit(solution)/shard_map/ppermute | solution.py:290
  0.5 17.1 %copy-start.1 = (s32[1,6,27]{2,0,1:T(1,128)S(1)}, s32[1,6,27]{2,0,1:T(1,128)}, u32[]{:S(2)}) copy-start(s32[1,6,27]{2,0,1:T(1,128)} %param.17) | copy-start | bytes 1948
  0.5 17.0 %collective-permute-start.2 = (bf16[6,128,256]{2,1,0:T(8,128)(2,1)}, bf16[6,128,256]{2,1,0:T(8,128)(2,1)S(1)}, u32[]{:S(2)}, u32[]{:S(2)}) collective-permute-start(bf16[6,128,256]{2,1,0:T(8,128)(2,1)} %bitcast.2), channel_id=1, source_target_pairs={{0,8},{4,12},{8,0},{12,4},{16,24},{20,28},{24,16},{28,20},{1,9},{5... | collective-permute-start | bytes 1179656 | tf_op jit(solution)/shard_map/ppermute | solution.py:290
  3.0 14.4 %collective-permute-start.3 = (bf16[6,128,256]{2,1,0:T(8,128)(2,1)}, bf16[6,128,256]{2,1,0:T(8,128)(2,1)S(1)}, u32[]{:S(2)}, u32[]{:S(2)}) collective-permute-start(bf16[6,128,256]{2,1,0:T(8,128)(2,1)} %bitcast.3), channel_id=1, source_target_pairs={{0,16},{4,20},{8,24},{12,28},{16,0},{20,4},{24,8},{28,12},{1,17},{... | collective-permute-start | bytes 1179656 | tf_op jit(solution)/shard_map/ppermute | solution.py:290
  4.5 13.0 %collective-permute-start.4 = (bf16[6,128,256]{2,1,0:T(8,128)(2,1)}, bf16[6,128,256]{2,1,0:T(8,128)(2,1)S(1)}, u32[]{:S(2)}, u32[]{:S(2)}) collective-permute-start(bf16[6,128,256]{2,1,0:T(8,128)(2,1)} %bitcast.4), channel_id=1, source_target_pairs={{1,0},{2,1},{3,2},{5,4},{6,5},{7,6},{9,8},{10,9},{11,10},{13,12},{... | collective-permute-start | bytes 1179656 | tf_op jit(solution)/shard_map/ppermute | solution.py:300
  17.5 21.1 %collective-permute-start.8 = (bf16[99,128,128]{2,1,0:T(8,128)(2,1)S(1)}, bf16[99,128,128]{2,1,0:T(8,128)(2,1)S(1)}, u32[]{:S(2)}, u32[]{:S(2)}) collective-permute-start(bf16[99,128,128]{2,1,0:T(8,128)(2,1)S(1)} %get-tuple-element.31.low_ref), channel_id=1, source_target_pairs={{0,4},{4,0},{8,12},{12,8},{16,20},{20,16},{24,28},{28,24},{1,5},{5... | collective-permute-start | bytes 9732104 | tf_op jit(solution)/shard_map/ppermute | solution.py:290
  17.5 5.8 %collective-permute-start = (s32[6,1,27]{2,1,0:T(1,128)S(1)}, s32[6,1,27]{2,1,0:T(1,128)S(1)}, u32[]{:S(2)}, u32[]{:S(2)}) collective-permute-start(s32[6,1,27]{2,1,0:T(1,128)S(1)} %bitcast.7), channel_id=1, source_target_pairs={{0,4},{4,0},{8,12},{12,8},{16,20},{20,16},{24,28},{28,24},{1,5},{5... | collective-permute-start | bytes 1952 | tf_op jit(solution)/shard_map/ppermute | solution.py:290
  18.0 19.4 %collective-permute-start.5 = (bf16[6,128,256]{2,1,0:T(8,128)(2,1)S(1)}, bf16[6,128,256]{2,1,0:T(8,128)(2,1)S(1)}, u32[]{:S(2)}, u32[]{:S(2)}) collective-permute-start(bf16[6,128,256]{2,1,0:T(8,128)(2,1)S(1)} %collective-permute-done.3.rest_2_), channel_id=1, source_target_pairs={{0,8},{4,12},{8,0},{12,4},{16,24},{20,28},{24,16},{28,20},{1,9},{5... | collective-permute-start | bytes 1179656 | tf_op jit(solution)/shard_map/ppermute | solution.py:290
  19.1 18.3 %collective-permute-start.6 = (bf16[6,128,256]{2,1,0:T(8,128)(2,1)S(1)}, bf16[6,128,256]{2,1,0:T(8,128)(2,1)S(1)}, u32[]{:S(2)}, u32[]{:S(2)}) collective-permute-start(bf16[6,128,256]{2,1,0:T(8,128)(2,1)S(1)} %collective-permute-done.2.rest_1_), channel_id=1, source_target_pairs={{1,0},{2,1},{3,2},{5,4},{6,5},{7,6},{9,8},{10,9},{11,10},{13,12},{... | collective-permute-start | bytes 1179656 | tf_op jit(solution)/shard_map/ppermute | solution.py:300
  23.3 14.2 %collective-permute-start.7 = (bf16[6,128,256]{2,1,0:T(8,128)(2,1)S(1)}, bf16[6,128,256]{2,1,0:T(8,128)(2,1)S(1)}, u32[]{:S(2)}, u32[]{:S(2)}) collective-permute-start(bf16[6,128,256]{2,1,0:T(8,128)(2,1)S(1)} %collective-permute-done.4.rest_3_), channel_id=1, source_target_pairs={{0,16},{4,20},{8,24},{12,28},{16,0},{20,4},{24,8},{28,12},{1,17},{... | collective-permute-start | bytes 1179656 | tf_op jit(solution)/shard_map/ppermute | solution.py:290
  26.6 12.0 %copy-start = (bf16[1,6,128,256]{3,2,1,0:T(8,128)(2,1)S(1)}, bf16[1,6,128,256]{3,2,1,0:T(8,128)(2,1)}, u32[]{:S(2)}) copy-start(bf16[1,6,128,256]{3,2,1,0:T(8,128)(2,1)} %param.9) | copy-start | bytes 1179652
  37.5 10.3 %collective-permute-start.9 = (bf16[3,128,256]{2,1,0:T(8,128)(2,1)S(1)}, bf16[3,128,256]{2,1,0:T(8,128)(2,1)S(1)}, u32[]{:S(2)}, u32[]{:S(2)}) collective-permute-start(bf16[3,128,256]{2,1,0:T(8,128)(2,1)S(1)} %slice.6), channel_id=1, source_target_pairs={{0,8},{4,12},{8,0},{12,4},{16,24},{20,28},{24,16},{28,20},{1,9},{5... | collective-permute-start | bytes 589832 | tf_op jit(solution)/shard_map/ppermute | solution.py:290
  38.5 9.3 %collective-permute-start.10 = (bf16[3,128,256]{2,1,0:T(8,128)(2,1)S(1)}, bf16[3,128,256]{2,1,0:T(8,128)(2,1)S(1)}, u32[]{:S(2)}, u32[]{:S(2)}) collective-permute-start(bf16[3,128,256]{2,1,0:T(8,128)(2,1)S(1)} %slice.7), channel_id=1, source_target_pairs={{0,16},{4,20},{8,24},{12,28},{16,0},{20,4},{24,8},{28,12},{1,17},{... | collective-permute-start | bytes 589832 | tf_op jit(solution)/shard_map/ppermute | solution.py:290
  44.2 4.3 %collective-permute-start.13 = (bf16[6,128,256]{2,1,0:T(8,128)(2,1)S(1)}, bf16[6,128,256]{2,1,0:T(8,128)(2,1)S(1)}, u32[]{:S(2)}, u32[]{:S(2)}) collective-permute-start(bf16[6,128,256]{2,1,0:T(8,128)(2,1)S(1)} %shard_map.94), channel_id=1, source_target_pairs={{0,4},{4,0},{8,12},{12,8},{16,20},{20,16},{24,28},{28,24},{1,5},{5... | collective-permute-start | bytes 1179656 | tf_op jit(solution)/shard_map/ppermute | solution.py:290
  47.8 3.6 %collective-permute-start.11 = (bf16[3,128,256]{2,1,0:T(8,128)(2,1)S(1)}, bf16[3,128,256]{2,1,0:T(8,128)(2,1)S(1)}, u32[]{:S(2)}, u32[]{:S(2)}) collective-permute-start(bf16[3,128,256]{2,1,0:T(8,128)(2,1)S(1)} %collective-permute-done.9.rest_0_), channel_id=1, source_target_pairs={{0,4},{4,0},{8,12},{12,8},{16,20},{20,16},{24,28},{28,24},{1,5},{5... | collective-permute-start | bytes 589832 | tf_op jit(solution)/shard_map/ppermute | solution.py:290
  48.4 3.1 %collective-permute-start.12 = (bf16[3,128,256]{2,1,0:T(8,128)(2,1)S(1)}, bf16[3,128,256]{2,1,0:T(8,128)(2,1)S(1)}, u32[]{:S(2)}, u32[]{:S(2)}) collective-permute-start(bf16[3,128,256]{2,1,0:T(8,128)(2,1)S(1)} %collective-permute-done.10.rest_1_), channel_id=1, source_target_pairs={{0,4},{4,0},{8,12},{12,8},{16,20},{20,16},{24,28},{28,24},{1,5},{5... | collective-permute-start | bytes 589832 | tf_op jit(solution)/shard_map/ppermute | solution.py:290

commit v6 on v4

--- a/solution.py
+++ b/solution.py
@@ -264,7 +264,6 @@
     first_count = pad_to(classes // 4, UNROLL)
     top = dir_count // 2
     inner = range(2, top, 2)
-    split = boxes // 2
     targets = 2 * boxes
 
     def partner(array, mask):
@@ -338,6 +337,9 @@
     rim[top] = partner(rim[0], top)
     for m in inner:
         rim[m] = beyond(field[m])
+    rim[0], near_other = lax.optimization_barrier((rim[0], near_other))
+    for m in inner:
+        rim[top + m] = partner(rim[0], top + m)
 
     table, near_here, near_map = pl.pallas_call(
         functools.partial(second_kernel, halo - near_halo),
@@ -385,14 +387,6 @@
             cost_estimate=pl.CostEstimate(flops=MIB, bytes_accessed=MIB, transcendentals=0),
         )(*args)
 
-    tied = lax.optimization_barrier(
-        (table, [field[top + m] for m in inner], [rim[m] for m in inner], rim[top])
-    )
-    table, far_fields, inner_rims, rim[top] = tied
-    for m, value, other in zip(inner, far_fields, inner_rims):
-        field[top + m], rim[m] = value, other
-    last = {m: [partner(rim[top][:split], m), partner(rim[m][split:], top)] for m in inner}
-
     full = (boxes, unknowns, incidences)
     early = [(False, m, [field[m]]) for m in (0, *inner, top)] + [(True, 0, [rim[0]])]
     middle = [(False, top + m, [field[top + m]]) for m in inner]
@@ -402,10 +396,11 @@
     from_other = partner(for_other, 1)
     total = apply(early, 0, None, None, F32, full)
 
-    total, last = lax.optimization_barrier((total, last))
-    turned = {m: [partner(part, 1) for part in last[m]] for m in inner}
+    total, last = lax.optimization_barrier((total, [rim[top + m] for m in inner]))
+    turned = [partner(part, 1) for part in last]
     total = apply(middle, 0, total, from_other, F32, full)
-    late = [(True, top + m, last[m]) for m in inner] + [(True, top + m + 1, turned[m]) for m in inner]
+    late = [(True, top + m, [part]) for m, part in zip(inner, last)]
+    late += [(True, top + m + 1, [part]) for m, part in zip(inner, turned)]
     return apply(late, 0, total, None, BF16, currents.shape)
 
 

time: 50.7 us -> 53.8 us (1.061); the launches traced: 51.2 us -> 53.6 us
  waiting for transfers between devices: 0.16 us -> 5.23 us
  starting transfers between devices: 16.8 us -> 14.2 us
    ppermute x11 -> x9, waiting for transfers between devices: 0.03 us -> 5.09 us  [partner(): return lax.ppermute(array, 'dir', [(i, i ^ mask) for i in range(dir_count)])]
    ppermute x11 -> x9, starting transfers between devices: 14.2 us -> 11.6 us  [partner(): return lax.ppermute(array, 'dir', [(i, i ^ mask) for i in range(dir_count)])]
  transfers between devices with their start and end apart: 13 -> 11, of which waited for: 1 -> 2; matrix products, arithmetic and copies ran while one was open for 0% -> 0% of each run, Pallas kernels for 61% -> 59%
where the time goes in v6:
time: 53.8 us; the launch traced here: 53.6 us
  Pallas kernels  34 us (63%)
  starting transfers between devices  14.2 us (26%)
  waiting for transfers between devices  5.23 us (10%)
    ppermute x9, starting transfers between devices, partner(): return lax.ppermute(array, 'dir', [(i, i ^ mask) for i in range(dir_count)])  11.6 us
    pallas_call x1, Pallas kernels, shards(): pl.pallas_call(functools.partial(first_kernel, first_count, boxes, halo,...  11.5 us
    pallas_call x1, Pallas kernels, shards(): pl.pallas_call(functools.partial(second_kernel, halo - near_halo), in_spe...  11.5 us
    pallas_call x4, Pallas kernels, apply(): pl.pallas_call(kernel, in_specs=specs, out_specs=vmem, out_shape=pltpu.VM...  11 us
    ppermute x9, waiting for transfers between devices, partner(): return lax.ppermute(array, 'dir', [(i, i ^ mask) for i in range(dir_count)])  5.09 us
    ppermute x2, starting transfers between devices, beyond(): return lax.ppermute(array, ('dir', 'region'), along)  2.56 us
  transfers between devices with their start and end apart: 11, of which 2 were waited for; matrix products, arithmetic and copies ran while one was open for 0% of the time, Pallas kernels for 59%

profile of v6, /device:TPU:0, one launch (start us, length us, event | category | flops | bytes accessed | tf_op | source)
XLA Modules:
  0.0 53.6 jit_solution(11530762177026602711)
XLA Ops:
  0.0 0.5 collective-permute-start.4
  0.5 2.5 %collective-permute-start.1 = (bf16[6,128,256]{2,1,0:T(8,128)(2,1)}, bf16[6,128,256]{2,1,0:T(8,128)(2,1)S(1)}, u32[]{:S(2)}, u32[]{:S(2)}) collective-permute-start(bf16[6,128,256]{2,1,0:T(8,128)(2,1)} %bitcast.2), channel_id=1, source_target_pairs={{0,8},{4,12},{8,0},{12,4},{16,24},{20,28},{24,16},{28,20},{1,9},{5... | collective-permute-start | bytes 1179656 | tf_op jit(solution)/shard_map/ppermute | solution.py:270
  2.9 1.5 %collective-permute-start.2 = (bf16[6,128,256]{2,1,0:T(8,128)(2,1)}, bf16[6,128,256]{2,1,0:T(8,128)(2,1)S(1)}, u32[]{:S(2)}, u32[]{:S(2)}) collective-permute-start(bf16[6,128,256]{2,1,0:T(8,128)(2,1)} %bitcast.3), channel_id=1, source_target_pairs={{0,16},{4,20},{8,24},{12,28},{16,0},{20,4},{24,8},{28,12},{1,17},{... | collective-permute-start | bytes 1179656 | tf_op jit(solution)/shard_map/ppermute | solution.py:270
  4.5 1.3 %collective-permute-start.3 = (bf16[6,128,256]{2,1,0:T(8,128)(2,1)}, bf16[6,128,256]{2,1,0:T(8,128)(2,1)S(1)}, u32[]{:S(2)}, u32[]{:S(2)}) collective-permute-start(bf16[6,128,256]{2,1,0:T(8,128)(2,1)} %bitcast.4), channel_id=1, source_target_pairs={{1,0},{2,1},{3,2},{5,4},{6,5},{7,6},{9,8},{10,9},{11,10},{13,12},{... | collective-permute-start | bytes 1179656 | tf_op jit(solution)/shard_map/ppermute | solution.py:280
  5.8 0.0 copy-start.1
  5.8 0.1 collective-permute-start
  5.8 11.5 %shard_map.91 = (bf16[80,128,128]{2,1,0:T(8,128)(2,1)S(1)}, bf16[128,1536]{1,0:T(8,128)(2,1)S(1)}, bf16[1536,128]{1,0:T(8,128)(2,1)S(1)}, f32[316,1536]{1,0:T(8,...) custom-call(s32[9]{0:T(128)} %off_hbm.1, s32[1,48,48]{2,1,0:T(8,128)} %src_hbm.1, s32[1,48,48]{2,1,0:T(8,128)} %tid_hbm.1, ...), custom_call_target="tpu_custom_call" | custom-call | flops 7952400384 | bytes 1048576 | tf_op jit(solution)/shard_map/pallas_call | solution.py:306
  17.4 0.0 collective-permute-done.1.rest_1_
  17.4 0.0 collective-permute-done.2.rest_2_
  17.4 0.1 collective-permute-done.3.rest_3_
  17.5 0.5 collective-permute-start.7
  18.1 1.3 %collective-permute-start.8 = (bf16[6,128,256]{2,1,0:T(8,128)(2,1)S(1)}, bf16[6,128,256]{2,1,0:T(8,128)(2,1)S(1)}, u32[]{:S(2)}, u32[]{:S(2)}) collective-permute-start(bf16[6,128,256]{2,1,0:T(8,128)(2,1)S(1)} %collective-permute-done.1.rest_1_), channel_id=1, source_target_pairs={{1,0},{2,1},{3,2},{5,4},{6,5},{7,6},{9,8},{10,9},{11,10},{13,12},{... | collective-permute-start | bytes 1179656 | tf_op jit(solution)/shard_map/ppermute | solution.py:280
  19.3 4.9 %collective-permute-start.9 = (bf16[6,128,256]{2,1,0:T(8,128)(2,1)S(1)}, bf16[6,128,256]{2,1,0:T(8,128)(2,1)S(1)}, u32[]{:S(2)}, u32[]{:S(2)}) collective-permute-start(bf16[6,128,256]{2,1,0:T(8,128)(2,1)S(1)} %collective-permute-done.3.rest_3_), channel_id=1, source_target_pairs={{0,16},{4,20},{8,24},{12,28},{16,0},{20,4},{24,8},{28,12},{1,17},{... | collective-permute-start | bytes 1179656 | tf_op jit(solution)/shard_map/ppermute | solution.py:270
  24.3 0.0 collective-permute-done.4.near_other_hbm
  24.3 1.0 %collective-permute-start.5 = (bf16[6,128,256]{2,1,0:T(8,128)(2,1)S(1)}, bf16[6,128,256]{2,1,0:T(8,128)(2,1)S(1)}, u32[]{:S(2)}, u32[]{:S(2)}) collective-permute-start(bf16[6,128,256]{2,1,0:T(8,128)(2,1)S(1)} %collective-permute-done.3.rest_3_), channel_id=1, source_target_pairs={{0,24},{4,28},{8,16},{12,20},{16,8},{20,12},{24,0},{28,4},{1,25},{... | collective-permute-start | bytes 1179656 | tf_op jit(solution)/shard_map/ppermute | solution.py:270
  25.3 0.0 collective-permute-done.near_src_other_ref
  25.3 0.0 copy-done.1
  25.3 0.0 copy-start
  25.3 11.5 %shard_map.92 = (bf16[317,128,128]{2,1,0:T(8,128)(2,1)S(1)}, bf16[12,28,128,128]{3,2,1,0:T(8,128)(2,1)S(1)}, s32[16,128]{1,0:T(8,128)S(1)}) custom-call(s32[8,384]{1,0:T(8,128)S(1)} %get-tuple-element.23.list_ref, f32[316,1536]{1,0:T(8,128)S(1)} %get-tuple-element.24.rows_ref, bf16[128,1536]{1,0:T(8,128)(2,1)S(1)} %get-tuple-element.25.weighted_ref, ...), custom_call_target="tpu_custom_call" | custom-call | flops 7952400384 | bytes 1048576 | tf_op jit(solution)/shard_map/pallas_call | solution.py:344
  36.8 0.0 collective-permute-done.7.rest_4_.rest_0_
  36.8 0.0 collective-permute-done.8.rest_5_.rest_1_
  36.8 5.1 %collective-permute-done.9.rest_6_.rest_2_ = bf16[6,128,256]{2,1,0:T(8,128)(2,1)S(1)} collective-permute-done((bf16[6,128,256]{2,1,0:T(8,128)(2,1)S(1)}, bf16[6,128,256]{2,1,0:T(8,128)(2,1)S(1)}, u32[]{:S(2)}, u32[]{:S(2)}) %collective-permute-start.9) | collective-permute-done | bytes 393248 | tf_op jit(solution)/shard_map/ppermute | solution.py:270
  41.9 0.0 copy-done
  41.9 3.6 %shard_map.94 = bf16[6,128,256]{2,1,0:T(8,128)(2,1)S(1)} custom-call(s32[16,128]{1,0:T(8,128)S(1)} %get-tuple-element.22.cls_ref, s32[16,128]{1,0:T(8,128)S(1)} %get-tuple-element.31.near_map_ref, s32[8,384]{1,0:T(8,128)S(1)} %get-tuple-element.23.list_ref, bf16[317,128,128]{2,1,0:T(8,128)(2,1)S(1)} %get-tuple-element.32.t_ref, ...), custom_call_target="tpu_custom_call" | custom-call | flops 1048576 | bytes 1048576 | tf_op jit(solution)/shard_map/pallas_call | solution.py:381
  45.5 0.1 collective-permute-start.10
  45.6 2.6 %shard_map.93.rest_3_ = f32[6,128,256]{2,1,0:T(8,128)S(1)} custom-call(s32[16,128]{1,0:T(8,128)S(1)} %get-tuple-element.22.cls_ref, s32[16,128]{1,0:T(8,128)S(1)} %get-tuple-element.31.near_map_ref, s32[8,384]{1,0:T(8,128)S(1)} %get-tuple-element.23.list_ref, bf16[317,128,128]{2,1,0:T(8,128)(2,1)S(1)} %get-tuple-element.32.t_ref, ...), custom_call_target="tpu_custom_call" | custom-call | flops 1048576 | bytes 1048576 | tf_op jit(solution)/shard_map/pallas_call | solution.py:381
  48.1 0.0 collective-permute-done.5.rest_0_
  48.1 0.6 %collective-permute-start.6 = (bf16[6,128,256]{2,1,0:T(8,128)(2,1)S(1)}, bf16[6,128,256]{2,1,0:T(8,128)(2,1)S(1)}, u32[]{:S(2)}, u32[]{:S(2)}) collective-permute-start(bf16[6,128,256]{2,1,0:T(8,128)(2,1)S(1)} %collective-permute-done.5.rest_0_), channel_id=1, source_target_pairs={{0,4},{4,0},{8,12},{12,8},{16,20},{20,16},{24,28},{28,24},{1,5},{5... | collective-permute-start | bytes 1179656 | tf_op jit(solution)/shard_map/ppermute | solution.py:270
  48.7 0.0 collective-permute-done.10.rest_4_
  48.7 2.2 %shard_map.95.rest_2_ = f32[6,128,256]{2,1,0:T(8,128)S(1)} custom-call(s32[16,128]{1,0:T(8,128)S(1)} %get-tuple-element.22.cls_ref, s32[16,128]{1,0:T(8,128)S(1)} %get-tuple-element.31.near_map_ref, s32[8,384]{1,0:T(8,128)S(1)} %get-tuple-element.23.list_ref, bf16[317,128,128]{2,1,0:T(8,128)(2,1)S(1)} %get-tuple-element.32.t_ref, ...), custom_call_target="tpu_custom_call" | custom-call | flops 1048576 | bytes 1048576 | tf_op jit(solution)/shard_map/pallas_call | solution.py:381
  50.9 0.0 collective-permute-done.6.rest_1_
  50.9 2.6 %shard_map.96 = bf16[1,6,128,256]{3,2,1,0:T(8,128)(2,1)} custom-call(s32[16,128]{1,0:T(8,128)S(1)} %get-tuple-element.22.cls_ref, s32[16,128]{1,0:T(8,128)S(1)} %get-tuple-element.31.near_map_ref, s32[8,384]{1,0:T(8,128)S(1)} %get-tuple-element.23.list_ref, bf16[317,128,128]{2,1,0:T(8,128)(2,1)S(1)} %get-tuple-element.32.t_ref, ...), custom_call_target="tpu_custom_call" | custom-call | flops 1048576 | bytes 1048576 | tf_op jit(solution)/shard_map/pallas_call | solution.py:381
Async XLA Ops:
  0.0 24.3 %collective-permute-start.4 = (bf16[1,6,27,128,128]{4,3,2,1,0:T(8,128)(2,1)}, bf16[1,6,27,128,128]{4,3,2,1,0:T(8,128)(2,1)S(1)}, u32[]{:S(2)}, u32[]{:S(2)}) collective-permute-start(bf16[1,6,27,128,128]{4,3,2,1,0:T(8,128)(2,1)} %near_hbm.1), channel_id=1, source_target_pairs={{0,4},{4,0},{8,12},{12,8},{16,20},{20,16},{24,28},{28,24},{1,5},{5... | collective-permute-start | bytes 15925256 | tf_op jit(solution)/shard_map/ppermute | solution.py:270
  0.5 16.9 %collective-permute-start.1 = (bf16[6,128,256]{2,1,0:T(8,128)(2,1)}, bf16[6,128,256]{2,1,0:T(8,128)(2,1)S(1)}, u32[]{:S(2)}, u32[]{:S(2)}) collective-permute-start(bf16[6,128,256]{2,1,0:T(8,128)(2,1)} %bitcast.2), channel_id=1, source_target_pairs={{0,8},{4,12},{8,0},{12,4},{16,24},{20,28},{24,16},{28,20},{1,9},{5... | collective-permute-start | bytes 1179656 | tf_op jit(solution)/shard_map/ppermute | solution.py:270
  2.9 14.4 %collective-permute-start.2 = (bf16[6,128,256]{2,1,0:T(8,128)(2,1)}, bf16[6,128,256]{2,1,0:T(8,128)(2,1)S(1)}, u32[]{:S(2)}, u32[]{:S(2)}) collective-permute-start(bf16[6,128,256]{2,1,0:T(8,128)(2,1)} %bitcast.3), channel_id=1, source_target_pairs={{0,16},{4,20},{8,24},{12,28},{16,0},{20,4},{24,8},{28,12},{1,17},{... | collective-permute-start | bytes 1179656 | tf_op jit(solution)/shard_map/ppermute | solution.py:270
  4.5 13.1 %collective-permute-start.3 = (bf16[6,128,256]{2,1,0:T(8,128)(2,1)}, bf16[6,128,256]{2,1,0:T(8,128)(2,1)S(1)}, u32[]{:S(2)}, u32[]{:S(2)}) collective-permute-start(bf16[6,128,256]{2,1,0:T(8,128)(2,1)} %bitcast.4), channel_id=1, source_target_pairs={{1,0},{2,1},{3,2},{5,4},{6,5},{7,6},{9,8},{10,9},{11,10},{13,12},{... | collective-permute-start | bytes 1179656 | tf_op jit(solution)/shard_map/ppermute | solution.py:280
  5.8 19.5 %copy-start.1 = (s32[1,6,27]{2,0,1:T(1,128)S(1)}, s32[1,6,27]{2,0,1:T(1,128)}, u32[]{:S(2)}) copy-start(s32[1,6,27]{2,0,1:T(1,128)} %param.17) | copy-start | bytes 1948
  5.8 19.5 %collective-permute-start = (s32[6,1,27]{2,1,0:T(1,128)}, s32[6,1,27]{2,1,0:T(1,128)S(1)}, u32[]{:S(2)}, u32[]{:S(2)}) collective-permute-start(s32[6,1,27]{2,1,0:T(1,128)} %bitcast.7), channel_id=1, source_target_pairs={{0,4},{4,0},{8,12},{12,8},{16,20},{20,16},{24,28},{28,24},{1,5},{5... | collective-permute-start | bytes 1952 | tf_op jit(solution)/shard_map/ppermute | solution.py:270
  17.5 19.3 %collective-permute-start.7 = (bf16[6,128,256]{2,1,0:T(8,128)(2,1)S(1)}, bf16[6,128,256]{2,1,0:T(8,128)(2,1)S(1)}, u32[]{:S(2)}, u32[]{:S(2)}) collective-permute-start(bf16[6,128,256]{2,1,0:T(8,128)(2,1)S(1)} %collective-permute-done.2.rest_2_), channel_id=1, source_target_pairs={{0,8},{4,12},{8,0},{12,4},{16,24},{20,28},{24,16},{28,20},{1,9},{5... | collective-permute-start | bytes 1179656 | tf_op jit(solution)/shard_map/ppermute | solution.py:270
  18.1 18.8 %collective-permute-start.8 = (bf16[6,128,256]{2,1,0:T(8,128)(2,1)S(1)}, bf16[6,128,256]{2,1,0:T(8,128)(2,1)S(1)}, u32[]{:S(2)}, u32[]{:S(2)}) collective-permute-start(bf16[6,128,256]{2,1,0:T(8,128)(2,1)S(1)} %collective-permute-done.1.rest_1_), channel_id=1, source_target_pairs={{1,0},{2,1},{3,2},{5,4},{6,5},{7,6},{9,8},{10,9},{11,10},{13,12},{... | collective-permute-start | bytes 1179656 | tf_op jit(solution)/shard_map/ppermute | solution.py:280
  19.3 22.6 %collective-permute-start.9 = (bf16[6,128,256]{2,1,0:T(8,128)(2,1)S(1)}, bf16[6,128,256]{2,1,0:T(8,128)(2,1)S(1)}, u32[]{:S(2)}, u32[]{:S(2)}) collective-permute-start(bf16[6,128,256]{2,1,0:T(8,128)(2,1)S(1)} %collective-permute-done.3.rest_3_), channel_id=1, source_target_pairs={{0,16},{4,20},{8,24},{12,28},{16,0},{20,4},{24,8},{28,12},{1,17},{... | collective-permute-start | bytes 1179656 | tf_op jit(solution)/shard_map/ppermute | solution.py:270
  24.3 23.9 %collective-permute-start.5 = (bf16[6,128,256]{2,1,0:T(8,128)(2,1)S(1)}, bf16[6,128,256]{2,1,0:T(8,128)(2,1)S(1)}, u32[]{:S(2)}, u32[]{:S(2)}) collective-permute-start(bf16[6,128,256]{2,1,0:T(8,128)(2,1)S(1)} %collective-permute-done.3.rest_3_), channel_id=1, source_target_pairs={{0,24},{4,28},{8,16},{12,20},{16,8},{20,12},{24,0},{28,4},{1,25},{... | collective-permute-start | bytes 1179656 | tf_op jit(solution)/shard_map/ppermute | solution.py:270
  25.3 16.6 %copy-start = (bf16[1,6,128,256]{3,2,1,0:T(8,128)(2,1)S(1)}, bf16[1,6,128,256]{3,2,1,0:T(8,128)(2,1)}, u32[]{:S(2)}) copy-start(bf16[1,6,128,256]{3,2,1,0:T(8,128)(2,1)} %param.9) | copy-start | bytes 1179652
  45.5 3.2 %collective-permute-start.10 = (bf16[6,128,256]{2,1,0:T(8,128)(2,1)S(1)}, bf16[6,128,256]{2,1,0:T(8,128)(2,1)S(1)}, u32[]{:S(2)}, u32[]{:S(2)}) collective-permute-start(bf16[6,128,256]{2,1,0:T(8,128)(2,1)S(1)} %shard_map.94), channel_id=1, source_target_pairs={{0,4},{4,0},{8,12},{12,8},{16,20},{20,16},{24,28},{28,24},{1,5},{5... | collective-permute-start | bytes 1179656 | tf_op jit(solution)/shard_map/ppermute | solution.py:270
  48.1 2.8 %collective-permute-start.6 = (bf16[6,128,256]{2,1,0:T(8,128)(2,1)S(1)}, bf16[6,128,256]{2,1,0:T(8,128)(2,1)S(1)}, u32[]{:S(2)}, u32[]{:S(2)}) collective-permute-start(bf16[6,128,256]{2,1,0:T(8,128)(2,1)S(1)} %collective-permute-done.5.rest_0_), channel_id=1, source_target_pairs={{0,4},{4,0},{8,12},{12,8},{16,20},{20,16},{24,28},{28,24},{1,5},{5... | collective-permute-start | bytes 1179656 | tf_op jit(solution)/shard_map/ppermute | solution.py:270

commit v7 on v4

--- a/solution.py
+++ b/solution.py
@@ -152,6 +152,7 @@
 
 
 def second_kernel(
+    second_end,
     near_shift,
     list_ref,
     rows_ref,
@@ -194,38 +195,28 @@
         value = jnp.where(found[1:2] > 0, found[0:1], near_slots)
         near_map = jnp.where(out_row == j, value, near_map)
     near_map_ref[...] = near_map
-    fill_operators(first_count, list_ref[2, 0], list_ref, rows_ref, weighted_ref, rad_ref, t_ref)
+    end = jnp.minimum(list_ref[2, 0], second_end)
+    fill_operators(first_count, end, list_ref, rows_ref, weighted_ref, rad_ref, t_ref)
     for copy in copies:
         copy.wait()
 
 
-def apply_kernel(
-    places, first_row, boxes, halo, with_total, with_other, dtype, cls_ref, near_map_ref, list_ref, t_ref, near_ref, *rest
-):
-    source_refs, rest = rest[: sum(parts for _, _, parts in places)], rest[sum(parts for _, _, parts in places) :]
-    if with_total:
-        sum_ref, *rest = rest
-    if with_other:
-        other_ref, *rest = rest
-    (out_ref,) = rest
+def add_products(places, first_row, boxes, halo, cls_ref, near_map_ref, list_ref, t_ref, near_ref, source_refs, start, store):
     me = lax.axis_index("dir")
     region_boxes = boxes * lax.axis_size("dir")
-    groups = []
-    at = 0
+    bases, groups, at = [], [], 0
     for rim, mask, parts in places:
+        groups.append(source_refs[at : at + parts])
+        at += parts
         owner = me ^ mask
         base = owner * boxes + halo
         if rim:
             base = base + jnp.where(owner * boxes >= halo, -region_boxes, region_boxes)
-        groups.append((base, source_refs[at : at + parts]))
-        at += parts
+        bases.append(base)
     for j in range(boxes):
         row = first_row + j
-        total = sum_ref[j] if with_total else None
-        if with_other:
-            other = other_ref[j].astype(F32)
-            total = other if total is None else total + other
-        for base, refs in groups:
+        total = start(j)
+        for base, refs in zip(bases, groups):
             blocks = []
             for b in range(boxes):
                 n = list_ref[1, cls_ref[row, base + b]]
@@ -234,10 +225,65 @@
             rhs = values[0] if len(values) == 1 else jnp.concatenate(values, 0)
             added = jnp.dot(jnp.concatenate(blocks, 1), rhs, preferred_element_type=F32)
             total = added if total is None else total + added
+        store(j, total)
+
+
+def third_kernel(
+    second_end,
+    places,
+    early,
+    boxes,
+    halo,
+    list_ref,
+    cls_ref,
+    near_map_ref,
+    rows_ref,
+    weighted_ref,
+    rad_ref,
+    near_ref,
+    *rest,
+):
+    source_count = sum(parts for _, _, parts in places)
+    source_refs, (_, t_ref, other_ref, own_ref) = rest[:source_count], rest[source_count:]
+    fill_operators(second_end, list_ref[2, 0], list_ref, rows_ref, weighted_ref, rad_ref, t_ref)
+
+    def store_other(j, total):
+        other_ref[j] = total.astype(other_ref.dtype)
+
+    def store_own(j, total):
+        own_ref[j] = total
+
+    refs = (cls_ref, near_map_ref, list_ref, t_ref, near_ref)
+    add_products(places, boxes, boxes, halo, *refs, source_refs, lambda j: None, store_other)
+    add_products(places[:early], 0, boxes, halo, *refs, source_refs, lambda j: None, store_own)
+
+
+def apply_kernel(
+    places, first_row, boxes, halo, with_total, with_other, cls_ref, near_map_ref, list_ref, t_ref, near_ref, *rest
+):
+    source_count = sum(parts for _, _, parts in places)
+    source_refs, rest = rest[:source_count], rest[source_count:]
+    if with_total:
+        sum_ref, *rest = rest
+    if with_other:
+        other_ref, *rest = rest
+    (out_ref,) = rest
+
+    def start(j):
+        total = sum_ref[j] if with_total else None
+        if with_other:
+            other = other_ref[j].astype(F32)
+            total = other if total is None else total + other
+        return total
+
+    def store(j, total):
         if len(out_ref.shape) == 4:
-            out_ref[0, j] = total.astype(dtype)
+            out_ref[0, j] = total.astype(out_ref.dtype)
         else:
-            out_ref[j] = total.astype(dtype)
+            out_ref[j] = total.astype(out_ref.dtype)
+
+    refs = (cls_ref, near_map_ref, list_ref, t_ref, near_ref)
+    add_products(places, first_row, boxes, halo, *refs, source_refs, start, store)
 
 
 def shards(
@@ -262,6 +308,7 @@
     near_halo = region_boxes // 4
     classes, directions = transfer_table.shape
     first_count = pad_to(classes // 4, UNROLL)
+    second_end = first_count + pad_to(classes // 5, UNROLL)
     top = dir_count // 2
     inner = range(2, top, 2)
     split = boxes // 2
@@ -340,7 +387,7 @@
         rim[m] = beyond(field[m])
 
     table, near_here, near_map = pl.pallas_call(
-        functools.partial(second_kernel, halo - near_halo),
+        functools.partial(second_kernel, second_end, halo - near_halo),
         in_specs=[smem] + [vmem] * 5 + [hbm] * 2 + [vmem],
         out_specs=[vmem] * 3,
         out_shape=(
@@ -364,17 +411,15 @@
     )
 
     def apply(places, first_row, total, other, dtype, shape):
-        full = (boxes, unknowns, incidences)
         if len(places) > GROUP:
             total = apply(places[:GROUP], first_row, total, None, F32, full)
             return apply(places[GROUP:], first_row, total, other, dtype, shape)
-        parts = [part for _, _, group in places for part in group]
-        args = [cls, near_map, listed, pinned(table), pinned(near_here)] + [pinned(part) for part in parts]
+        args = [cls, near_map, listed, pinned(table), pinned(near_here)] + [pinned(part) for _, _, parts in places for part in parts]
         args += [pinned(extra) for extra in (total, other) if extra is not None]
         specs = [smem] * 3 + [vmem] * (len(args) - 3)
-        layout = [(outside, mask, len(group)) for outside, mask, group in places]
+        layout = [(outside, mask, len(parts)) for outside, mask, parts in places]
         kernel = functools.partial(
-            apply_kernel, layout, first_row, boxes, halo, total is not None, other is not None, dtype
+            apply_kernel, layout, first_row, boxes, halo, total is not None, other is not None
         )
         return pl.pallas_call(
             kernel,
@@ -397,15 +442,38 @@
     early = [(False, m, [field[m]]) for m in (0, *inner, top)] + [(True, 0, [rim[0]])]
     middle = [(False, top + m, [field[top + m]]) for m in inner]
     middle += [(True, m, [rim[m]]) for m in (*inner, top)]
-    for_other = apply(early + middle, boxes, None, None, BF16, full)
-
+    ready = (early + middle)[:GROUP]
+    left = (early + middle)[GROUP:]
+    count = min(len(early), GROUP)
+    table, for_other, total = pl.pallas_call(
+        functools.partial(
+            third_kernel, second_end, [(outside, mask, 1) for outside, mask, _ in ready], count, boxes, halo
+        ),
+        in_specs=[smem] * 3 + [vmem] * (5 + len(ready)),
+        out_specs=[vmem] * 3,
+        out_shape=(
+            pltpu.VMEM(table_shape, BF16),
+            pltpu.VMEM(full, F32 if left else BF16),
+            pltpu.VMEM(full, F32),
+        ),
+        input_output_aliases={7 + len(ready): 0},
+        compiler_params=pltpu.CompilerParams(vmem_limit_bytes=12 * MIB),
+        cost_estimate=pl.CostEstimate(flops=MIB, bytes_accessed=MIB, transcendentals=0),
+    )(
+        listed,
+        cls,
+        near_map,
+        *[pinned(a) for a in (rows, weighted, rad_here, near_here, *[parts[0] for _, _, parts in ready], table)],
+    )
+    if left:
+        for_other = apply(left, boxes, for_other, None, BF16, full)
     from_other = partner(for_other, 1)
-    total = apply(early, 0, None, None, F32, full)
 
     total, last = lax.optimization_barrier((total, last))
     turned = {m: [partner(part, 1) for part in last[m]] for m in inner}
-    total = apply(middle, 0, total, from_other, F32, full)
-    late = [(True, top + m, last[m]) for m in inner] + [(True, top + m + 1, turned[m]) for m in inner]
+    total = apply((early + middle)[count:], 0, total, from_other, F32, full)
+    late = [(True, top + m, last[m]) for m in inner]
+    late += [(True, top + m + 1, turned[m]) for m in inner]
     return apply(late, 0, total, None, BF16, currents.shape)
 
 

time: 50.7 us -> 51.2 us (level); the launches traced: 51.2 us -> 50.4 us
  starting transfers between devices: 16.8 us -> 15.3 us
  waiting for transfers between devices: 0.16 us -> 1.14 us
    pallas_call x4 -> x2, Pallas kernels: 11 us -> 4.91 us  [apply(): pl.pallas_call(kernel, in_specs=specs, out_specs=vmem, out_shape=pltpu.VM...]
    pallas_call x1 -> x2, Pallas kernels: 11.5 us -> 16.9 us  [the longest x1 9.99 us: shards(): pl.pallas_call(functools.partial(second_kernel, second_end, halo - near_h...]
    ppermute x11, starting transfers between devices: 14.2 us -> 12.7 us  [partner(): return lax.ppermute(array, 'dir', [(i, i ^ mask) for i in range(dir_count)])]
    ppermute x11, waiting for transfers between devices: 0.03 us -> 1.14 us  [partner(): return lax.ppermute(array, 'dir', [(i, i ^ mask) for i in range(dir_count)])]
  transfers between devices with their start and end apart: 13 -> 13, of which waited for: 1 -> 1; matrix products, arithmetic and copies ran while one was open for 0% -> 0% of each run, Pallas kernels for 61% -> 62%
where the time goes in v7:
time: 51.2 us; the launch traced here: 50.4 us
  Pallas kernels  33.7 us (66%)
  starting transfers between devices  15.3 us (30%)
  waiting for transfers between devices  1.14 us (2%)
    ppermute x11, starting transfers between devices, partner(): return lax.ppermute(array, 'dir', [(i, i ^ mask) for i in range(dir_count)])  12.7 us
    pallas_call x1, Pallas kernels, shards(): pl.pallas_call(functools.partial(first_kernel, first_count, boxes, halo,...  12 us
    pallas_call x1, Pallas kernels, shards(): pl.pallas_call(functools.partial(second_kernel, second_end, halo - near_h...  9.99 us
    pallas_call x1, Pallas kernels, shards(): pl.pallas_call(functools.partial(third_kernel, second_end, [(outside, mas...  6.88 us
    pallas_call x2, Pallas kernels, apply(): pl.pallas_call(kernel, in_specs=specs, out_specs=vmem, out_shape=pltpu.VM...  4.91 us
    ppermute x2, starting transfers between devices, beyond(): return lax.ppermute(array, ('dir', 'region'), along)  2.57 us
    ppermute x11, waiting for transfers between devices, partner(): return lax.ppermute(array, 'dir', [(i, i ^ mask) for i in range(dir_count)])  1.14 us
  transfers between devices with their start and end apart: 13, of which 1 were waited for; matrix products, arithmetic and copies ran while one was open for 0% of the time, Pallas kernels for 62%

profile of v7, /device:TPU:0, one launch (start us, length us, event | category | flops | bytes accessed | tf_op | source)
XLA Modules:
  0.0 50.4 jit_solution(17377858846265942131)
XLA Ops:
  0.0 0.5 collective-permute-start.1
  0.5 1.3 %collective-permute-start.4 = (bf16[6,128,256]{2,1,0:T(8,128)(2,1)}, bf16[6,128,256]{2,1,0:T(8,128)(2,1)S(1)}, u32[]{:S(2)}, u32[]{:S(2)}) collective-permute-start(bf16[6,128,256]{2,1,0:T(8,128)(2,1)} %bitcast.2), channel_id=1, source_target_pairs={{1,0},{2,1},{3,2},{5,4},{6,5},{7,6},{9,8},{10,9},{11,10},{13,12},{... | collective-permute-start | bytes 1179656 | tf_op jit(solution)/shard_map/ppermute | solution.py:328
  1.7 4.8 %collective-permute-start.3 = (bf16[6,128,256]{2,1,0:T(8,128)(2,1)}, bf16[6,128,256]{2,1,0:T(8,128)(2,1)S(1)}, u32[]{:S(2)}, u32[]{:S(2)}) collective-permute-start(bf16[6,128,256]{2,1,0:T(8,128)(2,1)} %bitcast.3), channel_id=1, source_target_pairs={{0,16},{4,20},{8,24},{12,28},{16,0},{20,4},{24,8},{28,12},{1,17},{... | collective-permute-start | bytes 1179656 | tf_op jit(solution)/shard_map/ppermute | solution.py:318
  6.5 1.5 %collective-permute-start.2 = (bf16[6,128,256]{2,1,0:T(8,128)(2,1)}, bf16[6,128,256]{2,1,0:T(8,128)(2,1)S(1)}, u32[]{:S(2)}, u32[]{:S(2)}) collective-permute-start(bf16[6,128,256]{2,1,0:T(8,128)(2,1)} %bitcast.4), channel_id=1, source_target_pairs={{0,8},{4,12},{8,0},{12,4},{16,24},{20,28},{24,16},{28,20},{1,9},{5... | collective-permute-start | bytes 1179656 | tf_op jit(solution)/shard_map/ppermute | solution.py:318
  8.0 0.0 collective-permute-start
  8.0 12.0 %shard_map.91 = (bf16[80,128,128]{2,1,0:T(8,128)(2,1)S(1)}, bf16[128,1536]{1,0:T(8,128)(2,1)S(1)}, bf16[1536,128]{1,0:T(8,128)(2,1)S(1)}, f32[316,1536]{1,0:T(8,...) custom-call(s32[9]{0:T(128)} %off_hbm.1, s32[1,48,48]{2,1,0:T(8,128)} %src_hbm.1, s32[1,48,48]{2,1,0:T(8,128)} %tid_hbm.1, ...), custom_call_target="tpu_custom_call" | custom-call | flops 7952400384 | bytes 1048576 | tf_op jit(solution)/shard_map/pallas_call | solution.py:354
  20.0 0.0 collective-permute-done.4.rest_3_
  20.0 0.0 collective-permute-done.3.rest_2_
  20.0 0.0 collective-permute-done.2.rest_1_
  20.0 1.3 %collective-permute-start.6 = (bf16[6,128,256]{2,1,0:T(8,128)(2,1)S(1)}, bf16[6,128,256]{2,1,0:T(8,128)(2,1)S(1)}, u32[]{:S(2)}, u32[]{:S(2)}) collective-permute-start(bf16[6,128,256]{2,1,0:T(8,128)(2,1)S(1)} %collective-permute-done.2.rest_1_), channel_id=1, source_target_pairs={{1,0},{2,1},{3,2},{5,4},{6,5},{7,6},{9,8},{10,9},{11,10},{13,12},{... | collective-permute-start | bytes 1179656 | tf_op jit(solution)/shard_map/ppermute | solution.py:328
  21.3 0.6 %collective-permute-start.5 = (bf16[6,128,256]{2,1,0:T(8,128)(2,1)S(1)}, bf16[6,128,256]{2,1,0:T(8,128)(2,1)S(1)}, u32[]{:S(2)}, u32[]{:S(2)}) collective-permute-start(bf16[6,128,256]{2,1,0:T(8,128)(2,1)S(1)} %collective-permute-done.3.rest_2_), channel_id=1, source_target_pairs={{0,8},{4,12},{8,0},{12,4},{16,24},{20,28},{24,16},{28,20},{1,9},{5... | collective-permute-start | bytes 1179656 | tf_op jit(solution)/shard_map/ppermute | solution.py:318
  21.9 2.3 %collective-permute-start.7 = (bf16[6,128,256]{2,1,0:T(8,128)(2,1)S(1)}, bf16[6,128,256]{2,1,0:T(8,128)(2,1)S(1)}, u32[]{:S(2)}, u32[]{:S(2)}) collective-permute-start(bf16[6,128,256]{2,1,0:T(8,128)(2,1)S(1)} %collective-permute-done.4.rest_3_), channel_id=1, source_target_pairs={{0,16},{4,20},{8,24},{12,28},{16,0},{20,4},{24,8},{28,12},{1,17},{... | collective-permute-start | bytes 1179656 | tf_op jit(solution)/shard_map/ppermute | solution.py:318
  24.2 0.0 collective-permute-done.near_src_other_ref
  24.2 0.0 collective-permute-done.1.near_other_hbm
  24.2 0.0 copy-start
  24.2 10.0 %shard_map.92 = (bf16[317,128,128]{2,1,0:T(8,128)(2,1)S(1)}, bf16[12,28,128,128]{3,2,1,0:T(8,128)(2,1)S(1)}, s32[16,128]{1,0:T(8,128)S(1)}) custom-call(s32[8,384]{1,0:T(8,128)S(1)} %get-tuple-element.29.list_ref, f32[316,1536]{1,0:T(8,128)S(1)} %get-tuple-element.30.rows_ref, bf16[128,1536]{1,0:T(8,128)(2,1)S(1)} %get-tuple-element.31.weighted_ref, ...), custom_call_target="tpu_custom_call" | custom-call | flops 7952400384 | bytes 1048576 | tf_op jit(solution)/shard_map/pallas_call | solution.py:389
  34.2 0.0 collective-permute-done.6.rest_5_.rest_1_
  34.2 0.0 collective-permute-done.5.rest_4_.rest_0_
  34.2 0.0 collective-permute-done.7.rest_6_.rest_2_
  34.3 1.6 %collective-permute-start.8 = (bf16[3,128,256]{2,1,0:T(8,128)(2,1)S(1)}, bf16[3,128,256]{2,1,0:T(8,128)(2,1)S(1)}, u32[]{:S(2)}, u32[]{:S(2)}) collective-permute-start(bf16[3,128,256]{2,1,0:T(8,128)(2,1)S(1)} %slice.6), channel_id=1, source_target_pairs={{0,8},{4,12},{8,0},{12,4},{16,24},{20,28},{24,16},{28,20},{1,9},{5... | collective-permute-start | bytes 589832 | tf_op jit(solution)/shard_map/ppermute | solution.py:318
  35.9 0.9 %collective-permute-start.9 = (bf16[3,128,256]{2,1,0:T(8,128)(2,1)S(1)}, bf16[3,128,256]{2,1,0:T(8,128)(2,1)S(1)}, u32[]{:S(2)}, u32[]{:S(2)}) collective-permute-start(bf16[3,128,256]{2,1,0:T(8,128)(2,1)S(1)} %slice.7), channel_id=1, source_target_pairs={{0,16},{4,20},{8,24},{12,28},{16,0},{20,4},{24,8},{28,12},{1,17},{... | collective-permute-start | bytes 589832 | tf_op jit(solution)/shard_map/ppermute | solution.py:318
  36.8 6.9 %shard_map.93 = (bf16[317,128,128]{2,1,0:T(8,128)(2,1)S(1)}, bf16[6,128,256]{2,1,0:T(8,128)(2,1)S(1)}, f32[6,128,256]{2,1,0:T(8,128)S(1)}) custom-call(s32[8,384]{1,0:T(8,128)S(1)} %get-tuple-element.29.list_ref, s32[16,128]{1,0:T(8,128)S(1)} %get-tuple-element.28.cls_ref, ...), custom_call_target="tpu_custom_call", output_to_operand_aliasing={{0}: (14, {})} | custom-call | flops 1048576 | bytes 1048576 | tf_op jit(solution)/shard_map/pallas_call | solution.py:448
  43.6 0.1 collective-permute-start.12
  43.7 0.0 collective-permute-done.8.rest_0_
  43.7 0.0 collective-permute-done.9.rest_1_
  43.7 0.5 collective-permute-start.10
  44.2 0.1 collective-permute-start.11
  44.3 1.1 %collective-permute-done.12.rest_4_ = bf16[6,128,256]{2,1,0:T(8,128)(2,1)S(1)} collective-permute-done((bf16[6,128,256]{2,1,0:T(8,128)(2,1)S(1)}, bf16[6,128,256]{2,1,0:T(8,128)(2,1)S(1)}, u32[]{:S(2)}, u32[]{:S(2)}) %collective-permute-start.12) | collective-permute-done | bytes 393248 | tf_op jit(solution)/shard_map/ppermute | solution.py:318
  45.4 2.2 %shard_map.94.rest_4_ = f32[6,128,256]{2,1,0:T(8,128)S(1)} custom-call(s32[16,128]{1,0:T(8,128)S(1)} %get-tuple-element.28.cls_ref, s32[16,128]{1,0:T(8,128)S(1)} %get-tuple-element.35.near_map_ref, s32[8,384]{1,0:T(8,128)S(1)} %get-tuple-element.29.list_ref, bf16[317,128,128]{2,1,0:T(8,128)(2,1)S(1)} %get-tuple-element.45.t_ref, ...), custom_call_target="tpu_custom_call" | custom-call | flops 1048576 | bytes 1048576 | tf_op jit(solution)/shard_map/pallas_call | solution.py:424
  47.7 0.0 collective-permute-done.10.rest_2_
  47.7 0.0 collective-permute-done.11.rest_3_
  47.7 2.7 %shard_map.95 = bf16[1,6,128,256]{3,2,1,0:T(8,128)(2,1)} custom-call(s32[16,128]{1,0:T(8,128)S(1)} %get-tuple-element.28.cls_ref, s32[16,128]{1,0:T(8,128)S(1)} %get-tuple-element.35.near_map_ref, s32[8,384]{1,0:T(8,128)S(1)} %get-tuple-element.29.list_ref, bf16[317,128,128]{2,1,0:T(8,128)(2,1)S(1)} %get-tuple-element.45.t_ref, ...), custom_call_target="tpu_custom_call" | custom-call | flops 1048576 | bytes 1048576 | tf_op jit(solution)/shard_map/pallas_call | solution.py:424
  (5 shorter events, 0.0 us)
Async XLA Ops:
  0.0 24.2 %collective-permute-start.1 = (bf16[1,6,27,128,128]{4,3,2,1,0:T(8,128)(2,1)}, bf16[1,6,27,128,128]{4,3,2,1,0:T(8,128)(2,1)S(1)}, u32[]{:S(2)}, u32[]{:S(2)}) collective-permute-start(bf16[1,6,27,128,128]{4,3,2,1,0:T(8,128)(2,1)} %near_hbm.1), channel_id=1, source_target_pairs={{0,4},{4,0},{8,12},{12,8},{16,20},{20,16},{24,28},{28,24},{1,5},{5... | collective-permute-start | bytes 15925256 | tf_op jit(solution)/shard_map/ppermute | solution.py:318
  0.5 19.5 %collective-permute-start.4 = (bf16[6,128,256]{2,1,0:T(8,128)(2,1)}, bf16[6,128,256]{2,1,0:T(8,128)(2,1)S(1)}, u32[]{:S(2)}, u32[]{:S(2)}) collective-permute-start(bf16[6,128,256]{2,1,0:T(8,128)(2,1)} %bitcast.2), channel_id=1, source_target_pairs={{1,0},{2,1},{3,2},{5,4},{6,5},{7,6},{9,8},{10,9},{11,10},{13,12},{... | collective-permute-start | bytes 1179656 | tf_op jit(solution)/shard_map/ppermute | solution.py:328
  1.7 18.3 %collective-permute-start.3 = (bf16[6,128,256]{2,1,0:T(8,128)(2,1)}, bf16[6,128,256]{2,1,0:T(8,128)(2,1)S(1)}, u32[]{:S(2)}, u32[]{:S(2)}) collective-permute-start(bf16[6,128,256]{2,1,0:T(8,128)(2,1)} %bitcast.3), channel_id=1, source_target_pairs={{0,16},{4,20},{8,24},{12,28},{16,0},{20,4},{24,8},{28,12},{1,17},{... | collective-permute-start | bytes 1179656 | tf_op jit(solution)/shard_map/ppermute | solution.py:318
  6.5 13.5 %collective-permute-start.2 = (bf16[6,128,256]{2,1,0:T(8,128)(2,1)}, bf16[6,128,256]{2,1,0:T(8,128)(2,1)S(1)}, u32[]{:S(2)}, u32[]{:S(2)}) collective-permute-start(bf16[6,128,256]{2,1,0:T(8,128)(2,1)} %bitcast.4), channel_id=1, source_target_pairs={{0,8},{4,12},{8,0},{12,4},{16,24},{20,28},{24,16},{28,20},{1,9},{5... | collective-permute-start | bytes 1179656 | tf_op jit(solution)/shard_map/ppermute | solution.py:318
  8.0 16.2 %copy-start.1 = (s32[1,6,27]{2,0,1:T(1,128)S(1)}, s32[1,6,27]{2,0,1:T(1,128)}, u32[]{:S(2)}) copy-start(s32[1,6,27]{2,0,1:T(1,128)} %param.17) | copy-start | bytes 1948
  8.0 16.2 %collective-permute-start = (s32[6,1,27]{2,1,0:T(1,128)}, s32[6,1,27]{2,1,0:T(1,128)S(1)}, u32[]{:S(2)}, u32[]{:S(2)}) collective-permute-start(s32[6,1,27]{2,1,0:T(1,128)} %bitcast.6), channel_id=1, source_target_pairs={{0,4},{4,0},{8,12},{12,8},{16,20},{20,16},{24,28},{28,24},{1,5},{5... | collective-permute-start | bytes 1952 | tf_op jit(solution)/shard_map/ppermute | solution.py:318
  20.0 14.2 %collective-permute-start.6 = (bf16[6,128,256]{2,1,0:T(8,128)(2,1)S(1)}, bf16[6,128,256]{2,1,0:T(8,128)(2,1)S(1)}, u32[]{:S(2)}, u32[]{:S(2)}) collective-permute-start(bf16[6,128,256]{2,1,0:T(8,128)(2,1)S(1)} %collective-permute-done.2.rest_1_), channel_id=1, source_target_pairs={{1,0},{2,1},{3,2},{5,4},{6,5},{7,6},{9,8},{10,9},{11,10},{13,12},{... | collective-permute-start | bytes 1179656 | tf_op jit(solution)/shard_map/ppermute | solution.py:328
  21.3 12.9 %collective-permute-start.5 = (bf16[6,128,256]{2,1,0:T(8,128)(2,1)S(1)}, bf16[6,128,256]{2,1,0:T(8,128)(2,1)S(1)}, u32[]{:S(2)}, u32[]{:S(2)}) collective-permute-start(bf16[6,128,256]{2,1,0:T(8,128)(2,1)S(1)} %collective-permute-done.3.rest_2_), channel_id=1, source_target_pairs={{0,8},{4,12},{8,0},{12,4},{16,24},{20,28},{24,16},{28,20},{1,9},{5... | collective-permute-start | bytes 1179656 | tf_op jit(solution)/shard_map/ppermute | solution.py:318
  21.9 12.3 %collective-permute-start.7 = (bf16[6,128,256]{2,1,0:T(8,128)(2,1)S(1)}, bf16[6,128,256]{2,1,0:T(8,128)(2,1)S(1)}, u32[]{:S(2)}, u32[]{:S(2)}) collective-permute-start(bf16[6,128,256]{2,1,0:T(8,128)(2,1)S(1)} %collective-permute-done.4.rest_3_), channel_id=1, source_target_pairs={{0,16},{4,20},{8,24},{12,28},{16,0},{20,4},{24,8},{28,12},{1,17},{... | collective-permute-start | bytes 1179656 | tf_op jit(solution)/shard_map/ppermute | solution.py:318
  24.2 12.5 %copy-start = (bf16[1,6,128,256]{3,2,1,0:T(8,128)(2,1)S(1)}, bf16[1,6,128,256]{3,2,1,0:T(8,128)(2,1)}, u32[]{:S(2)}) copy-start(bf16[1,6,128,256]{3,2,1,0:T(8,128)(2,1)} %param.9) | copy-start | bytes 1179652
  34.3 9.4 %collective-permute-start.8 = (bf16[3,128,256]{2,1,0:T(8,128)(2,1)S(1)}, bf16[3,128,256]{2,1,0:T(8,128)(2,1)S(1)}, u32[]{:S(2)}, u32[]{:S(2)}) collective-permute-start(bf16[3,128,256]{2,1,0:T(8,128)(2,1)S(1)} %slice.6), channel_id=1, source_target_pairs={{0,8},{4,12},{8,0},{12,4},{16,24},{20,28},{24,16},{28,20},{1,9},{5... | collective-permute-start | bytes 589832 | tf_op jit(solution)/shard_map/ppermute | solution.py:318
  35.9 7.9 %collective-permute-start.9 = (bf16[3,128,256]{2,1,0:T(8,128)(2,1)S(1)}, bf16[3,128,256]{2,1,0:T(8,128)(2,1)S(1)}, u32[]{:S(2)}, u32[]{:S(2)}) collective-permute-start(bf16[3,128,256]{2,1,0:T(8,128)(2,1)S(1)} %slice.7), channel_id=1, source_target_pairs={{0,16},{4,20},{8,24},{12,28},{16,0},{20,4},{24,8},{28,12},{1,17},{... | collective-permute-start | bytes 589832 | tf_op jit(solution)/shard_map/ppermute | solution.py:318
  43.6 1.8 %collective-permute-start.12 = (bf16[6,128,256]{2,1,0:T(8,128)(2,1)S(1)}, bf16[6,128,256]{2,1,0:T(8,128)(2,1)S(1)}, u32[]{:S(2)}, u32[]{:S(2)}) collective-permute-start(bf16[6,128,256]{2,1,0:T(8,128)(2,1)S(1)} %get-tuple-element.50), channel_id=1, source_target_pairs={{0,4},{4,0},{8,12},{12,8},{16,20},{20,16},{24,28},{28,24},{1,5},{5... | collective-permute-start | bytes 1179656 | tf_op jit(solution)/shard_map/ppermute | solution.py:318
  43.7 3.9 %collective-permute-start.10 = (bf16[3,128,256]{2,1,0:T(8,128)(2,1)S(1)}, bf16[3,128,256]{2,1,0:T(8,128)(2,1)S(1)}, u32[]{:S(2)}, u32[]{:S(2)}) collective-permute-start(bf16[3,128,256]{2,1,0:T(8,128)(2,1)S(1)} %collective-permute-done.8.rest_0_), channel_id=1, source_target_pairs={{0,4},{4,0},{8,12},{12,8},{16,20},{20,16},{24,28},{28,24},{1,5},{5... | collective-permute-start | bytes 589832 | tf_op jit(solution)/shard_map/ppermute | solution.py:318
  44.2 3.5 %collective-permute-start.11 = (bf16[3,128,256]{2,1,0:T(8,128)(2,1)S(1)}, bf16[3,128,256]{2,1,0:T(8,128)(2,1)S(1)}, u32[]{:S(2)}, u32[]{:S(2)}) collective-permute-start(bf16[3,128,256]{2,1,0:T(8,128)(2,1)S(1)} %collective-permute-done.9.rest_1_), channel_id=1, source_target_pairs={{0,4},{4,0},{8,12},{12,8},{16,20},{20,16},{24,28},{28,24},{1,5},{5... | collective-permute-start | bytes 589832 | tf_op jit(solution)/shard_map/ppermute | solution.py:318

commit v8 on v7

--- a/solution.py
+++ b/solution.py
@@ -52,7 +52,7 @@
 
 
 def first_kernel(
-    first_count,
+    shared,
     boxes,
     halo,
     region_boxes,
@@ -100,6 +100,7 @@
     row_at = lax.broadcasted_iota(I32, (ROWS, slots), 0)
     out_row = lax.broadcasted_iota(I32, cls_ref.shape, 0)
     seen = jnp.zeros((used_width, slots), F32)
+    seen_by_chip = seen
     cls = jnp.full(cls_ref.shape, classes, I32)
     copies[0].wait()
     copies[1].wait()
@@ -113,23 +114,37 @@
         even = (mask & 1) == 0
         here = (src >= 0) & ((even | late) if j < boxes else (even & ~late))
         seen = jnp.where((class_at == tid) & here, 1.0, seen)
+        seen_by_chip = jnp.where((class_at == tid) & (src >= 0), 1.0, seen_by_chip)
         parts = jnp.where(row_at == 0, tid // 16, jnp.where(row_at == 1, tid % 16, 1))
         found = lookup(parts, jnp.where(ext_at == src, 1.0, 0.0))
         value = jnp.where(found[2:3] > 0, found[0:1] * 16 + found[1:2], classes)
         cls = jnp.where(out_row == j, value, cls)
     cls_ref[...] = cls
-    is_used = jnp.minimum(lookup(jnp.ones((ROWS, slots), I32), seen), 1)
+    lane = lax.broadcasted_iota(I32, (ROWS, used_width), 1)
+    list_row = lax.broadcasted_iota(I32, (ROWS, used_width), 0)
+    ones = jnp.ones((ROWS, slots), I32)
+    by_chip = jnp.where(lane < shared, jnp.minimum(lookup(ones, seen_by_chip), 1), 0)
+    by_core = jnp.where(lane >= shared, jnp.minimum(lookup(ones, seen), 1), 0)
+    is_used = jnp.where(list_row == 0, by_chip, by_core)
     down = lax.broadcasted_iota(I32, (used_width, used_width), 0)
     across = lax.broadcasted_iota(I32, (used_width, used_width), 1)
     rank = lookup(is_used, jnp.where(across < down, 1.0, 0.0))
-    here = (down == rank[0:1]) & (is_used[0:1] > 0)
-    lane = lax.broadcasted_iota(I32, (ROWS, used_width), 1)
-    list_row = lax.broadcasted_iota(I32, (ROWS, used_width), 0)
+    shared_rank, own_rank = rank[0:1], rank[1:2]
+    one_lane = lane[0:1]
+    capacity = (shared + 1) // 2
+    empty = capacity + classes - shared
+    other = (shared_rank ^ me) & 1
+    shared_place = shared_rank // 2 + other * (empty + 1)
+    place = jnp.where(one_lane < shared, shared_place, capacity + own_rank)
+    place = jnp.where(one_lane == classes, empty, place)
+    listed_here = jnp.where(one_lane < shared, is_used[0:1] * (1 - other), is_used[1:2])
+    here = down == jnp.where(listed_here > 0, place, -1)
     found = lookup(jnp.where(list_row == 0, lane // 16, lane % 16), jnp.where(here, 1.0, 0.0))
     ordered = found[0:1] * 16 + found[1:2]
-    rank = jnp.where(lane == classes, classes, rank)
-    count = jnp.sum(is_used[0:1].astype(F32), axis=1, keepdims=True).astype(I32)
-    listed = jnp.where(list_row == 0, ordered, jnp.where(list_row == 1, rank, count))
+    count = jnp.sum(is_used.astype(F32), axis=1, keepdims=True).astype(I32)
+    first_end = (count[0:1] - (me & 1) + 1) // 2
+    ends = jnp.where(one_lane == 0, first_end, capacity + count[1:2])
+    listed = jnp.where(list_row == 0, ordered, jnp.where(list_row == 1, place, ends))
     listed_ref[...] = listed
     to_smem = pltpu.make_async_copy(listed_ref, list_ref, sems.at[len(pairs)])
     to_smem.start()
@@ -146,13 +161,13 @@
     copies[4].wait()
     rows_ref[...] = table_ref[...].astype(F32)
     to_smem.wait()
-    count = list_ref[2, 0]
     copies[5].wait()
-    fill_operators(0, jnp.minimum(count, first_count), list_ref, rows_ref, weighted_ref, rad_ref, t_ref)
+    fill_operators(0, list_ref[2, 0], list_ref, rows_ref, weighted_ref, rad_ref, t_ref)
 
 
 def second_kernel(
     second_end,
+    empty,
     near_shift,
     list_ref,
     rows_ref,
@@ -180,7 +195,7 @@
     first_count = low_ref.shape[0]
     copies.append(pltpu.make_async_copy(low_ref, t_ref.at[pl.ds(0, first_count)], sems.at[2 * boxes]))
     copies[-1].start()
-    t_ref[t_ref.shape[0] - 1] = jnp.zeros(t_ref.shape[1:], BF16)
+    t_ref[empty] = jnp.zeros(t_ref.shape[1:], BF16)
     for row in range(2 * boxes):
         near_ref[row, near_slots] = jnp.zeros(near_ref.shape[2:], BF16)
     width = near_map_ref.shape[1]
@@ -195,7 +210,7 @@
         value = jnp.where(found[1:2] > 0, found[0:1], near_slots)
         near_map = jnp.where(out_row == j, value, near_map)
     near_map_ref[...] = near_map
-    end = jnp.minimum(list_ref[2, 0], second_end)
+    end = jnp.minimum(list_ref[2, 1], second_end)
     fill_operators(first_count, end, list_ref, rows_ref, weighted_ref, rad_ref, t_ref)
     for copy in copies:
         copy.wait()
@@ -230,6 +245,7 @@
 
 def third_kernel(
     second_end,
+    empty,
     places,
     early,
     boxes,
@@ -241,11 +257,15 @@
     weighted_ref,
     rad_ref,
     near_ref,
+    low_ref,
     *rest,
 ):
     source_count = sum(parts for _, _, parts in places)
-    source_refs, (_, t_ref, other_ref, own_ref) = rest[:source_count], rest[source_count:]
-    fill_operators(second_end, list_ref[2, 0], list_ref, rows_ref, weighted_ref, rad_ref, t_ref)
+    source_refs, (_, t_ref, other_ref, own_ref, sem) = rest[:source_count], rest[source_count:]
+    copy = pltpu.make_async_copy(low_ref, t_ref.at[pl.ds(empty + 1, low_ref.shape[0])], sem)
+    copy.start()
+    fill_operators(second_end, list_ref[2, 1], list_ref, rows_ref, weighted_ref, rad_ref, t_ref)
+    copy.wait()
 
     def store_other(j, total):
         other_ref[j] = total.astype(other_ref.dtype)
@@ -307,8 +327,10 @@
     halo = region_boxes // 2
     near_halo = region_boxes // 4
     classes, directions = transfer_table.shape
-    first_count = pad_to(classes // 4, UNROLL)
-    second_end = first_count + pad_to(classes // 5, UNROLL)
+    shared = classes * 5 // 8
+    capacity = (shared + 1) // 2
+    empty = capacity + classes - shared
+    second_end = capacity + pad_to(classes // 5, UNROLL)
     top = dir_count // 2
     inner = range(2, top, 2)
     split = boxes // 2
@@ -335,8 +357,8 @@
 
     width = pad_to(region_boxes + 2 * halo, LANES)
     map_shape = (pad_to(targets, ROWS), width)
-    table_shape = (classes + 1, unknowns, unknowns)
-    low_shape = (first_count, unknowns, unknowns)
+    table_shape = (empty + 1 + capacity, unknowns, unknowns)
+    low_shape = (capacity, unknowns, unknowns)
     list_shape = (ROWS, pad_to(classes + 1, LANES))
     vmem, smem, hbm = whole(pltpu.VMEM), whole(pltpu.SMEM), whole(pltpu.HBM)
     operator_cost = pl.CostEstimate(
@@ -352,7 +374,7 @@
     near_other = partner(near_blocks, 1)
     near_src_other = partner(near_src, 1)
     low, weighted, rad_here, rows, cls, listed = pl.pallas_call(
-        functools.partial(first_kernel, first_count, boxes, halo, region_boxes),
+        functools.partial(first_kernel, shared, boxes, halo, region_boxes),
         in_specs=[hbm] * 6,
         out_specs=[vmem] * 6,
         out_shape=(
@@ -380,6 +402,8 @@
     low, inner_fields, field[top], rim[0] = tied
     for m, value in zip(inner, inner_fields):
         field[m] = value
+    low, near_other, near_src_other = lax.optimization_barrier((low, near_other, near_src_other))
+    low_other = partner(low, 1)
     for m in inner:
         field[top + m] = partner(field[top], m)
     rim[top] = partner(rim[0], top)
@@ -387,7 +411,7 @@
         rim[m] = beyond(field[m])
 
     table, near_here, near_map = pl.pallas_call(
-        functools.partial(second_kernel, second_end, halo - near_halo),
+        functools.partial(second_kernel, second_end, empty, halo - near_halo),
         in_specs=[smem] + [vmem] * 5 + [hbm] * 2 + [vmem],
         out_specs=[vmem] * 3,
         out_shape=(
@@ -447,23 +471,24 @@
     count = min(len(early), GROUP)
     table, for_other, total = pl.pallas_call(
         functools.partial(
-            third_kernel, second_end, [(outside, mask, 1) for outside, mask, _ in ready], count, boxes, halo
+            third_kernel, second_end, empty, [(outside, mask, 1) for outside, mask, _ in ready], count, boxes, halo
         ),
-        in_specs=[smem] * 3 + [vmem] * (5 + len(ready)),
+        in_specs=[smem] * 3 + [vmem] * (6 + len(ready)),
         out_specs=[vmem] * 3,
         out_shape=(
             pltpu.VMEM(table_shape, BF16),
             pltpu.VMEM(full, F32 if left else BF16),
             pltpu.VMEM(full, F32),
         ),
-        input_output_aliases={7 + len(ready): 0},
+        input_output_aliases={8 + len(ready): 0},
+        scratch_shapes=[pltpu.SemaphoreType.DMA],
         compiler_params=pltpu.CompilerParams(vmem_limit_bytes=12 * MIB),
         cost_estimate=pl.CostEstimate(flops=MIB, bytes_accessed=MIB, transcendentals=0),
     )(
         listed,
         cls,
         near_map,
-        *[pinned(a) for a in (rows, weighted, rad_here, near_here, *[parts[0] for _, _, parts in ready], table)],
+        *[pinned(a) for a in (rows, weighted, rad_here, near_here, low_other, *[parts[0] for _, _, parts in ready], table)],
     )
     if left:
         for_other = apply(left, boxes, for_other, None, BF16, full)

time: 51.2 us -> 49.7 us (0.971); the launches traced: 50.4 us -> 49.6 us
  Pallas kernels: 33.7 us -> 31.4 us
  starting transfers between devices: 15.3 us -> 16.8 us
    pallas_call x3, Pallas kernels: 28.8 us -> 26.5 us  [the longest x1 11.3 us: shards(): pl.pallas_call(functools.partial(first_kernel, shared, boxes, halo, regio...]
    ppermute x11 -> x12, starting transfers between devices: 12.7 us -> 14.2 us  [partner(): return lax.ppermute(array, 'dir', [(i, i ^ mask) for i in range(dir_count)])]
    ppermute x11 -> x12, waiting for transfers between devices: 1.14 us -> 1.14 us  [partner(): return lax.ppermute(array, 'dir', [(i, i ^ mask) for i in range(dir_count)])]
  transfers between devices with their start and end apart: 13 -> 14, of which waited for: 1 -> 1; matrix products, arithmetic and copies ran while one was open for 0% -> 0% of each run, Pallas kernels for 62% -> 58%
where the time goes in v8:
time: 49.7 us; the launch traced here: 49.6 us
  Pallas kernels  31.4 us (63%)
  starting transfers between devices  16.8 us (34%)
  waiting for transfers between devices  1.15 us (2%)
    ppermute x12, starting transfers between devices, partner(): return lax.ppermute(array, 'dir', [(i, i ^ mask) for i in range(dir_count)])  14.2 us
    pallas_call x1, Pallas kernels, shards(): pl.pallas_call(functools.partial(first_kernel, shared, boxes, halo, regio...  11.3 us
    pallas_call x1, Pallas kernels, shards(): pl.pallas_call(functools.partial(second_kernel, second_end, empty, halo -...  9.73 us
    pallas_call x1, Pallas kernels, shards(): pl.pallas_call(functools.partial(third_kernel, second_end, empty, [(outsi...  5.51 us
    pallas_call x2, Pallas kernels, apply(): pl.pallas_call(kernel, in_specs=specs, out_specs=vmem, out_shape=pltpu.VM...  4.9 us
    ppermute x2, starting transfers between devices, beyond(): return lax.ppermute(array, ('dir', 'region'), along)  2.56 us
    ppermute x12, waiting for transfers between devices, partner(): return lax.ppermute(array, 'dir', [(i, i ^ mask) for i in range(dir_count)])  1.14 us
  transfers between devices with their start and end apart: 14, of which 1 were waited for; matrix products, arithmetic and copies ran while one was open for 0% of the time, Pallas kernels for 58%

profile of v8, /device:TPU:0, one launch (start us, length us, event | category | flops | bytes accessed | tf_op | source)
XLA Modules:
  0.0 49.6 jit_solution(11685135719939648595)
XLA Ops:
  0.0 0.5 collective-permute-start.3
  0.5 1.3 %collective-permute-start.2 = (bf16[6,128,256]{2,1,0:T(8,128)(2,1)}, bf16[6,128,256]{2,1,0:T(8,128)(2,1)S(1)}, u32[]{:S(2)}, u32[]{:S(2)}) collective-permute-start(bf16[6,128,256]{2,1,0:T(8,128)(2,1)} %bitcast.2), channel_id=1, source_target_pairs={{1,0},{2,1},{3,2},{5,4},{6,5},{7,6},{9,8},{10,9},{11,10},{13,12},{... | collective-permute-start | bytes 1179656 | tf_op jit(solution)/shard_map/ppermute | solution.py:350
  1.7 4.8 %collective-permute-start.1 = (bf16[6,128,256]{2,1,0:T(8,128)(2,1)}, bf16[6,128,256]{2,1,0:T(8,128)(2,1)S(1)}, u32[]{:S(2)}, u32[]{:S(2)}) collective-permute-start(bf16[6,128,256]{2,1,0:T(8,128)(2,1)} %bitcast.3), channel_id=1, source_target_pairs={{0,16},{4,20},{8,24},{12,28},{16,0},{20,4},{24,8},{28,12},{1,17},{... | collective-permute-start | bytes 1179656 | tf_op jit(solution)/shard_map/ppermute | solution.py:340
  6.5 1.5 %collective-permute-start = (bf16[6,128,256]{2,1,0:T(8,128)(2,1)}, bf16[6,128,256]{2,1,0:T(8,128)(2,1)S(1)}, u32[]{:S(2)}, u32[]{:S(2)}) collective-permute-start(bf16[6,128,256]{2,1,0:T(8,128)(2,1)} %bitcast.4), channel_id=1, source_target_pairs={{0,8},{4,12},{8,0},{12,4},{16,24},{20,28},{24,16},{28,20},{1,9},{5... | collective-permute-start | bytes 1179656 | tf_op jit(solution)/shard_map/ppermute | solution.py:340
  8.0 0.0 collective-permute-start.4
  8.0 11.3 %shard_map.91 = (bf16[99,128,128]{2,1,0:T(8,128)(2,1)S(1)}, bf16[128,1536]{1,0:T(8,128)(2,1)S(1)}, bf16[1536,128]{1,0:T(8,128)(2,1)S(1)}, f32[316,1536]{1,0:T(8,...) custom-call(s32[9]{0:T(128)} %off_hbm.1, s32[1,48,48]{2,1,0:T(8,128)} %src_hbm.1, s32[1,48,48]{2,1,0:T(8,128)} %tid_hbm.1, ...), custom_call_target="tpu_custom_call" | custom-call | flops 7952400384 | bytes 1048576 | tf_op jit(solution)/shard_map/pallas_call | solution.py:376
  19.3 0.0 collective-permute-done.2.rest_3_
  19.3 0.0 collective-permute-done.1.rest_2_
  19.4 0.0 collective-permute-done.rest_1_
  19.4 0.0 collective-permute-done.4.near_src_other_ref
  19.4 0.0 collective-permute-done.3.near_other_hbm
  19.4 0.6 %collective-permute-start.5 = (bf16[99,128,128]{2,1,0:T(8,128)(2,1)S(1)}, bf16[99,128,128]{2,1,0:T(8,128)(2,1)S(1)}, u32[]{:S(2)}, u32[]{:S(2)}) collective-permute-start(bf16[99,128,128]{2,1,0:T(8,128)(2,1)S(1)} %get-tuple-element.40.low_ref), channel_id=1, source_target_pairs={{0,4},{4,0},{8,12},{12,8},{16,20},{20,16},{24,28},{28,24},{1,5},{5... | collective-permute-start | bytes 9732104 | tf_op jit(solution)/shard_map/ppermute | solution.py:340
  19.9 1.3 %collective-permute-start.7 = (bf16[6,128,256]{2,1,0:T(8,128)(2,1)S(1)}, bf16[6,128,256]{2,1,0:T(8,128)(2,1)S(1)}, u32[]{:S(2)}, u32[]{:S(2)}) collective-permute-start(bf16[6,128,256]{2,1,0:T(8,128)(2,1)S(1)} %collective-permute-done.rest_1_), channel_id=1, source_target_pairs={{1,0},{2,1},{3,2},{5,4},{6,5},{7,6},{9,8},{10,9},{11,10},{13,12},{... | collective-permute-start | bytes 1179656 | tf_op jit(solution)/shard_map/ppermute | solution.py:350
  21.2 1.2 %collective-permute-start.6 = (bf16[6,128,256]{2,1,0:T(8,128)(2,1)S(1)}, bf16[6,128,256]{2,1,0:T(8,128)(2,1)S(1)}, u32[]{:S(2)}, u32[]{:S(2)}) collective-permute-start(bf16[6,128,256]{2,1,0:T(8,128)(2,1)S(1)} %collective-permute-done.1.rest_2_), channel_id=1, source_target_pairs={{0,8},{4,12},{8,0},{12,4},{16,24},{20,28},{24,16},{28,20},{1,9},{5... | collective-permute-start | bytes 1179656 | tf_op jit(solution)/shard_map/ppermute | solution.py:340
  22.4 2.4 %collective-permute-start.8 = (bf16[6,128,256]{2,1,0:T(8,128)(2,1)S(1)}, bf16[6,128,256]{2,1,0:T(8,128)(2,1)S(1)}, u32[]{:S(2)}, u32[]{:S(2)}) collective-permute-start(bf16[6,128,256]{2,1,0:T(8,128)(2,1)S(1)} %collective-permute-done.2.rest_3_), channel_id=1, source_target_pairs={{0,16},{4,20},{8,24},{12,28},{16,0},{20,4},{24,8},{28,12},{1,17},{... | collective-permute-start | bytes 1179656 | tf_op jit(solution)/shard_map/ppermute | solution.py:340
  24.8 9.7 %shard_map.92 = (bf16[318,128,128]{2,1,0:T(8,128)(2,1)S(1)}, bf16[12,28,128,128]{3,2,1,0:T(8,128)(2,1)S(1)}, s32[16,128]{1,0:T(8,128)S(1)}) custom-call(s32[8,384]{1,0:T(8,128)S(1)} %get-tuple-element.32.list_ref, f32[316,1536]{1,0:T(8,128)S(1)} %get-tuple-element.33.rows_ref, bf16[128,1536]{1,0:T(8,128)(2,1)S(1)} %get-tuple-element.34.weighted_ref, ...), custom_call_target="tpu_custom_call" | custom-call | flops 7952400384 | bytes 1048576 | tf_op jit(solution)/shard_map/pallas_call | solution.py:413
  34.5 0.0 collective-permute-done.7.rest_5_.rest_1_
  34.5 0.0 collective-permute-done.6.rest_4_.rest_0_
  34.6 0.0 collective-permute-done.8.rest_6_.rest_2_
  34.6 1.4 %collective-permute-start.9 = (bf16[3,128,256]{2,1,0:T(8,128)(2,1)S(1)}, bf16[3,128,256]{2,1,0:T(8,128)(2,1)S(1)}, u32[]{:S(2)}, u32[]{:S(2)}) collective-permute-start(bf16[3,128,256]{2,1,0:T(8,128)(2,1)S(1)} %slice.6), channel_id=1, source_target_pairs={{0,8},{4,12},{8,0},{12,4},{16,24},{20,28},{24,16},{28,20},{1,9},{5... | collective-permute-start | bytes 589832 | tf_op jit(solution)/shard_map/ppermute | solution.py:340
  36.1 1.3 %collective-permute-start.10 = (bf16[3,128,256]{2,1,0:T(8,128)(2,1)S(1)}, bf16[3,128,256]{2,1,0:T(8,128)(2,1)S(1)}, u32[]{:S(2)}, u32[]{:S(2)}) collective-permute-start(bf16[3,128,256]{2,1,0:T(8,128)(2,1)S(1)} %slice.7), channel_id=1, source_target_pairs={{0,16},{4,20},{8,24},{12,28},{16,0},{20,4},{24,8},{28,12},{1,17},{... | collective-permute-start | bytes 589832 | tf_op jit(solution)/shard_map/ppermute | solution.py:340
  37.3 0.0 collective-permute-done.5.low_ref
  37.3 5.5 %shard_map.93 = (bf16[318,128,128]{2,1,0:T(8,128)(2,1)S(1)}, bf16[6,128,256]{2,1,0:T(8,128)(2,1)S(1)}, f32[6,128,256]{2,1,0:T(8,128)S(1)}) custom-call(s32[8,384]{1,0:T(8,128)S(1)} %get-tuple-element.32.list_ref, s32[16,128]{1,0:T(8,128)S(1)} %get-tuple-element.31.cls_ref, ...), custom_call_target="tpu_custom_call", output_to_operand_aliasing={{0}: (15, {})} | custom-call | flops 1048576 | bytes 1048576 | tf_op jit(solution)/shard_map/pallas_call | solution.py:472
  42.8 0.1 collective-permute-start.13
  42.9 0.0 collective-permute-done.9.rest_0_
  42.9 0.0 collective-permute-done.10.rest_1_
  42.9 0.5 collective-permute-start.11
  43.4 0.1 collective-permute-start.12
  43.5 1.1 %collective-permute-done.13.rest_4_ = bf16[6,128,256]{2,1,0:T(8,128)(2,1)S(1)} collective-permute-done((bf16[6,128,256]{2,1,0:T(8,128)(2,1)S(1)}, bf16[6,128,256]{2,1,0:T(8,128)(2,1)S(1)}, u32[]{:S(2)}, u32[]{:S(2)}) %collective-permute-start.13) | collective-permute-done | bytes 393248 | tf_op jit(solution)/shard_map/ppermute | solution.py:340
  44.6 2.2 %shard_map.94.rest_4_ = f32[6,128,256]{2,1,0:T(8,128)S(1)} custom-call(s32[16,128]{1,0:T(8,128)S(1)} %get-tuple-element.31.cls_ref, s32[16,128]{1,0:T(8,128)S(1)} %get-tuple-element.41.near_map_ref, s32[8,384]{1,0:T(8,128)S(1)} %get-tuple-element.32.list_ref, bf16[318,128,128]{2,1,0:T(8,128)(2,1)S(1)} %get-tuple-element.51.t_ref, ...), custom_call_target="tpu_custom_call" | custom-call | flops 1048576 | bytes 1048576 | tf_op jit(solution)/shard_map/pallas_call | solution.py:448
  46.9 0.0 collective-permute-done.11.rest_2_
  46.9 2.7 %shard_map.95 = bf16[1,6,128,256]{3,2,1,0:T(8,128)(2,1)} custom-call(s32[16,128]{1,0:T(8,128)S(1)} %get-tuple-element.31.cls_ref, s32[16,128]{1,0:T(8,128)S(1)} %get-tuple-element.41.near_map_ref, s32[8,384]{1,0:T(8,128)S(1)} %get-tuple-element.32.list_ref, bf16[318,128,128]{2,1,0:T(8,128)(2,1)S(1)} %get-tuple-element.51.t_ref, ...), custom_call_target="tpu_custom_call" | custom-call | flops 1048576 | bytes 1048576 | tf_op jit(solution)/shard_map/pallas_call | solution.py:448
  (7 shorter events, 0.0 us)
Async XLA Ops:
  0.0 19.4 %collective-permute-start.3 = (bf16[1,6,27,128,128]{4,3,2,1,0:T(8,128)(2,1)}, bf16[1,6,27,128,128]{4,3,2,1,0:T(8,128)(2,1)S(1)}, u32[]{:S(2)}, u32[]{:S(2)}) collective-permute-start(bf16[1,6,27,128,128]{4,3,2,1,0:T(8,128)(2,1)} %near_hbm.1), channel_id=1, source_target_pairs={{0,4},{4,0},{8,12},{12,8},{16,20},{20,16},{24,28},{28,24},{1,5},{5... | collective-permute-start | bytes 15925256 | tf_op jit(solution)/shard_map/ppermute | solution.py:340
  0.5 18.9 %collective-permute-start.2 = (bf16[6,128,256]{2,1,0:T(8,128)(2,1)}, bf16[6,128,256]{2,1,0:T(8,128)(2,1)S(1)}, u32[]{:S(2)}, u32[]{:S(2)}) collective-permute-start(bf16[6,128,256]{2,1,0:T(8,128)(2,1)} %bitcast.2), channel_id=1, source_target_pairs={{1,0},{2,1},{3,2},{5,4},{6,5},{7,6},{9,8},{10,9},{11,10},{13,12},{... | collective-permute-start | bytes 1179656 | tf_op jit(solution)/shard_map/ppermute | solution.py:350
  1.7 17.6 %collective-permute-start.1 = (bf16[6,128,256]{2,1,0:T(8,128)(2,1)}, bf16[6,128,256]{2,1,0:T(8,128)(2,1)S(1)}, u32[]{:S(2)}, u32[]{:S(2)}) collective-permute-start(bf16[6,128,256]{2,1,0:T(8,128)(2,1)} %bitcast.3), channel_id=1, source_target_pairs={{0,16},{4,20},{8,24},{12,28},{16,0},{20,4},{24,8},{28,12},{1,17},{... | collective-permute-start | bytes 1179656 | tf_op jit(solution)/shard_map/ppermute | solution.py:340
  6.5 12.8 %collective-permute-start = (bf16[6,128,256]{2,1,0:T(8,128)(2,1)}, bf16[6,128,256]{2,1,0:T(8,128)(2,1)S(1)}, u32[]{:S(2)}, u32[]{:S(2)}) collective-permute-start(bf16[6,128,256]{2,1,0:T(8,128)(2,1)} %bitcast.4), channel_id=1, source_target_pairs={{0,8},{4,12},{8,0},{12,4},{16,24},{20,28},{24,16},{28,20},{1,9},{5... | collective-permute-start | bytes 1179656 | tf_op jit(solution)/shard_map/ppermute | solution.py:340
  8.0 16.8 %copy-start.1 = (s32[1,6,27]{2,0,1:T(1,128)S(1)}, s32[1,6,27]{2,0,1:T(1,128)}, u32[]{:S(2)}) copy-start(s32[1,6,27]{2,0,1:T(1,128)} %param.17) | copy-start | bytes 1948
  8.0 11.3 %collective-permute-start.4 = (s32[6,1,27]{2,1,0:T(1,128)}, s32[6,1,27]{2,1,0:T(1,128)S(1)}, u32[]{:S(2)}, u32[]{:S(2)}) collective-permute-start(s32[6,1,27]{2,1,0:T(1,128)} %bitcast.6), channel_id=1, source_target_pairs={{0,4},{4,0},{8,12},{12,8},{16,20},{20,16},{24,28},{28,24},{1,5},{5... | collective-permute-start | bytes 1952 | tf_op jit(solution)/shard_map/ppermute | solution.py:340
  19.4 17.9 %collective-permute-start.5 = (bf16[99,128,128]{2,1,0:T(8,128)(2,1)S(1)}, bf16[99,128,128]{2,1,0:T(8,128)(2,1)S(1)}, u32[]{:S(2)}, u32[]{:S(2)}) collective-permute-start(bf16[99,128,128]{2,1,0:T(8,128)(2,1)S(1)} %get-tuple-element.40.low_ref), channel_id=1, source_target_pairs={{0,4},{4,0},{8,12},{12,8},{16,20},{20,16},{24,28},{28,24},{1,5},{5... | collective-permute-start | bytes 9732104 | tf_op jit(solution)/shard_map/ppermute | solution.py:340
  19.9 14.6 %collective-permute-start.7 = (bf16[6,128,256]{2,1,0:T(8,128)(2,1)S(1)}, bf16[6,128,256]{2,1,0:T(8,128)(2,1)S(1)}, u32[]{:S(2)}, u32[]{:S(2)}) collective-permute-start(bf16[6,128,256]{2,1,0:T(8,128)(2,1)S(1)} %collective-permute-done.rest_1_), channel_id=1, source_target_pairs={{1,0},{2,1},{3,2},{5,4},{6,5},{7,6},{9,8},{10,9},{11,10},{13,12},{... | collective-permute-start | bytes 1179656 | tf_op jit(solution)/shard_map/ppermute | solution.py:350
  21.2 13.3 %collective-permute-start.6 = (bf16[6,128,256]{2,1,0:T(8,128)(2,1)S(1)}, bf16[6,128,256]{2,1,0:T(8,128)(2,1)S(1)}, u32[]{:S(2)}, u32[]{:S(2)}) collective-permute-start(bf16[6,128,256]{2,1,0:T(8,128)(2,1)S(1)} %collective-permute-done.1.rest_2_), channel_id=1, source_target_pairs={{0,8},{4,12},{8,0},{12,4},{16,24},{20,28},{24,16},{28,20},{1,9},{5... | collective-permute-start | bytes 1179656 | tf_op jit(solution)/shard_map/ppermute | solution.py:340
  22.4 12.2 %collective-permute-start.8 = (bf16[6,128,256]{2,1,0:T(8,128)(2,1)S(1)}, bf16[6,128,256]{2,1,0:T(8,128)(2,1)S(1)}, u32[]{:S(2)}, u32[]{:S(2)}) collective-permute-start(bf16[6,128,256]{2,1,0:T(8,128)(2,1)S(1)} %collective-permute-done.2.rest_3_), channel_id=1, source_target_pairs={{0,16},{4,20},{8,24},{12,28},{16,0},{20,4},{24,8},{28,12},{1,17},{... | collective-permute-start | bytes 1179656 | tf_op jit(solution)/shard_map/ppermute | solution.py:340
  24.8 12.5 %copy-start = (bf16[1,6,128,256]{3,2,1,0:T(8,128)(2,1)S(1)}, bf16[1,6,128,256]{3,2,1,0:T(8,128)(2,1)}, u32[]{:S(2)}) copy-start(bf16[1,6,128,256]{3,2,1,0:T(8,128)(2,1)} %param.9) | copy-start | bytes 1179652
  34.6 8.3 %collective-permute-start.9 = (bf16[3,128,256]{2,1,0:T(8,128)(2,1)S(1)}, bf16[3,128,256]{2,1,0:T(8,128)(2,1)S(1)}, u32[]{:S(2)}, u32[]{:S(2)}) collective-permute-start(bf16[3,128,256]{2,1,0:T(8,128)(2,1)S(1)} %slice.6), channel_id=1, source_target_pairs={{0,8},{4,12},{8,0},{12,4},{16,24},{20,28},{24,16},{28,20},{1,9},{5... | collective-permute-start | bytes 589832 | tf_op jit(solution)/shard_map/ppermute | solution.py:340
  36.1 6.9 %collective-permute-start.10 = (bf16[3,128,256]{2,1,0:T(8,128)(2,1)S(1)}, bf16[3,128,256]{2,1,0:T(8,128)(2,1)S(1)}, u32[]{:S(2)}, u32[]{:S(2)}) collective-permute-start(bf16[3,128,256]{2,1,0:T(8,128)(2,1)S(1)} %slice.7), channel_id=1, source_target_pairs={{0,16},{4,20},{8,24},{12,28},{16,0},{20,4},{24,8},{28,12},{1,17},{... | collective-permute-start | bytes 589832 | tf_op jit(solution)/shard_map/ppermute | solution.py:340
  42.8 1.8 %collective-permute-start.13 = (bf16[6,128,256]{2,1,0:T(8,128)(2,1)S(1)}, bf16[6,128,256]{2,1,0:T(8,128)(2,1)S(1)}, u32[]{:S(2)}, u32[]{:S(2)}) collective-permute-start(bf16[6,128,256]{2,1,0:T(8,128)(2,1)S(1)} %get-tuple-element.56), channel_id=1, source_target_pairs={{0,4},{4,0},{8,12},{12,8},{16,20},{20,16},{24,28},{28,24},{1,5},{5... | collective-permute-start | bytes 1179656 | tf_op jit(solution)/shard_map/ppermute | solution.py:340
  42.9 3.9 %collective-permute-start.11 = (bf16[3,128,256]{2,1,0:T(8,128)(2,1)S(1)}, bf16[3,128,256]{2,1,0:T(8,128)(2,1)S(1)}, u32[]{:S(2)}, u32[]{:S(2)}) collective-permute-start(bf16[3,128,256]{2,1,0:T(8,128)(2,1)S(1)} %collective-permute-done.9.rest_0_), channel_id=1, source_target_pairs={{0,4},{4,0},{8,12},{12,8},{16,20},{20,16},{24,28},{28,24},{1,5},{5... | collective-permute-start | bytes 589832 | tf_op jit(solution)/shard_map/ppermute | solution.py:340
  43.4 3.5 %collective-permute-start.12 = (bf16[3,128,256]{2,1,0:T(8,128)(2,1)S(1)}, bf16[3,128,256]{2,1,0:T(8,128)(2,1)S(1)}, u32[]{:S(2)}, u32[]{:S(2)}) collective-permute-start(bf16[3,128,256]{2,1,0:T(8,128)(2,1)S(1)} %collective-permute-done.10.rest_1_), channel_id=1, source_target_pairs={{0,4},{4,0},{8,12},{12,8},{16,20},{20,16},{24,28},{28,24},{1,5},{5... | collective-permute-start | bytes 589832 | tf_op jit(solution)/shard_map/ppermute | solution.py:340

commit v9 on v8

--- a/solution.py
+++ b/solution.py
@@ -100,7 +100,6 @@
     row_at = lax.broadcasted_iota(I32, (ROWS, slots), 0)
     out_row = lax.broadcasted_iota(I32, cls_ref.shape, 0)
     seen = jnp.zeros((used_width, slots), F32)
-    seen_by_chip = seen
     cls = jnp.full(cls_ref.shape, classes, I32)
     copies[0].wait()
     copies[1].wait()
@@ -113,8 +112,7 @@
         late = beyond & ((mask & top) != 0) & ((mask & (top - 2)) != 0)
         even = (mask & 1) == 0
         here = (src >= 0) & ((even | late) if j < boxes else (even & ~late))
-        seen = jnp.where((class_at == tid) & here, 1.0, seen)
-        seen_by_chip = jnp.where((class_at == tid) & (src >= 0), 1.0, seen_by_chip)
+        seen = jnp.maximum(seen, jnp.where(class_at == tid, jnp.where(here, 2.0, jnp.where(src >= 0, 1.0, 0.0)), 0.0))
         parts = jnp.where(row_at == 0, tid // 16, jnp.where(row_at == 1, tid % 16, 1))
         found = lookup(parts, jnp.where(ext_at == src, 1.0, 0.0))
         value = jnp.where(found[2:3] > 0, found[0:1] * 16 + found[1:2], classes)
@@ -123,8 +121,8 @@
     lane = lax.broadcasted_iota(I32, (ROWS, used_width), 1)
     list_row = lax.broadcasted_iota(I32, (ROWS, used_width), 0)
     ones = jnp.ones((ROWS, slots), I32)
-    by_chip = jnp.where(lane < shared, jnp.minimum(lookup(ones, seen_by_chip), 1), 0)
-    by_core = jnp.where(lane >= shared, jnp.minimum(lookup(ones, seen), 1), 0)
+    by_chip = jnp.where(lane < shared, jnp.minimum(lookup(ones, jnp.where(seen > 0.0, 1.0, 0.0)), 1), 0)
+    by_core = jnp.where(lane >= shared, jnp.minimum(lookup(ones, jnp.where(seen > 1.0, 1.0, 0.0)), 1), 0)
     is_used = jnp.where(list_row == 0, by_chip, by_core)
     down = lax.broadcasted_iota(I32, (used_width, used_width), 0)
     across = lax.broadcasted_iota(I32, (used_width, used_width), 1)
@@ -330,7 +328,7 @@
     shared = classes * 5 // 8
     capacity = (shared + 1) // 2
     empty = capacity + classes - shared
-    second_end = capacity + pad_to(classes // 5, UNROLL)
+    second_end = capacity + pad_to(classes // 8, UNROLL)
     top = dir_count // 2
     inner = range(2, top, 2)
     split = boxes // 2
@@ -496,10 +494,10 @@
 
     total, last = lax.optimization_barrier((total, last))
     turned = {m: [partner(part, 1) for part in last[m]] for m in inner}
-    total = apply((early + middle)[count:], 0, total, from_other, F32, full)
+    total = apply((early + middle)[count:], 0, total, None, F32, full)
     late = [(True, top + m, last[m]) for m in inner]
     late += [(True, top + m + 1, turned[m]) for m in inner]
-    return apply(late, 0, total, None, BF16, currents.shape)
+    return apply(late, 0, total, from_other, BF16, currents.shape)
 
 
 def solution(mesh):

time: 49.7 us -> 49.7 us (level)
    pallas_call x1, Pallas kernels: 9.73 us -> 8.03 us  [shards(): pl.pallas_call(functools.partial(second_kernel, second_end, empty, halo -...]
    pallas_call x1, Pallas kernels: 5.51 us -> 7.2 us  [shards(): pl.pallas_call(functools.partial(third_kernel, second_end, empty, [(outsi...]
    ppermute x12, waiting for transfers between devices: 1.14 us -> 0.03 us  [partner(): return lax.ppermute(array, 'dir', [(i, i ^ mask) for i in range(dir_count)])]
    ppermute x2, waiting for transfers between devices: 0.01 us -> 1.11 us  [beyond(): return lax.ppermute(array, ('dir', 'region'), along)]
where the time goes in v9:
time: 49.7 us; the launch traced here: 49.3 us
  Pallas kernels  31.1 us (63%)
  starting transfers between devices  16.8 us (34%)
  waiting for transfers between devices  1.15 us (2%)
    ppermute x12, starting transfers between devices, partner(): return lax.ppermute(array, 'dir', [(i, i ^ mask) for i in range(dir_count)])  14.3 us
    pallas_call x1, Pallas kernels, shards(): pl.pallas_call(functools.partial(first_kernel, shared, boxes, halo, regio...  10.9 us
    pallas_call x1, Pallas kernels, shards(): pl.pallas_call(functools.partial(second_kernel, second_end, empty, halo -...  8.03 us
    pallas_call x1, Pallas kernels, shards(): pl.pallas_call(functools.partial(third_kernel, second_end, empty, [(outsi...  7.2 us
    pallas_call x2, Pallas kernels, apply(): pl.pallas_call(kernel, in_specs=specs, out_specs=vmem, out_shape=pltpu.VM...  4.92 us
    ppermute x2, starting transfers between devices, beyond(): return lax.ppermute(array, ('dir', 'region'), along)  2.57 us
    ppermute x2, waiting for transfers between devices, beyond(): return lax.ppermute(array, ('dir', 'region'), along)  1.11 us
  transfers between devices with their start and end apart: 14, of which 1 were waited for; matrix products, arithmetic and copies ran while one was open for 0% of the time, Pallas kernels for 58%

profile of v9, /device:TPU:0, one launch (start us, length us, event | category | flops | bytes accessed | tf_op | source)
XLA Modules:
  0.0 49.3 jit_solution(18096813488685373906)
XLA Ops:
  0.0 0.5 collective-permute-start.3
  0.5 1.3 %collective-permute-start.2 = (bf16[6,128,256]{2,1,0:T(8,128)(2,1)}, bf16[6,128,256]{2,1,0:T(8,128)(2,1)S(1)}, u32[]{:S(2)}, u32[]{:S(2)}) collective-permute-start(bf16[6,128,256]{2,1,0:T(8,128)(2,1)} %bitcast.2), channel_id=1, source_target_pairs={{1,0},{2,1},{3,2},{5,4},{6,5},{7,6},{9,8},{10,9},{11,10},{13,12},{... | collective-permute-start | bytes 1179656 | tf_op jit(solution)/shard_map/ppermute | solution.py:348
  1.7 4.8 %collective-permute-start.1 = (bf16[6,128,256]{2,1,0:T(8,128)(2,1)}, bf16[6,128,256]{2,1,0:T(8,128)(2,1)S(1)}, u32[]{:S(2)}, u32[]{:S(2)}) collective-permute-start(bf16[6,128,256]{2,1,0:T(8,128)(2,1)} %bitcast.3), channel_id=1, source_target_pairs={{0,16},{4,20},{8,24},{12,28},{16,0},{20,4},{24,8},{28,12},{1,17},{... | collective-permute-start | bytes 1179656 | tf_op jit(solution)/shard_map/ppermute | solution.py:338
  6.5 1.5 %collective-permute-start = (bf16[6,128,256]{2,1,0:T(8,128)(2,1)}, bf16[6,128,256]{2,1,0:T(8,128)(2,1)S(1)}, u32[]{:S(2)}, u32[]{:S(2)}) collective-permute-start(bf16[6,128,256]{2,1,0:T(8,128)(2,1)} %bitcast.4), channel_id=1, source_target_pairs={{0,8},{4,12},{8,0},{12,4},{16,24},{20,28},{24,16},{28,20},{1,9},{5... | collective-permute-start | bytes 1179656 | tf_op jit(solution)/shard_map/ppermute | solution.py:338
  8.0 0.0 collective-permute-start.4
  8.0 10.9 %shard_map.91 = (bf16[99,128,128]{2,1,0:T(8,128)(2,1)S(1)}, bf16[128,1536]{1,0:T(8,128)(2,1)S(1)}, bf16[1536,128]{1,0:T(8,128)(2,1)S(1)}, f32[316,1536]{1,0:T(8,...) custom-call(s32[9]{0:T(128)} %off_hbm.1, s32[1,48,48]{2,1,0:T(8,128)} %src_hbm.1, s32[1,48,48]{2,1,0:T(8,128)} %tid_hbm.1, ...), custom_call_target="tpu_custom_call" | custom-call | flops 7952400384 | bytes 1048576 | tf_op jit(solution)/shard_map/pallas_call | solution.py:374
  19.0 0.0 collective-permute-done.2.rest_3_
  19.0 0.0 collective-permute-done.1.rest_2_
  19.0 0.0 collective-permute-done.rest_1_
  19.0 0.0 collective-permute-done.4.near_src_other_ref
  19.0 0.0 collective-permute-done.3.near_other_hbm
  19.0 0.1 collective-permute-start.5
  19.1 1.3 %collective-permute-start.7 = (bf16[6,128,256]{2,1,0:T(8,128)(2,1)S(1)}, bf16[6,128,256]{2,1,0:T(8,128)(2,1)S(1)}, u32[]{:S(2)}, u32[]{:S(2)}) collective-permute-start(bf16[6,128,256]{2,1,0:T(8,128)(2,1)S(1)} %collective-permute-done.rest_1_), channel_id=1, source_target_pairs={{1,0},{2,1},{3,2},{5,4},{6,5},{7,6},{9,8},{10,9},{11,10},{13,12},{... | collective-permute-start | bytes 1179656 | tf_op jit(solution)/shard_map/ppermute | solution.py:348
  20.4 1.6 %collective-permute-start.6 = (bf16[6,128,256]{2,1,0:T(8,128)(2,1)S(1)}, bf16[6,128,256]{2,1,0:T(8,128)(2,1)S(1)}, u32[]{:S(2)}, u32[]{:S(2)}) collective-permute-start(bf16[6,128,256]{2,1,0:T(8,128)(2,1)S(1)} %collective-permute-done.1.rest_2_), channel_id=1, source_target_pairs={{0,8},{4,12},{8,0},{12,4},{16,24},{20,28},{24,16},{28,20},{1,9},{5... | collective-permute-start | bytes 1179656 | tf_op jit(solution)/shard_map/ppermute | solution.py:338
  22.0 2.3 %collective-permute-start.8 = (bf16[6,128,256]{2,1,0:T(8,128)(2,1)S(1)}, bf16[6,128,256]{2,1,0:T(8,128)(2,1)S(1)}, u32[]{:S(2)}, u32[]{:S(2)}) collective-permute-start(bf16[6,128,256]{2,1,0:T(8,128)(2,1)S(1)} %collective-permute-done.2.rest_3_), channel_id=1, source_target_pairs={{0,16},{4,20},{8,24},{12,28},{16,0},{20,4},{24,8},{28,12},{1,17},{... | collective-permute-start | bytes 1179656 | tf_op jit(solution)/shard_map/ppermute | solution.py:338
  24.3 8.0 %shard_map.92 = (bf16[318,128,128]{2,1,0:T(8,128)(2,1)S(1)}, bf16[12,28,128,128]{3,2,1,0:T(8,128)(2,1)S(1)}, s32[16,128]{1,0:T(8,128)S(1)}) custom-call(s32[8,384]{1,0:T(8,128)S(1)} %get-tuple-element.32.list_ref, f32[316,1536]{1,0:T(8,128)S(1)} %get-tuple-element.33.rows_ref, bf16[128,1536]{1,0:T(8,128)(2,1)S(1)} %get-tuple-element.34.weighted_ref, ...), custom_call_target="tpu_custom_call" | custom-call | flops 7952400384 | bytes 1048576 | tf_op jit(solution)/shard_map/pallas_call | solution.py:411
  32.4 1.1 %collective-permute-done.7.rest_5_.rest_1_ = bf16[6,128,256]{2,1,0:T(8,128)(2,1)S(1)} collective-permute-done((bf16[6,128,256]{2,1,0:T(8,128)(2,1)S(1)}, bf16[6,128,256]{2,1,0:T(8,128)(2,1)S(1)}, u32[]{:S(2)}, u32[]{:S(2)}) %collective-permute-start.7) | collective-permute-done | bytes 393248 | tf_op jit(solution)/shard_map/ppermute | solution.py:348
  33.5 0.0 collective-permute-done.6.rest_4_.rest_0_
  33.5 0.0 collective-permute-done.8.rest_6_.rest_2_
  33.5 1.1 %collective-permute-start.9 = (bf16[3,128,256]{2,1,0:T(8,128)(2,1)S(1)}, bf16[3,128,256]{2,1,0:T(8,128)(2,1)S(1)}, u32[]{:S(2)}, u32[]{:S(2)}) collective-permute-start(bf16[3,128,256]{2,1,0:T(8,128)(2,1)S(1)} %slice.6), channel_id=1, source_target_pairs={{0,8},{4,12},{8,0},{12,4},{16,24},{20,28},{24,16},{28,20},{1,9},{5... | collective-permute-start | bytes 589832 | tf_op jit(solution)/shard_map/ppermute | solution.py:338
  34.7 1.7 %collective-permute-start.10 = (bf16[3,128,256]{2,1,0:T(8,128)(2,1)S(1)}, bf16[3,128,256]{2,1,0:T(8,128)(2,1)S(1)}, u32[]{:S(2)}, u32[]{:S(2)}) collective-permute-start(bf16[3,128,256]{2,1,0:T(8,128)(2,1)S(1)} %slice.7), channel_id=1, source_target_pairs={{0,16},{4,20},{8,24},{12,28},{16,0},{20,4},{24,8},{28,12},{1,17},{... | collective-permute-start | bytes 589832 | tf_op jit(solution)/shard_map/ppermute | solution.py:338
  36.4 0.0 collective-permute-done.5.low_ref
  36.4 7.2 %shard_map.93 = (bf16[318,128,128]{2,1,0:T(8,128)(2,1)S(1)}, bf16[6,128,256]{2,1,0:T(8,128)(2,1)S(1)}, f32[6,128,256]{2,1,0:T(8,128)S(1)}) custom-call(s32[8,384]{1,0:T(8,128)S(1)} %get-tuple-element.32.list_ref, s32[16,128]{1,0:T(8,128)S(1)} %get-tuple-element.31.cls_ref, ...), custom_call_target="tpu_custom_call", output_to_operand_aliasing={{0}: (15, {})} | custom-call | flops 1048576 | bytes 1048576 | tf_op jit(solution)/shard_map/pallas_call | solution.py:470
  43.6 0.1 collective-permute-start.13
  43.7 0.0 collective-permute-done.9.rest_0_
  43.7 0.0 collective-permute-done.10.rest_1_
  43.7 0.5 collective-permute-start.11
  44.2 0.1 collective-permute-start.12
  44.3 2.3 %shard_map.94.rest_4_ = f32[6,128,256]{2,1,0:T(8,128)S(1)} custom-call(s32[16,128]{1,0:T(8,128)S(1)} %get-tuple-element.31.cls_ref, s32[16,128]{1,0:T(8,128)S(1)} %get-tuple-element.41.near_map_ref, s32[8,384]{1,0:T(8,128)S(1)} %get-tuple-element.32.list_ref, bf16[318,128,128]{2,1,0:T(8,128)(2,1)S(1)} %get-tuple-element.51.t_ref, ...), custom_call_target="tpu_custom_call" | custom-call | flops 1048576 | bytes 1048576 | tf_op jit(solution)/shard_map/pallas_call | solution.py:446
  46.6 0.0 collective-permute-done.11.rest_2_
  46.6 0.0 collective-permute-done.12.rest_3_
  46.6 2.7 %shard_map.95 = bf16[1,6,128,256]{3,2,1,0:T(8,128)(2,1)} custom-call(s32[16,128]{1,0:T(8,128)S(1)} %get-tuple-element.31.cls_ref, s32[16,128]{1,0:T(8,128)S(1)} %get-tuple-element.41.near_map_ref, s32[8,384]{1,0:T(8,128)S(1)} %get-tuple-element.32.list_ref, bf16[318,128,128]{2,1,0:T(8,128)(2,1)S(1)} %get-tuple-element.51.t_ref, ...), custom_call_target="tpu_custom_call" | custom-call | flops 1048576 | bytes 1048576 | tf_op jit(solution)/shard_map/pallas_call | solution.py:446
  (7 shorter events, 0.0 us)
Async XLA Ops:
  0.0 19.0 %collective-permute-start.3 = (bf16[1,6,27,128,128]{4,3,2,1,0:T(8,128)(2,1)}, bf16[1,6,27,128,128]{4,3,2,1,0:T(8,128)(2,1)S(1)}, u32[]{:S(2)}, u32[]{:S(2)}) collective-permute-start(bf16[1,6,27,128,128]{4,3,2,1,0:T(8,128)(2,1)} %near_hbm.1), channel_id=1, source_target_pairs={{0,4},{4,0},{8,12},{12,8},{16,20},{20,16},{24,28},{28,24},{1,5},{5... | collective-permute-start | bytes 15925256 | tf_op jit(solution)/shard_map/ppermute | solution.py:338
  0.5 18.5 %collective-permute-start.2 = (bf16[6,128,256]{2,1,0:T(8,128)(2,1)}, bf16[6,128,256]{2,1,0:T(8,128)(2,1)S(1)}, u32[]{:S(2)}, u32[]{:S(2)}) collective-permute-start(bf16[6,128,256]{2,1,0:T(8,128)(2,1)} %bitcast.2), channel_id=1, source_target_pairs={{1,0},{2,1},{3,2},{5,4},{6,5},{7,6},{9,8},{10,9},{11,10},{13,12},{... | collective-permute-start | bytes 1179656 | tf_op jit(solution)/shard_map/ppermute | solution.py:348
  1.7 17.2 %collective-permute-start.1 = (bf16[6,128,256]{2,1,0:T(8,128)(2,1)}, bf16[6,128,256]{2,1,0:T(8,128)(2,1)S(1)}, u32[]{:S(2)}, u32[]{:S(2)}) collective-permute-start(bf16[6,128,256]{2,1,0:T(8,128)(2,1)} %bitcast.3), channel_id=1, source_target_pairs={{0,16},{4,20},{8,24},{12,28},{16,0},{20,4},{24,8},{28,12},{1,17},{... | collective-permute-start | bytes 1179656 | tf_op jit(solution)/shard_map/ppermute | solution.py:338
  6.5 12.5 %collective-permute-start = (bf16[6,128,256]{2,1,0:T(8,128)(2,1)}, bf16[6,128,256]{2,1,0:T(8,128)(2,1)S(1)}, u32[]{:S(2)}, u32[]{:S(2)}) collective-permute-start(bf16[6,128,256]{2,1,0:T(8,128)(2,1)} %bitcast.4), channel_id=1, source_target_pairs={{0,8},{4,12},{8,0},{12,4},{16,24},{20,28},{24,16},{28,20},{1,9},{5... | collective-permute-start | bytes 1179656 | tf_op jit(solution)/shard_map/ppermute | solution.py:338
  8.0 16.3 %copy-start.1 = (s32[1,6,27]{2,0,1:T(1,128)S(1)}, s32[1,6,27]{2,0,1:T(1,128)}, u32[]{:S(2)}) copy-start(s32[1,6,27]{2,0,1:T(1,128)} %param.17) | copy-start | bytes 1948
  8.0 11.0 %collective-permute-start.4 = (s32[6,1,27]{2,1,0:T(1,128)}, s32[6,1,27]{2,1,0:T(1,128)S(1)}, u32[]{:S(2)}, u32[]{:S(2)}) collective-permute-start(s32[6,1,27]{2,1,0:T(1,128)} %bitcast.6), channel_id=1, source_target_pairs={{0,4},{4,0},{8,12},{12,8},{16,20},{20,16},{24,28},{28,24},{1,5},{5... | collective-permute-start | bytes 1952 | tf_op jit(solution)/shard_map/ppermute | solution.py:338
  19.0 17.4 %collective-permute-start.5 = (bf16[99,128,128]{2,1,0:T(8,128)(2,1)S(1)}, bf16[99,128,128]{2,1,0:T(8,128)(2,1)S(1)}, u32[]{:S(2)}, u32[]{:S(2)}) collective-permute-start(bf16[99,128,128]{2,1,0:T(8,128)(2,1)S(1)} %get-tuple-element.40.low_ref), channel_id=1, source_target_pairs={{0,4},{4,0},{8,12},{12,8},{16,20},{20,16},{24,28},{28,24},{1,5},{5... | collective-permute-start | bytes 9732104 | tf_op jit(solution)/shard_map/ppermute | solution.py:338
  19.1 14.4 %collective-permute-start.7 = (bf16[6,128,256]{2,1,0:T(8,128)(2,1)S(1)}, bf16[6,128,256]{2,1,0:T(8,128)(2,1)S(1)}, u32[]{:S(2)}, u32[]{:S(2)}) collective-permute-start(bf16[6,128,256]{2,1,0:T(8,128)(2,1)S(1)} %collective-permute-done.rest_1_), channel_id=1, source_target_pairs={{1,0},{2,1},{3,2},{5,4},{6,5},{7,6},{9,8},{10,9},{11,10},{13,12},{... | collective-permute-start | bytes 1179656 | tf_op jit(solution)/shard_map/ppermute | solution.py:348
  20.4 13.1 %collective-permute-start.6 = (bf16[6,128,256]{2,1,0:T(8,128)(2,1)S(1)}, bf16[6,128,256]{2,1,0:T(8,128)(2,1)S(1)}, u32[]{:S(2)}, u32[]{:S(2)}) collective-permute-start(bf16[6,128,256]{2,1,0:T(8,128)(2,1)S(1)} %collective-permute-done.1.rest_2_), channel_id=1, source_target_pairs={{0,8},{4,12},{8,0},{12,4},{16,24},{20,28},{24,16},{28,20},{1,9},{5... | collective-permute-start | bytes 1179656 | tf_op jit(solution)/shard_map/ppermute | solution.py:338
  22.0 11.4 %collective-permute-start.8 = (bf16[6,128,256]{2,1,0:T(8,128)(2,1)S(1)}, bf16[6,128,256]{2,1,0:T(8,128)(2,1)S(1)}, u32[]{:S(2)}, u32[]{:S(2)}) collective-permute-start(bf16[6,128,256]{2,1,0:T(8,128)(2,1)S(1)} %collective-permute-done.2.rest_3_), channel_id=1, source_target_pairs={{0,16},{4,20},{8,24},{12,28},{16,0},{20,4},{24,8},{28,12},{1,17},{... | collective-permute-start | bytes 1179656 | tf_op jit(solution)/shard_map/ppermute | solution.py:338
  24.3 12.1 %copy-start = (bf16[1,6,128,256]{3,2,1,0:T(8,128)(2,1)S(1)}, bf16[1,6,128,256]{3,2,1,0:T(8,128)(2,1)}, u32[]{:S(2)}) copy-start(bf16[1,6,128,256]{3,2,1,0:T(8,128)(2,1)} %param.9) | copy-start | bytes 1179652
  33.5 10.2 %collective-permute-start.9 = (bf16[3,128,256]{2,1,0:T(8,128)(2,1)S(1)}, bf16[3,128,256]{2,1,0:T(8,128)(2,1)S(1)}, u32[]{:S(2)}, u32[]{:S(2)}) collective-permute-start(bf16[3,128,256]{2,1,0:T(8,128)(2,1)S(1)} %slice.6), channel_id=1, source_target_pairs={{0,8},{4,12},{8,0},{12,4},{16,24},{20,28},{24,16},{28,20},{1,9},{5... | collective-permute-start | bytes 589832 | tf_op jit(solution)/shard_map/ppermute | solution.py:338
  34.7 9.1 %collective-permute-start.10 = (bf16[3,128,256]{2,1,0:T(8,128)(2,1)S(1)}, bf16[3,128,256]{2,1,0:T(8,128)(2,1)S(1)}, u32[]{:S(2)}, u32[]{:S(2)}) collective-permute-start(bf16[3,128,256]{2,1,0:T(8,128)(2,1)S(1)} %slice.7), channel_id=1, source_target_pairs={{0,16},{4,20},{8,24},{12,28},{16,0},{20,4},{24,8},{28,12},{1,17},{... | collective-permute-start | bytes 589832 | tf_op jit(solution)/shard_map/ppermute | solution.py:338
  43.6 3.0 %collective-permute-start.13 = (bf16[6,128,256]{2,1,0:T(8,128)(2,1)S(1)}, bf16[6,128,256]{2,1,0:T(8,128)(2,1)S(1)}, u32[]{:S(2)}, u32[]{:S(2)}) collective-permute-start(bf16[6,128,256]{2,1,0:T(8,128)(2,1)S(1)} %get-tuple-element.56), channel_id=1, source_target_pairs={{0,4},{4,0},{8,12},{12,8},{16,20},{20,16},{24,28},{28,24},{1,5},{5... | collective-permute-start | bytes 1179656 | tf_op jit(solution)/shard_map/ppermute | solution.py:338
  43.7 2.8 %collective-permute-start.11 = (bf16[3,128,256]{2,1,0:T(8,128)(2,1)S(1)}, bf16[3,128,256]{2,1,0:T(8,128)(2,1)S(1)}, u32[]{:S(2)}, u32[]{:S(2)}) collective-permute-start(bf16[3,128,256]{2,1,0:T(8,128)(2,1)S(1)} %collective-permute-done.9.rest_0_), channel_id=1, source_target_pairs={{0,4},{4,0},{8,12},{12,8},{16,20},{20,16},{24,28},{28,24},{1,5},{5... | collective-permute-start | bytes 589832 | tf_op jit(solution)/shard_map/ppermute | solution.py:338
  44.2 2.4 %collective-permute-start.12 = (bf16[3,128,256]{2,1,0:T(8,128)(2,1)S(1)}, bf16[3,128,256]{2,1,0:T(8,128)(2,1)S(1)}, u32[]{:S(2)}, u32[]{:S(2)}) collective-permute-start(bf16[3,128,256]{2,1,0:T(8,128)(2,1)S(1)} %collective-permute-done.10.rest_1_), channel_id=1, source_target_pairs={{0,4},{4,0},{8,12},{12,8},{16,20},{20,16},{24,28},{28,24},{1,5},{5... | collective-permute-start | bytes 589832 | tf_op jit(solution)/shard_map/ppermute | solution.py:338

commit v10 on v9

--- a/solution.py
+++ b/solution.py
@@ -325,13 +325,12 @@
     halo = region_boxes // 2
     near_halo = region_boxes // 4
     classes, directions = transfer_table.shape
-    shared = classes * 5 // 8
+    shared = classes // 2
     capacity = (shared + 1) // 2
     empty = capacity + classes - shared
-    second_end = capacity + pad_to(classes // 8, UNROLL)
+    second_end = capacity + pad_to(classes // 5, UNROLL)
     top = dir_count // 2
     inner = range(2, top, 2)
-    split = boxes // 2
     targets = 2 * boxes
 
     def partner(array, mask):
@@ -452,13 +451,10 @@
             cost_estimate=pl.CostEstimate(flops=MIB, bytes_accessed=MIB, transcendentals=0),
         )(*args)
 
-    tied = lax.optimization_barrier(
-        (table, [field[top + m] for m in inner], [rim[m] for m in inner], rim[top])
-    )
-    table, far_fields, inner_rims, rim[top] = tied
-    for m, value, other in zip(inner, far_fields, inner_rims):
-        field[top + m], rim[m] = value, other
-    last = {m: [partner(rim[top][:split], m), partner(rim[m][split:], top)] for m in inner}
+    table, inner_rims = lax.optimization_barrier((table, [rim[m] for m in inner]))
+    for m, value in zip(inner, inner_rims):
+        rim[m] = value
+    last = {m: partner(rim[m], top) for m in inner}
 
     full = (boxes, unknowns, incidences)
     early = [(False, m, [field[m]]) for m in (0, *inner, top)] + [(True, 0, [rim[0]])]
@@ -493,10 +489,10 @@
     from_other = partner(for_other, 1)
 
     total, last = lax.optimization_barrier((total, last))
-    turned = {m: [partner(part, 1) for part in last[m]] for m in inner}
+    turned = {m: partner(last[m], 1) for m in inner}
     total = apply((early + middle)[count:], 0, total, None, F32, full)
-    late = [(True, top + m, last[m]) for m in inner]
-    late += [(True, top + m + 1, turned[m]) for m in inner]
+    late = [(True, top + m, [last[m]]) for m in inner]
+    late += [(True, top + m + 1, [turned[m]]) for m in inner]
     return apply(late, 0, total, from_other, BF16, currents.shape)
 
 

time: 49.7 us -> 49.3 us (level)
  starting transfers between devices: 16.8 us -> 14.1 us
  Pallas kernels: 31.1 us -> 33.7 us
    ppermute x12 -> x10, starting transfers between devices: 14.3 us -> 11.5 us  [partner(): return lax.ppermute(array, 'dir', [(i, i ^ mask) for i in range(dir_count)])]
    pallas_call x1, Pallas kernels: 8.03 us -> 10.2 us  [shards(): pl.pallas_call(functools.partial(second_kernel, second_end, empty, halo -...]
    ppermute x2, waiting for transfers between devices: 1.11 us -> 0.01 us  [beyond(): return lax.ppermute(array, ('dir', 'region'), along)]
    ppermute x12 -> x10, waiting for transfers between devices: 0.03 us -> 1.11 us  [partner(): return lax.ppermute(array, 'dir', [(i, i ^ mask) for i in range(dir_count)])]
    pallas_call x1, Pallas kernels: 7.2 us -> 8.06 us  [shards(): pl.pallas_call(functools.partial(third_kernel, second_end, empty, [(outsi...]
  transfers between devices with their start and end apart: 14 -> 12, of which waited for: 1 -> 1; matrix products, arithmetic and copies ran while one was open for 0% -> 0% of each run, Pallas kernels for 58% -> 63%
where the time goes in v10:
time: 49.3 us; the launch traced here: 49.1 us
  Pallas kernels  33.7 us (68%)
  starting transfers between devices  14.1 us (29%)
  waiting for transfers between devices  1.12 us (2%)
    ppermute x10, starting transfers between devices, partner(): return lax.ppermute(array, 'dir', [(i, i ^ mask) for i in range(dir_count)])  11.5 us
    pallas_call x1, Pallas kernels, shards(): pl.pallas_call(functools.partial(first_kernel, shared, boxes, halo, regio...  10.5 us
    pallas_call x1, Pallas kernels, shards(): pl.pallas_call(functools.partial(second_kernel, second_end, empty, halo -...  10.2 us
    pallas_call x1, Pallas kernels, shards(): pl.pallas_call(functools.partial(third_kernel, second_end, empty, [(outsi...  8.06 us
    pallas_call x2, Pallas kernels, apply(): pl.pallas_call(kernel, in_specs=specs, out_specs=vmem, out_shape=pltpu.VM...  4.88 us
    ppermute x2, starting transfers between devices, beyond(): return lax.ppermute(array, ('dir', 'region'), along)  2.56 us
    ppermute x10, waiting for transfers between devices, partner(): return lax.ppermute(array, 'dir', [(i, i ^ mask) for i in range(dir_count)])  1.11 us
  transfers between devices with their start and end apart: 12, of which 1 were waited for; matrix products, arithmetic and copies ran while one was open for 0% of the time, Pallas kernels for 63%

profile of v10, /device:TPU:0, one launch (start us, length us, event | category | flops | bytes accessed | tf_op | source)
XLA Modules:
  0.0 49.1 jit_solution(4632063711793313745)
XLA Ops:
  0.0 0.5 collective-permute-start.3
  0.5 1.3 %collective-permute-start.2 = (bf16[6,128,256]{2,1,0:T(8,128)(2,1)}, bf16[6,128,256]{2,1,0:T(8,128)(2,1)S(1)}, u32[]{:S(2)}, u32[]{:S(2)}) collective-permute-start(bf16[6,128,256]{2,1,0:T(8,128)(2,1)} %bitcast.2), channel_id=1, source_target_pairs={{1,0},{2,1},{3,2},{5,4},{6,5},{7,6},{9,8},{10,9},{11,10},{13,12},{... | collective-permute-start | bytes 1179656 | tf_op jit(solution)/shard_map/ppermute | solution.py:347
  1.7 4.8 %collective-permute-start.1 = (bf16[6,128,256]{2,1,0:T(8,128)(2,1)}, bf16[6,128,256]{2,1,0:T(8,128)(2,1)S(1)}, u32[]{:S(2)}, u32[]{:S(2)}) collective-permute-start(bf16[6,128,256]{2,1,0:T(8,128)(2,1)} %bitcast.3), channel_id=1, source_target_pairs={{0,16},{4,20},{8,24},{12,28},{16,0},{20,4},{24,8},{28,12},{1,17},{... | collective-permute-start | bytes 1179656 | tf_op jit(solution)/shard_map/ppermute | solution.py:337
  6.5 1.5 %collective-permute-start = (bf16[6,128,256]{2,1,0:T(8,128)(2,1)}, bf16[6,128,256]{2,1,0:T(8,128)(2,1)S(1)}, u32[]{:S(2)}, u32[]{:S(2)}) collective-permute-start(bf16[6,128,256]{2,1,0:T(8,128)(2,1)} %bitcast.4), channel_id=1, source_target_pairs={{0,8},{4,12},{8,0},{12,4},{16,24},{20,28},{24,16},{28,20},{1,9},{5... | collective-permute-start | bytes 1179656 | tf_op jit(solution)/shard_map/ppermute | solution.py:337
  8.0 0.0 copy-start.1
  8.0 0.0 collective-permute-start.4
  8.0 10.5 %shard_map.91 = (bf16[79,128,128]{2,1,0:T(8,128)(2,1)S(1)}, bf16[128,1536]{1,0:T(8,128)(2,1)S(1)}, bf16[1536,128]{1,0:T(8,128)(2,1)S(1)}, f32[316,1536]{1,0:T(8,...) custom-call(s32[9]{0:T(128)} %off_hbm.1, s32[1,48,48]{2,1,0:T(8,128)} %src_hbm.1, s32[1,48,48]{2,1,0:T(8,128)} %tid_hbm.1, ...), custom_call_target="tpu_custom_call" | custom-call | flops 7952400384 | bytes 1048576 | tf_op jit(solution)/shard_map/pallas_call | solution.py:373
  18.6 0.0 collective-permute-done.2.rest_3_
  18.6 0.0 collective-permute-done.1.rest_2_
  18.6 0.0 collective-permute-done.rest_1_
  18.6 0.0 collective-permute-done.4.near_src_other_ref
  18.6 0.0 collective-permute-done.3.near_other_hbm
  18.6 0.6 %collective-permute-start.5 = (bf16[79,128,128]{2,1,0:T(8,128)(2,1)S(1)}, bf16[79,128,128]{2,1,0:T(8,128)(2,1)S(1)}, u32[]{:S(2)}, u32[]{:S(2)}) collective-permute-start(bf16[79,128,128]{2,1,0:T(8,128)(2,1)S(1)} %get-tuple-element.37.low_ref), channel_id=1, source_target_pairs={{0,4},{4,0},{8,12},{12,8},{16,20},{20,16},{24,28},{28,24},{1,5},{5... | collective-permute-start | bytes 7766024 | tf_op jit(solution)/shard_map/ppermute | solution.py:337
  19.2 1.3 %collective-permute-start.7 = (bf16[6,128,256]{2,1,0:T(8,128)(2,1)S(1)}, bf16[6,128,256]{2,1,0:T(8,128)(2,1)S(1)}, u32[]{:S(2)}, u32[]{:S(2)}) collective-permute-start(bf16[6,128,256]{2,1,0:T(8,128)(2,1)S(1)} %collective-permute-done.rest_1_), channel_id=1, source_target_pairs={{1,0},{2,1},{3,2},{5,4},{6,5},{7,6},{9,8},{10,9},{11,10},{13,12},{... | collective-permute-start | bytes 1179656 | tf_op jit(solution)/shard_map/ppermute | solution.py:347
  20.5 0.1 collective-permute-start.6
  20.6 2.6 %collective-permute-start.8 = (bf16[6,128,256]{2,1,0:T(8,128)(2,1)S(1)}, bf16[6,128,256]{2,1,0:T(8,128)(2,1)S(1)}, u32[]{:S(2)}, u32[]{:S(2)}) collective-permute-start(bf16[6,128,256]{2,1,0:T(8,128)(2,1)S(1)} %collective-permute-done.2.rest_3_), channel_id=1, source_target_pairs={{0,16},{4,20},{8,24},{12,28},{16,0},{20,4},{24,8},{28,12},{1,17},{... | collective-permute-start | bytes 1179656 | tf_op jit(solution)/shard_map/ppermute | solution.py:337
  23.2 0.0 copy-done.1
  23.2 10.2 %shard_map.92 = (bf16[317,128,128]{2,1,0:T(8,128)(2,1)S(1)}, bf16[12,28,128,128]{3,2,1,0:T(8,128)(2,1)S(1)}, s32[16,128]{1,0:T(8,128)S(1)}) custom-call(s32[8,384]{1,0:T(8,128)S(1)} %get-tuple-element.29.list_ref, f32[316,1536]{1,0:T(8,128)S(1)} %get-tuple-element.30.rows_ref, bf16[128,1536]{1,0:T(8,128)(2,1)S(1)} %get-tuple-element.31.weighted_ref, ...), custom_call_target="tpu_custom_call" | custom-call | flops 7952400384 | bytes 1048576 | tf_op jit(solution)/shard_map/pallas_call | solution.py:410
  33.4 0.0 collective-permute-done.7.rest_5_.rest_1_
  33.4 0.1 collective-permute-start.9
  33.5 0.0 collective-permute-done.6.rest_4_.rest_0_
  33.5 0.0 collective-permute-done.8.rest_6_.rest_2_
  33.5 0.0 collective-permute-done.5.low_ref
  33.5 0.0 copy-done
  33.5 8.1 %shard_map.93 = (bf16[317,128,128]{2,1,0:T(8,128)(2,1)S(1)}, bf16[6,128,256]{2,1,0:T(8,128)(2,1)S(1)}, f32[6,128,256]{2,1,0:T(8,128)S(1)}) custom-call(s32[8,384]{1,0:T(8,128)S(1)} %get-tuple-element.29.list_ref, s32[16,128]{1,0:T(8,128)S(1)} %get-tuple-element.28.cls_ref, ...), custom_call_target="tpu_custom_call", output_to_operand_aliasing={{0}: (15, {})} | custom-call | flops 1048576 | bytes 1048576 | tf_op jit(solution)/shard_map/pallas_call | solution.py:466
  41.6 1.5 %collective-permute-start.11 = (bf16[6,128,256]{2,1,0:T(8,128)(2,1)S(1)}, bf16[6,128,256]{2,1,0:T(8,128)(2,1)S(1)}, u32[]{:S(2)}, u32[]{:S(2)}) collective-permute-start(bf16[6,128,256]{2,1,0:T(8,128)(2,1)S(1)} %get-tuple-element.50), channel_id=1, source_target_pairs={{0,4},{4,0},{8,12},{12,8},{16,20},{20,16},{24,28},{28,24},{1,5},{5... | collective-permute-start | bytes 1179656 | tf_op jit(solution)/shard_map/ppermute | solution.py:337
  43.1 1.1 %collective-permute-done.9.rest_0_ = bf16[6,128,256]{2,1,0:T(8,128)(2,1)S(1)} collective-permute-done((bf16[6,128,256]{2,1,0:T(8,128)(2,1)S(1)}, bf16[6,128,256]{2,1,0:T(8,128)(2,1)S(1)}, u32[]{:S(2)}, u32[]{:S(2)}) %collective-permute-start.9) | collective-permute-done | bytes 393248 | tf_op jit(solution)/shard_map/ppermute | solution.py:337
  44.1 0.0 collective-permute-start.10
  44.1 2.2 %shard_map.94.rest_2_ = f32[6,128,256]{2,1,0:T(8,128)S(1)} custom-call(s32[16,128]{1,0:T(8,128)S(1)} %get-tuple-element.28.cls_ref, s32[16,128]{1,0:T(8,128)S(1)} %get-tuple-element.38.near_map_ref, s32[8,384]{1,0:T(8,128)S(1)} %get-tuple-element.29.list_ref, bf16[317,128,128]{2,1,0:T(8,128)(2,1)S(1)} %get-tuple-element.46.t_ref, ...), custom_call_target="tpu_custom_call" | custom-call | flops 1048576 | bytes 1048576 | tf_op jit(solution)/shard_map/pallas_call | solution.py:445
  46.4 0.0 collective-permute-done.11.rest_3_
  46.4 0.0 collective-permute-done.10.rest_1_
  46.4 2.6 %shard_map.95 = bf16[1,6,128,256]{3,2,1,0:T(8,128)(2,1)} custom-call(s32[16,128]{1,0:T(8,128)S(1)} %get-tuple-element.28.cls_ref, s32[16,128]{1,0:T(8,128)S(1)} %get-tuple-element.38.near_map_ref, s32[8,384]{1,0:T(8,128)S(1)} %get-tuple-element.29.list_ref, bf16[317,128,128]{2,1,0:T(8,128)(2,1)S(1)} %get-tuple-element.46.t_ref, ...), custom_call_target="tpu_custom_call" | custom-call | flops 1048576 | bytes 1048576 | tf_op jit(solution)/shard_map/pallas_call | solution.py:445
  (1 shorter events, 0.0 us)
Async XLA Ops:
  0.0 18.6 %collective-permute-start.3 = (bf16[1,6,27,128,128]{4,3,2,1,0:T(8,128)(2,1)}, bf16[1,6,27,128,128]{4,3,2,1,0:T(8,128)(2,1)S(1)}, u32[]{:S(2)}, u32[]{:S(2)}) collective-permute-start(bf16[1,6,27,128,128]{4,3,2,1,0:T(8,128)(2,1)} %near_hbm.1), channel_id=1, source_target_pairs={{0,4},{4,0},{8,12},{12,8},{16,20},{20,16},{24,28},{28,24},{1,5},{5... | collective-permute-start | bytes 15925256 | tf_op jit(solution)/shard_map/ppermute | solution.py:337
  0.5 18.1 %collective-permute-start.2 = (bf16[6,128,256]{2,1,0:T(8,128)(2,1)}, bf16[6,128,256]{2,1,0:T(8,128)(2,1)S(1)}, u32[]{:S(2)}, u32[]{:S(2)}) collective-permute-start(bf16[6,128,256]{2,1,0:T(8,128)(2,1)} %bitcast.2), channel_id=1, source_target_pairs={{1,0},{2,1},{3,2},{5,4},{6,5},{7,6},{9,8},{10,9},{11,10},{13,12},{... | collective-permute-start | bytes 1179656 | tf_op jit(solution)/shard_map/ppermute | solution.py:347
  1.7 16.8 %collective-permute-start.1 = (bf16[6,128,256]{2,1,0:T(8,128)(2,1)}, bf16[6,128,256]{2,1,0:T(8,128)(2,1)S(1)}, u32[]{:S(2)}, u32[]{:S(2)}) collective-permute-start(bf16[6,128,256]{2,1,0:T(8,128)(2,1)} %bitcast.3), channel_id=1, source_target_pairs={{0,16},{4,20},{8,24},{12,28},{16,0},{20,4},{24,8},{28,12},{1,17},{... | collective-permute-start | bytes 1179656 | tf_op jit(solution)/shard_map/ppermute | solution.py:337
  6.5 12.0 %collective-permute-start = (bf16[6,128,256]{2,1,0:T(8,128)(2,1)}, bf16[6,128,256]{2,1,0:T(8,128)(2,1)S(1)}, u32[]{:S(2)}, u32[]{:S(2)}) collective-permute-start(bf16[6,128,256]{2,1,0:T(8,128)(2,1)} %bitcast.4), channel_id=1, source_target_pairs={{0,8},{4,12},{8,0},{12,4},{16,24},{20,28},{24,16},{28,20},{1,9},{5... | collective-permute-start | bytes 1179656 | tf_op jit(solution)/shard_map/ppermute | solution.py:337
  8.0 15.1 %copy-start.1 = (s32[1,6,27]{2,0,1:T(1,128)S(1)}, s32[1,6,27]{2,0,1:T(1,128)}, u32[]{:S(2)}) copy-start(s32[1,6,27]{2,0,1:T(1,128)} %param.17) | copy-start | bytes 1948
  8.0 10.6 %collective-permute-start.4 = (s32[6,1,27]{2,1,0:T(1,128)}, s32[6,1,27]{2,1,0:T(1,128)S(1)}, u32[]{:S(2)}, u32[]{:S(2)}) collective-permute-start(s32[6,1,27]{2,1,0:T(1,128)} %bitcast.6), channel_id=1, source_target_pairs={{0,4},{4,0},{8,12},{12,8},{16,20},{20,16},{24,28},{28,24},{1,5},{5... | collective-permute-start | bytes 1952 | tf_op jit(solution)/shard_map/ppermute | solution.py:337
  18.6 14.9 %collective-permute-start.5 = (bf16[79,128,128]{2,1,0:T(8,128)(2,1)S(1)}, bf16[79,128,128]{2,1,0:T(8,128)(2,1)S(1)}, u32[]{:S(2)}, u32[]{:S(2)}) collective-permute-start(bf16[79,128,128]{2,1,0:T(8,128)(2,1)S(1)} %get-tuple-element.37.low_ref), channel_id=1, source_target_pairs={{0,4},{4,0},{8,12},{12,8},{16,20},{20,16},{24,28},{28,24},{1,5},{5... | collective-permute-start | bytes 7766024 | tf_op jit(solution)/shard_map/ppermute | solution.py:337
  19.2 14.2 %collective-permute-start.7 = (bf16[6,128,256]{2,1,0:T(8,128)(2,1)S(1)}, bf16[6,128,256]{2,1,0:T(8,128)(2,1)S(1)}, u32[]{:S(2)}, u32[]{:S(2)}) collective-permute-start(bf16[6,128,256]{2,1,0:T(8,128)(2,1)S(1)} %collective-permute-done.rest_1_), channel_id=1, source_target_pairs={{1,0},{2,1},{3,2},{5,4},{6,5},{7,6},{9,8},{10,9},{11,10},{13,12},{... | collective-permute-start | bytes 1179656 | tf_op jit(solution)/shard_map/ppermute | solution.py:347
  20.5 13.0 %collective-permute-start.6 = (bf16[6,128,256]{2,1,0:T(8,128)(2,1)S(1)}, bf16[6,128,256]{2,1,0:T(8,128)(2,1)S(1)}, u32[]{:S(2)}, u32[]{:S(2)}) collective-permute-start(bf16[6,128,256]{2,1,0:T(8,128)(2,1)S(1)} %collective-permute-done.1.rest_2_), channel_id=1, source_target_pairs={{0,8},{4,12},{8,0},{12,4},{16,24},{20,28},{24,16},{28,20},{1,9},{5... | collective-permute-start | bytes 1179656 | tf_op jit(solution)/shard_map/ppermute | solution.py:337
  20.6 12.9 %collective-permute-start.8 = (bf16[6,128,256]{2,1,0:T(8,128)(2,1)S(1)}, bf16[6,128,256]{2,1,0:T(8,128)(2,1)S(1)}, u32[]{:S(2)}, u32[]{:S(2)}) collective-permute-start(bf16[6,128,256]{2,1,0:T(8,128)(2,1)S(1)} %collective-permute-done.2.rest_3_), channel_id=1, source_target_pairs={{0,16},{4,20},{8,24},{12,28},{16,0},{20,4},{24,8},{28,12},{1,17},{... | collective-permute-start | bytes 1179656 | tf_op jit(solution)/shard_map/ppermute | solution.py:337
  23.2 10.3 %copy-start = (bf16[1,6,128,256]{3,2,1,0:T(8,128)(2,1)S(1)}, bf16[1,6,128,256]{3,2,1,0:T(8,128)(2,1)}, u32[]{:S(2)}) copy-start(bf16[1,6,128,256]{3,2,1,0:T(8,128)(2,1)} %param.9) | copy-start | bytes 1179652
  33.4 10.7 %collective-permute-start.9 = (bf16[6,128,256]{2,1,0:T(8,128)(2,1)S(1)}, bf16[6,128,256]{2,1,0:T(8,128)(2,1)S(1)}, u32[]{:S(2)}, u32[]{:S(2)}) collective-permute-start(bf16[6,128,256]{2,1,0:T(8,128)(2,1)S(1)} %collective-permute-done.7.rest_5_.rest_1_), channel_id=1, source_target_pairs={{0,16},{4,20},{8,24},{12,28},{16,0},{20,4},{24,8},{28,12},{1,17},{... | collective-permute-start | bytes 1179656 | tf_op jit(solution)/shard_map/ppermute | solution.py:337
  41.6 4.8 %collective-permute-start.11 = (bf16[6,128,256]{2,1,0:T(8,128)(2,1)S(1)}, bf16[6,128,256]{2,1,0:T(8,128)(2,1)S(1)}, u32[]{:S(2)}, u32[]{:S(2)}) collective-permute-start(bf16[6,128,256]{2,1,0:T(8,128)(2,1)S(1)} %get-tuple-element.50), channel_id=1, source_target_pairs={{0,4},{4,0},{8,12},{12,8},{16,20},{20,16},{24,28},{28,24},{1,5},{5... | collective-permute-start | bytes 1179656 | tf_op jit(solution)/shard_map/ppermute | solution.py:337
  44.1 2.3 %collective-permute-start.10 = (bf16[6,128,256]{2,1,0:T(8,128)(2,1)S(1)}, bf16[6,128,256]{2,1,0:T(8,128)(2,1)S(1)}, u32[]{:S(2)}, u32[]{:S(2)}) collective-permute-start(bf16[6,128,256]{2,1,0:T(8,128)(2,1)S(1)} %collective-permute-done.9.rest_0_), channel_id=1, source_target_pairs={{0,4},{4,0},{8,12},{12,8},{16,20},{20,16},{24,28},{28,24},{1,5},{5... | collective-permute-start | bytes 1179656 | tf_op jit(solution)/shard_map/ppermute | solution.py:337

commit v11 on v10

--- a/solution.py
+++ b/solution.py
@@ -328,7 +328,7 @@
     shared = classes // 2
     capacity = (shared + 1) // 2
     empty = capacity + classes - shared
-    second_end = capacity + pad_to(classes // 5, UNROLL)
+    second_end = capacity + pad_to(classes // 8, UNROLL)
     top = dir_count // 2
     inner = range(2, top, 2)
     targets = 2 * boxes

time: 49.3 us -> 47.7 us (0.968)
  starting transfers between devices: 14.1 us -> 12.7 us
  Pallas kernels: 33.7 us -> 33.1 us
    pallas_call x1, Pallas kernels: 10.2 us -> 8.35 us  [shards(): pl.pallas_call(functools.partial(second_kernel, second_end, empty, halo -...]
    ppermute x10, starting transfers between devices: 11.5 us -> 10.1 us  [partner(): return lax.ppermute(array, 'dir', [(i, i ^ mask) for i in range(dir_count)])]
    pallas_call x1, Pallas kernels: 8.06 us -> 9.34 us  [shards(): pl.pallas_call(functools.partial(third_kernel, second_end, empty, [(outsi...]
    ppermute x2, waiting for transfers between devices: 0.01 us -> 0.57 us  [beyond(): return lax.ppermute(array, ('dir', 'region'), along)]
  transfers between devices with their start and end apart: 12 -> 12, of which waited for: 1 -> 3; matrix products, arithmetic and copies ran while one was open for 0% -> 0% of each run, Pallas kernels for 63% -> 64%
where the time goes in v11:
time: 47.7 us; the launch traced here: 47.2 us
  Pallas kernels  33.1 us (69%)
  starting transfers between devices  12.7 us (27%)
  waiting for transfers between devices  1.35 us (3%)
    pallas_call x1, Pallas kernels, shards(): pl.pallas_call(functools.partial(first_kernel, shared, boxes, halo, regio...  10.5 us
    ppermute x10, starting transfers between devices, partner(): return lax.ppermute(array, 'dir', [(i, i ^ mask) for i in range(dir_count)])  10.1 us
    pallas_call x1, Pallas kernels, shards(): pl.pallas_call(functools.partial(third_kernel, second_end, empty, [(outsi...  9.34 us
    pallas_call x1, Pallas kernels, shards(): pl.pallas_call(functools.partial(second_kernel, second_end, empty, halo -...  8.35 us
    pallas_call x2, Pallas kernels, apply(): pl.pallas_call(kernel, in_specs=specs, out_specs=vmem, out_shape=pltpu.VM...  4.87 us
    ppermute x2, starting transfers between devices, beyond(): return lax.ppermute(array, ('dir', 'region'), along)  2.56 us
  transfers between devices with their start and end apart: 12, of which 3 were waited for; matrix products, arithmetic and copies ran while one was open for 0% of the time, Pallas kernels for 64%

profile of v11, /device:TPU:0, one launch (start us, length us, event | category | flops | bytes accessed | tf_op | source)
XLA Modules:
  0.0 47.2 jit_solution(16294031964969146098)
XLA Ops:
  0.0 0.5 collective-permute-start.3
  0.5 1.3 %collective-permute-start.2 = (bf16[6,128,256]{2,1,0:T(8,128)(2,1)}, bf16[6,128,256]{2,1,0:T(8,128)(2,1)S(1)}, u32[]{:S(2)}, u32[]{:S(2)}) collective-permute-start(bf16[6,128,256]{2,1,0:T(8,128)(2,1)} %bitcast.2), channel_id=1, source_target_pairs={{1,0},{2,1},{3,2},{5,4},{6,5},{7,6},{9,8},{10,9},{11,10},{13,12},{... | collective-permute-start | bytes 1179656 | tf_op jit(solution)/shard_map/ppermute | solution.py:347
  1.7 4.8 %collective-permute-start.1 = (bf16[6,128,256]{2,1,0:T(8,128)(2,1)}, bf16[6,128,256]{2,1,0:T(8,128)(2,1)S(1)}, u32[]{:S(2)}, u32[]{:S(2)}) collective-permute-start(bf16[6,128,256]{2,1,0:T(8,128)(2,1)} %bitcast.3), channel_id=1, source_target_pairs={{0,16},{4,20},{8,24},{12,28},{16,0},{20,4},{24,8},{28,12},{1,17},{... | collective-permute-start | bytes 1179656 | tf_op jit(solution)/shard_map/ppermute | solution.py:337
  6.5 1.5 %collective-permute-start = (bf16[6,128,256]{2,1,0:T(8,128)(2,1)}, bf16[6,128,256]{2,1,0:T(8,128)(2,1)S(1)}, u32[]{:S(2)}, u32[]{:S(2)}) collective-permute-start(bf16[6,128,256]{2,1,0:T(8,128)(2,1)} %bitcast.4), channel_id=1, source_target_pairs={{0,8},{4,12},{8,0},{12,4},{16,24},{20,28},{24,16},{28,20},{1,9},{5... | collective-permute-start | bytes 1179656 | tf_op jit(solution)/shard_map/ppermute | solution.py:337
  8.0 0.0 copy-start.1
  8.0 0.0 collective-permute-start.4
  8.0 10.5 %shard_map.91 = (bf16[79,128,128]{2,1,0:T(8,128)(2,1)S(1)}, bf16[128,1536]{1,0:T(8,128)(2,1)S(1)}, bf16[1536,128]{1,0:T(8,128)(2,1)S(1)}, f32[316,1536]{1,0:T(8,...) custom-call(s32[9]{0:T(128)} %off_hbm.1, s32[1,48,48]{2,1,0:T(8,128)} %src_hbm.1, s32[1,48,48]{2,1,0:T(8,128)} %tid_hbm.1, ...), custom_call_target="tpu_custom_call" | custom-call | flops 7952400384 | bytes 1048576 | tf_op jit(solution)/shard_map/pallas_call | solution.py:373
  18.6 0.0 collective-permute-done.2.rest_3_
  18.6 0.0 collective-permute-done.1.rest_2_
  18.6 0.0 collective-permute-done.rest_1_
  18.6 0.0 collective-permute-done.4.near_src_other_ref
  18.6 0.0 collective-permute-done.3.near_other_hbm
  18.6 0.6 %collective-permute-start.5 = (bf16[79,128,128]{2,1,0:T(8,128)(2,1)S(1)}, bf16[79,128,128]{2,1,0:T(8,128)(2,1)S(1)}, u32[]{:S(2)}, u32[]{:S(2)}) collective-permute-start(bf16[79,128,128]{2,1,0:T(8,128)(2,1)S(1)} %get-tuple-element.37.low_ref), channel_id=1, source_target_pairs={{0,4},{4,0},{8,12},{12,8},{16,20},{20,16},{24,28},{28,24},{1,5},{5... | collective-permute-start | bytes 7766024 | tf_op jit(solution)/shard_map/ppermute | solution.py:337
  19.2 1.3 %collective-permute-start.7 = (bf16[6,128,256]{2,1,0:T(8,128)(2,1)S(1)}, bf16[6,128,256]{2,1,0:T(8,128)(2,1)S(1)}, u32[]{:S(2)}, u32[]{:S(2)}) collective-permute-start(bf16[6,128,256]{2,1,0:T(8,128)(2,1)S(1)} %collective-permute-done.rest_1_), channel_id=1, source_target_pairs={{1,0},{2,1},{3,2},{5,4},{6,5},{7,6},{9,8},{10,9},{11,10},{13,12},{... | collective-permute-start | bytes 1179656 | tf_op jit(solution)/shard_map/ppermute | solution.py:347
  20.5 0.1 collective-permute-start.6
  20.6 2.6 %collective-permute-start.8 = (bf16[6,128,256]{2,1,0:T(8,128)(2,1)S(1)}, bf16[6,128,256]{2,1,0:T(8,128)(2,1)S(1)}, u32[]{:S(2)}, u32[]{:S(2)}) collective-permute-start(bf16[6,128,256]{2,1,0:T(8,128)(2,1)S(1)} %collective-permute-done.2.rest_3_), channel_id=1, source_target_pairs={{0,16},{4,20},{8,24},{12,28},{16,0},{20,4},{24,8},{28,12},{1,17},{... | collective-permute-start | bytes 1179656 | tf_op jit(solution)/shard_map/ppermute | solution.py:337
  23.2 0.0 copy-done.1
  23.2 8.3 %shard_map.92 = (bf16[317,128,128]{2,1,0:T(8,128)(2,1)S(1)}, bf16[12,28,128,128]{3,2,1,0:T(8,128)(2,1)S(1)}, s32[16,128]{1,0:T(8,128)S(1)}) custom-call(s32[8,384]{1,0:T(8,128)S(1)} %get-tuple-element.29.list_ref, f32[316,1536]{1,0:T(8,128)S(1)} %get-tuple-element.30.rows_ref, bf16[128,1536]{1,0:T(8,128)(2,1)S(1)} %get-tuple-element.31.weighted_ref, ...), custom_call_target="tpu_custom_call" | custom-call | flops 7952400384 | bytes 1048576 | tf_op jit(solution)/shard_map/pallas_call | solution.py:410
  31.5 0.6 %collective-permute-done.7.rest_5_.rest_1_ = bf16[6,128,256]{2,1,0:T(8,128)(2,1)S(1)} collective-permute-done((bf16[6,128,256]{2,1,0:T(8,128)(2,1)S(1)}, bf16[6,128,256]{2,1,0:T(8,128)(2,1)S(1)}, u32[]{:S(2)}, u32[]{:S(2)}) %collective-permute-start.7) | collective-permute-done | bytes 393248 | tf_op jit(solution)/shard_map/ppermute | solution.py:347
  32.1 0.0 collective-permute-start.9
  32.1 0.0 collective-permute-done.6.rest_4_.rest_0_
  32.1 0.3 collective-permute-done.8.rest_6_.rest_2_
  32.4 0.0 collective-permute-done.5.low_ref
  32.4 0.0 copy-done
  32.4 9.3 %shard_map.93 = (bf16[317,128,128]{2,1,0:T(8,128)(2,1)S(1)}, bf16[6,128,256]{2,1,0:T(8,128)(2,1)S(1)}, f32[6,128,256]{2,1,0:T(8,128)S(1)}) custom-call(s32[8,384]{1,0:T(8,128)S(1)} %get-tuple-element.29.list_ref, s32[16,128]{1,0:T(8,128)S(1)} %get-tuple-element.28.cls_ref, ...), custom_call_target="tpu_custom_call", output_to_operand_aliasing={{0}: (15, {})} | custom-call | flops 1048576 | bytes 1048576 | tf_op jit(solution)/shard_map/pallas_call | solution.py:466
  41.7 0.1 collective-permute-start.11
  41.8 0.5 %collective-permute-done.9.rest_0_ = bf16[6,128,256]{2,1,0:T(8,128)(2,1)S(1)} collective-permute-done((bf16[6,128,256]{2,1,0:T(8,128)(2,1)S(1)}, bf16[6,128,256]{2,1,0:T(8,128)(2,1)S(1)}, u32[]{:S(2)}, u32[]{:S(2)}) %collective-permute-start.9) | collective-permute-done | bytes 393248 | tf_op jit(solution)/shard_map/ppermute | solution.py:337
  42.3 0.0 collective-permute-start.10
  42.3 2.2 %shard_map.94.rest_2_ = f32[6,128,256]{2,1,0:T(8,128)S(1)} custom-call(s32[16,128]{1,0:T(8,128)S(1)} %get-tuple-element.28.cls_ref, s32[16,128]{1,0:T(8,128)S(1)} %get-tuple-element.38.near_map_ref, s32[8,384]{1,0:T(8,128)S(1)} %get-tuple-element.29.list_ref, bf16[317,128,128]{2,1,0:T(8,128)(2,1)S(1)} %get-tuple-element.46.t_ref, ...), custom_call_target="tpu_custom_call" | custom-call | flops 1048576 | bytes 1048576 | tf_op jit(solution)/shard_map/pallas_call | solution.py:445
  44.6 0.0 collective-permute-done.11.rest_3_
  44.6 0.0 collective-permute-done.10.rest_1_
  44.6 2.6 %shard_map.95 = bf16[1,6,128,256]{3,2,1,0:T(8,128)(2,1)} custom-call(s32[16,128]{1,0:T(8,128)S(1)} %get-tuple-element.28.cls_ref, s32[16,128]{1,0:T(8,128)S(1)} %get-tuple-element.38.near_map_ref, s32[8,384]{1,0:T(8,128)S(1)} %get-tuple-element.29.list_ref, bf16[317,128,128]{2,1,0:T(8,128)(2,1)S(1)} %get-tuple-element.46.t_ref, ...), custom_call_target="tpu_custom_call" | custom-call | flops 1048576 | bytes 1048576 | tf_op jit(solution)/shard_map/pallas_call | solution.py:445
  (1 shorter events, 0.0 us)
Async XLA Ops:
  0.0 18.6 %collective-permute-start.3 = (bf16[1,6,27,128,128]{4,3,2,1,0:T(8,128)(2,1)}, bf16[1,6,27,128,128]{4,3,2,1,0:T(8,128)(2,1)S(1)}, u32[]{:S(2)}, u32[]{:S(2)}) collective-permute-start(bf16[1,6,27,128,128]{4,3,2,1,0:T(8,128)(2,1)} %near_hbm.1), channel_id=1, source_target_pairs={{0,4},{4,0},{8,12},{12,8},{16,20},{20,16},{24,28},{28,24},{1,5},{5... | collective-permute-start | bytes 15925256 | tf_op jit(solution)/shard_map/ppermute | solution.py:337
  0.5 18.1 %collective-permute-start.2 = (bf16[6,128,256]{2,1,0:T(8,128)(2,1)}, bf16[6,128,256]{2,1,0:T(8,128)(2,1)S(1)}, u32[]{:S(2)}, u32[]{:S(2)}) collective-permute-start(bf16[6,128,256]{2,1,0:T(8,128)(2,1)} %bitcast.2), channel_id=1, source_target_pairs={{1,0},{2,1},{3,2},{5,4},{6,5},{7,6},{9,8},{10,9},{11,10},{13,12},{... | collective-permute-start | bytes 1179656 | tf_op jit(solution)/shard_map/ppermute | solution.py:347
  1.7 16.8 %collective-permute-start.1 = (bf16[6,128,256]{2,1,0:T(8,128)(2,1)}, bf16[6,128,256]{2,1,0:T(8,128)(2,1)S(1)}, u32[]{:S(2)}, u32[]{:S(2)}) collective-permute-start(bf16[6,128,256]{2,1,0:T(8,128)(2,1)} %bitcast.3), channel_id=1, source_target_pairs={{0,16},{4,20},{8,24},{12,28},{16,0},{20,4},{24,8},{28,12},{1,17},{... | collective-permute-start | bytes 1179656 | tf_op jit(solution)/shard_map/ppermute | solution.py:337
  6.5 12.0 %collective-permute-start = (bf16[6,128,256]{2,1,0:T(8,128)(2,1)}, bf16[6,128,256]{2,1,0:T(8,128)(2,1)S(1)}, u32[]{:S(2)}, u32[]{:S(2)}) collective-permute-start(bf16[6,128,256]{2,1,0:T(8,128)(2,1)} %bitcast.4), channel_id=1, source_target_pairs={{0,8},{4,12},{8,0},{12,4},{16,24},{20,28},{24,16},{28,20},{1,9},{5... | collective-permute-start | bytes 1179656 | tf_op jit(solution)/shard_map/ppermute | solution.py:337
  8.0 15.1 %copy-start.1 = (s32[1,6,27]{2,0,1:T(1,128)S(1)}, s32[1,6,27]{2,0,1:T(1,128)}, u32[]{:S(2)}) copy-start(s32[1,6,27]{2,0,1:T(1,128)} %param.17) | copy-start | bytes 1948
  8.0 10.6 %collective-permute-start.4 = (s32[6,1,27]{2,1,0:T(1,128)}, s32[6,1,27]{2,1,0:T(1,128)S(1)}, u32[]{:S(2)}, u32[]{:S(2)}) collective-permute-start(s32[6,1,27]{2,1,0:T(1,128)} %bitcast.6), channel_id=1, source_target_pairs={{0,4},{4,0},{8,12},{12,8},{16,20},{20,16},{24,28},{28,24},{1,5},{5... | collective-permute-start | bytes 1952 | tf_op jit(solution)/shard_map/ppermute | solution.py:337
  18.6 13.8 %collective-permute-start.5 = (bf16[79,128,128]{2,1,0:T(8,128)(2,1)S(1)}, bf16[79,128,128]{2,1,0:T(8,128)(2,1)S(1)}, u32[]{:S(2)}, u32[]{:S(2)}) collective-permute-start(bf16[79,128,128]{2,1,0:T(8,128)(2,1)S(1)} %get-tuple-element.37.low_ref), channel_id=1, source_target_pairs={{0,4},{4,0},{8,12},{12,8},{16,20},{20,16},{24,28},{28,24},{1,5},{5... | collective-permute-start | bytes 7766024 | tf_op jit(solution)/shard_map/ppermute | solution.py:337
  19.2 12.9 %collective-permute-start.7 = (bf16[6,128,256]{2,1,0:T(8,128)(2,1)S(1)}, bf16[6,128,256]{2,1,0:T(8,128)(2,1)S(1)}, u32[]{:S(2)}, u32[]{:S(2)}) collective-permute-start(bf16[6,128,256]{2,1,0:T(8,128)(2,1)S(1)} %collective-permute-done.rest_1_), channel_id=1, source_target_pairs={{1,0},{2,1},{3,2},{5,4},{6,5},{7,6},{9,8},{10,9},{11,10},{13,12},{... | collective-permute-start | bytes 1179656 | tf_op jit(solution)/shard_map/ppermute | solution.py:347
  20.5 11.6 %collective-permute-start.6 = (bf16[6,128,256]{2,1,0:T(8,128)(2,1)S(1)}, bf16[6,128,256]{2,1,0:T(8,128)(2,1)S(1)}, u32[]{:S(2)}, u32[]{:S(2)}) collective-permute-start(bf16[6,128,256]{2,1,0:T(8,128)(2,1)S(1)} %collective-permute-done.1.rest_2_), channel_id=1, source_target_pairs={{0,8},{4,12},{8,0},{12,4},{16,24},{20,28},{24,16},{28,20},{1,9},{5... | collective-permute-start | bytes 1179656 | tf_op jit(solution)/shard_map/ppermute | solution.py:337
  20.6 11.8 %collective-permute-start.8 = (bf16[6,128,256]{2,1,0:T(8,128)(2,1)S(1)}, bf16[6,128,256]{2,1,0:T(8,128)(2,1)S(1)}, u32[]{:S(2)}, u32[]{:S(2)}) collective-permute-start(bf16[6,128,256]{2,1,0:T(8,128)(2,1)S(1)} %collective-permute-done.2.rest_3_), channel_id=1, source_target_pairs={{0,16},{4,20},{8,24},{12,28},{16,0},{20,4},{24,8},{28,12},{1,17},{... | collective-permute-start | bytes 1179656 | tf_op jit(solution)/shard_map/ppermute | solution.py:337
  23.2 9.2 %copy-start = (bf16[1,6,128,256]{3,2,1,0:T(8,128)(2,1)S(1)}, bf16[1,6,128,256]{3,2,1,0:T(8,128)(2,1)}, u32[]{:S(2)}) copy-start(bf16[1,6,128,256]{3,2,1,0:T(8,128)(2,1)} %param.9) | copy-start | bytes 1179652
  32.1 10.2 %collective-permute-start.9 = (bf16[6,128,256]{2,1,0:T(8,128)(2,1)S(1)}, bf16[6,128,256]{2,1,0:T(8,128)(2,1)S(1)}, u32[]{:S(2)}, u32[]{:S(2)}) collective-permute-start(bf16[6,128,256]{2,1,0:T(8,128)(2,1)S(1)} %collective-permute-done.7.rest_5_.rest_1_), channel_id=1, source_target_pairs={{0,16},{4,20},{8,24},{12,28},{16,0},{20,4},{24,8},{28,12},{1,17},{... | collective-permute-start | bytes 1179656 | tf_op jit(solution)/shard_map/ppermute | solution.py:337
  41.7 2.8 %collective-permute-start.11 = (bf16[6,128,256]{2,1,0:T(8,128)(2,1)S(1)}, bf16[6,128,256]{2,1,0:T(8,128)(2,1)S(1)}, u32[]{:S(2)}, u32[]{:S(2)}) collective-permute-start(bf16[6,128,256]{2,1,0:T(8,128)(2,1)S(1)} %get-tuple-element.50), channel_id=1, source_target_pairs={{0,4},{4,0},{8,12},{12,8},{16,20},{20,16},{24,28},{28,24},{1,5},{5... | collective-permute-start | bytes 1179656 | tf_op jit(solution)/shard_map/ppermute | solution.py:337
  42.3 2.3 %collective-permute-start.10 = (bf16[6,128,256]{2,1,0:T(8,128)(2,1)S(1)}, bf16[6,128,256]{2,1,0:T(8,128)(2,1)S(1)}, u32[]{:S(2)}, u32[]{:S(2)}) collective-permute-start(bf16[6,128,256]{2,1,0:T(8,128)(2,1)S(1)} %collective-permute-done.9.rest_0_), channel_id=1, source_target_pairs={{0,4},{4,0},{8,12},{12,8},{16,20},{20,16},{24,28},{28,24},{1,5},{5... | collective-permute-start | bytes 1179656 | tf_op jit(solution)/shard_map/ppermute | solution.py:337

commit v12 on v11

--- a/solution.py
+++ b/solution.py
@@ -325,7 +325,7 @@
     halo = region_boxes // 2
     near_halo = region_boxes // 4
     classes, directions = transfer_table.shape
-    shared = classes // 2
+    shared = classes * 5 // 8
     capacity = (shared + 1) // 2
     empty = capacity + classes - shared
     second_end = capacity + pad_to(classes // 8, UNROLL)

time: 47.7 us -> 49.2 us (1.031)
  waiting for transfers between devices: 1.35 us -> 3.51 us
  Pallas kernels: 33.1 us -> 31.7 us
  starting transfers between devices: 12.7 us -> 13.4 us
    ppermute x10, waiting for transfers between devices: 0.78 us -> 3.2 us  [partner(): return lax.ppermute(array, 'dir', [(i, i ^ mask) for i in range(dir_count)])]
    pallas_call x1, Pallas kernels: 9.34 us -> 7.24 us  [shards(): pl.pallas_call(functools.partial(third_kernel, second_end, empty, [(outsi...]
    pallas_call x1, Pallas kernels: 10.5 us -> 11.3 us  [shards(): pl.pallas_call(functools.partial(first_kernel, shared, boxes, halo, regio...]
    ppermute x10, starting transfers between devices: 10.1 us -> 10.8 us  [partner(): return lax.ppermute(array, 'dir', [(i, i ^ mask) for i in range(dir_count)])]
  transfers between devices with their start and end apart: 12 -> 12, of which waited for: 3 -> 3; matrix products, arithmetic and copies ran while one was open for 0% -> 0% of each run, Pallas kernels for 64% -> 60%
where the time goes in v12:
time: 49.2 us; the launch traced here: 48.7 us
  Pallas kernels  31.7 us (64%)
  starting transfers between devices  13.4 us (27%)
  waiting for transfers between devices  3.51 us (7%)
    pallas_call x1, Pallas kernels, shards(): pl.pallas_call(functools.partial(first_kernel, shared, boxes, halo, regio...  11.3 us
    ppermute x10, starting transfers between devices, partner(): return lax.ppermute(array, 'dir', [(i, i ^ mask) for i in range(dir_count)])  10.8 us
    pallas_call x1, Pallas kernels, shards(): pl.pallas_call(functools.partial(second_kernel, second_end, empty, halo -...  8.26 us
    pallas_call x1, Pallas kernels, shards(): pl.pallas_call(functools.partial(third_kernel, second_end, empty, [(outsi...  7.24 us
    pallas_call x2, Pallas kernels, apply(): pl.pallas_call(kernel, in_specs=specs, out_specs=vmem, out_shape=pltpu.VM...  4.91 us
    ppermute x10, waiting for transfers between devices, partner(): return lax.ppermute(array, 'dir', [(i, i ^ mask) for i in range(dir_count)])  3.2 us
    ppermute x2, starting transfers between devices, beyond(): return lax.ppermute(array, ('dir', 'region'), along)  2.57 us
  transfers between devices with their start and end apart: 12, of which 3 were waited for; matrix products, arithmetic and copies ran while one was open for 0% of the time, Pallas kernels for 60%

profile of v12, /device:TPU:0, one launch (start us, length us, event | category | flops | bytes accessed | tf_op | source)
XLA Modules:
  0.0 48.7 jit_solution(11122163980771643160)
XLA Ops:
  0.0 0.5 collective-permute-start.3
  0.5 1.3 %collective-permute-start.2 = (bf16[6,128,256]{2,1,0:T(8,128)(2,1)}, bf16[6,128,256]{2,1,0:T(8,128)(2,1)S(1)}, u32[]{:S(2)}, u32[]{:S(2)}) collective-permute-start(bf16[6,128,256]{2,1,0:T(8,128)(2,1)} %bitcast.2), channel_id=1, source_target_pairs={{1,0},{2,1},{3,2},{5,4},{6,5},{7,6},{9,8},{10,9},{11,10},{13,12},{... | collective-permute-start | bytes 1179656 | tf_op jit(solution)/shard_map/ppermute | solution.py:347
  1.7 4.8 %collective-permute-start.1 = (bf16[6,128,256]{2,1,0:T(8,128)(2,1)}, bf16[6,128,256]{2,1,0:T(8,128)(2,1)S(1)}, u32[]{:S(2)}, u32[]{:S(2)}) collective-permute-start(bf16[6,128,256]{2,1,0:T(8,128)(2,1)} %bitcast.3), channel_id=1, source_target_pairs={{0,16},{4,20},{8,24},{12,28},{16,0},{20,4},{24,8},{28,12},{1,17},{... | collective-permute-start | bytes 1179656 | tf_op jit(solution)/shard_map/ppermute | solution.py:337
  6.5 1.5 %collective-permute-start = (bf16[6,128,256]{2,1,0:T(8,128)(2,1)}, bf16[6,128,256]{2,1,0:T(8,128)(2,1)S(1)}, u32[]{:S(2)}, u32[]{:S(2)}) collective-permute-start(bf16[6,128,256]{2,1,0:T(8,128)(2,1)} %bitcast.4), channel_id=1, source_target_pairs={{0,8},{4,12},{8,0},{12,4},{16,24},{20,28},{24,16},{28,20},{1,9},{5... | collective-permute-start | bytes 1179656 | tf_op jit(solution)/shard_map/ppermute | solution.py:337
  8.0 0.0 copy-start.1
  8.0 0.0 collective-permute-start.4
  8.0 11.3 %shard_map.91 = (bf16[99,128,128]{2,1,0:T(8,128)(2,1)S(1)}, bf16[128,1536]{1,0:T(8,128)(2,1)S(1)}, bf16[1536,128]{1,0:T(8,128)(2,1)S(1)}, f32[316,1536]{1,0:T(8,...) custom-call(s32[9]{0:T(128)} %off_hbm.1, s32[1,48,48]{2,1,0:T(8,128)} %src_hbm.1, s32[1,48,48]{2,1,0:T(8,128)} %tid_hbm.1, ...), custom_call_target="tpu_custom_call" | custom-call | flops 7952400384 | bytes 1048576 | tf_op jit(solution)/shard_map/pallas_call | solution.py:373
  19.3 0.0 collective-permute-done.2.rest_3_
  19.3 0.0 collective-permute-done.1.rest_2_
  19.3 0.0 collective-permute-done.rest_1_
  19.3 0.0 collective-permute-done.4.near_src_other_ref
  19.3 0.0 collective-permute-done.3.near_other_hbm
  19.4 0.1 collective-permute-start.5
  19.4 1.3 %collective-permute-start.7 = (bf16[6,128,256]{2,1,0:T(8,128)(2,1)S(1)}, bf16[6,128,256]{2,1,0:T(8,128)(2,1)S(1)}, u32[]{:S(2)}, u32[]{:S(2)}) collective-permute-start(bf16[6,128,256]{2,1,0:T(8,128)(2,1)S(1)} %collective-permute-done.rest_1_), channel_id=1, source_target_pairs={{1,0},{2,1},{3,2},{5,4},{6,5},{7,6},{9,8},{10,9},{11,10},{13,12},{... | collective-permute-start | bytes 1179656 | tf_op jit(solution)/shard_map/ppermute | solution.py:347
  20.7 1.2 %collective-permute-start.6 = (bf16[6,128,256]{2,1,0:T(8,128)(2,1)S(1)}, bf16[6,128,256]{2,1,0:T(8,128)(2,1)S(1)}, u32[]{:S(2)}, u32[]{:S(2)}) collective-permute-start(bf16[6,128,256]{2,1,0:T(8,128)(2,1)S(1)} %collective-permute-done.1.rest_2_), channel_id=1, source_target_pairs={{0,8},{4,12},{8,0},{12,4},{16,24},{20,28},{24,16},{28,20},{1,9},{5... | collective-permute-start | bytes 1179656 | tf_op jit(solution)/shard_map/ppermute | solution.py:337
  21.9 2.7 %collective-permute-start.8 = (bf16[6,128,256]{2,1,0:T(8,128)(2,1)S(1)}, bf16[6,128,256]{2,1,0:T(8,128)(2,1)S(1)}, u32[]{:S(2)}, u32[]{:S(2)}) collective-permute-start(bf16[6,128,256]{2,1,0:T(8,128)(2,1)S(1)} %collective-permute-done.2.rest_3_), channel_id=1, source_target_pairs={{0,16},{4,20},{8,24},{12,28},{16,0},{20,4},{24,8},{28,12},{1,17},{... | collective-permute-start | bytes 1179656 | tf_op jit(solution)/shard_map/ppermute | solution.py:337
  24.7 0.0 copy-done.1
  24.7 8.3 %shard_map.92 = (bf16[318,128,128]{2,1,0:T(8,128)(2,1)S(1)}, bf16[12,28,128,128]{3,2,1,0:T(8,128)(2,1)S(1)}, s32[16,128]{1,0:T(8,128)S(1)}) custom-call(s32[8,384]{1,0:T(8,128)S(1)} %get-tuple-element.29.list_ref, f32[316,1536]{1,0:T(8,128)S(1)} %get-tuple-element.30.rows_ref, bf16[128,1536]{1,0:T(8,128)(2,1)S(1)} %get-tuple-element.31.weighted_ref, ...), custom_call_target="tpu_custom_call" | custom-call | flops 7952400384 | bytes 1048576 | tf_op jit(solution)/shard_map/pallas_call | solution.py:410
  32.9 0.3 collective-permute-done.7.rest_5_.rest_1_
  33.3 0.0 collective-permute-start.9
  33.3 0.0 collective-permute-done.6.rest_4_.rest_0_
  33.3 0.1 collective-permute-done.8.rest_6_.rest_2_
  33.4 0.0 collective-permute-done.5.low_ref
  33.4 0.0 copy-done
  33.4 7.2 %shard_map.93 = (bf16[318,128,128]{2,1,0:T(8,128)(2,1)S(1)}, bf16[6,128,256]{2,1,0:T(8,128)(2,1)S(1)}, f32[6,128,256]{2,1,0:T(8,128)S(1)}) custom-call(s32[8,384]{1,0:T(8,128)S(1)} %get-tuple-element.29.list_ref, s32[16,128]{1,0:T(8,128)S(1)} %get-tuple-element.28.cls_ref, ...), custom_call_target="tpu_custom_call", output_to_operand_aliasing={{0}: (15, {})} | custom-call | flops 1048576 | bytes 1048576 | tf_op jit(solution)/shard_map/pallas_call | solution.py:466
  40.7 0.1 collective-permute-start.11
  40.7 3.0 %collective-permute-done.9.rest_0_ = bf16[6,128,256]{2,1,0:T(8,128)(2,1)S(1)} collective-permute-done((bf16[6,128,256]{2,1,0:T(8,128)(2,1)S(1)}, bf16[6,128,256]{2,1,0:T(8,128)(2,1)S(1)}, u32[]{:S(2)}, u32[]{:S(2)}) %collective-permute-start.9) | collective-permute-done | bytes 393248 | tf_op jit(solution)/shard_map/ppermute | solution.py:337
  43.8 0.0 collective-permute-start.10
  43.8 2.3 %shard_map.94.rest_2_ = f32[6,128,256]{2,1,0:T(8,128)S(1)} custom-call(s32[16,128]{1,0:T(8,128)S(1)} %get-tuple-element.28.cls_ref, s32[16,128]{1,0:T(8,128)S(1)} %get-tuple-element.38.near_map_ref, s32[8,384]{1,0:T(8,128)S(1)} %get-tuple-element.29.list_ref, bf16[318,128,128]{2,1,0:T(8,128)(2,1)S(1)} %get-tuple-element.46.t_ref, ...), custom_call_target="tpu_custom_call" | custom-call | flops 1048576 | bytes 1048576 | tf_op jit(solution)/shard_map/pallas_call | solution.py:445
  46.0 0.0 collective-permute-done.11.rest_3_
  46.1 0.0 collective-permute-done.10.rest_1_
  46.1 2.6 %shard_map.95 = bf16[1,6,128,256]{3,2,1,0:T(8,128)(2,1)} custom-call(s32[16,128]{1,0:T(8,128)S(1)} %get-tuple-element.28.cls_ref, s32[16,128]{1,0:T(8,128)S(1)} %get-tuple-element.38.near_map_ref, s32[8,384]{1,0:T(8,128)S(1)} %get-tuple-element.29.list_ref, bf16[318,128,128]{2,1,0:T(8,128)(2,1)S(1)} %get-tuple-element.46.t_ref, ...), custom_call_target="tpu_custom_call" | custom-call | flops 1048576 | bytes 1048576 | tf_op jit(solution)/shard_map/pallas_call | solution.py:445
  (1 shorter events, 0.0 us)
Async XLA Ops:
  0.0 19.3 %collective-permute-start.3 = (bf16[1,6,27,128,128]{4,3,2,1,0:T(8,128)(2,1)}, bf16[1,6,27,128,128]{4,3,2,1,0:T(8,128)(2,1)S(1)}, u32[]{:S(2)}, u32[]{:S(2)}) collective-permute-start(bf16[1,6,27,128,128]{4,3,2,1,0:T(8,128)(2,1)} %near_hbm.1), channel_id=1, source_target_pairs={{0,4},{4,0},{8,12},{12,8},{16,20},{20,16},{24,28},{28,24},{1,5},{5... | collective-permute-start | bytes 15925256 | tf_op jit(solution)/shard_map/ppermute | solution.py:337
  0.5 18.9 %collective-permute-start.2 = (bf16[6,128,256]{2,1,0:T(8,128)(2,1)}, bf16[6,128,256]{2,1,0:T(8,128)(2,1)S(1)}, u32[]{:S(2)}, u32[]{:S(2)}) collective-permute-start(bf16[6,128,256]{2,1,0:T(8,128)(2,1)} %bitcast.2), channel_id=1, source_target_pairs={{1,0},{2,1},{3,2},{5,4},{6,5},{7,6},{9,8},{10,9},{11,10},{13,12},{... | collective-permute-start | bytes 1179656 | tf_op jit(solution)/shard_map/ppermute | solution.py:347
  1.7 17.6 %collective-permute-start.1 = (bf16[6,128,256]{2,1,0:T(8,128)(2,1)}, bf16[6,128,256]{2,1,0:T(8,128)(2,1)S(1)}, u32[]{:S(2)}, u32[]{:S(2)}) collective-permute-start(bf16[6,128,256]{2,1,0:T(8,128)(2,1)} %bitcast.3), channel_id=1, source_target_pairs={{0,16},{4,20},{8,24},{12,28},{16,0},{20,4},{24,8},{28,12},{1,17},{... | collective-permute-start | bytes 1179656 | tf_op jit(solution)/shard_map/ppermute | solution.py:337
  6.5 12.8 %collective-permute-start = (bf16[6,128,256]{2,1,0:T(8,128)(2,1)}, bf16[6,128,256]{2,1,0:T(8,128)(2,1)S(1)}, u32[]{:S(2)}, u32[]{:S(2)}) collective-permute-start(bf16[6,128,256]{2,1,0:T(8,128)(2,1)} %bitcast.4), channel_id=1, source_target_pairs={{0,8},{4,12},{8,0},{12,4},{16,24},{20,28},{24,16},{28,20},{1,9},{5... | collective-permute-start | bytes 1179656 | tf_op jit(solution)/shard_map/ppermute | solution.py:337
  8.0 16.6 %copy-start.1 = (s32[1,6,27]{2,0,1:T(1,128)S(1)}, s32[1,6,27]{2,0,1:T(1,128)}, u32[]{:S(2)}) copy-start(s32[1,6,27]{2,0,1:T(1,128)} %param.17) | copy-start | bytes 1948
  8.0 11.3 %collective-permute-start.4 = (s32[6,1,27]{2,1,0:T(1,128)}, s32[6,1,27]{2,1,0:T(1,128)S(1)}, u32[]{:S(2)}, u32[]{:S(2)}) collective-permute-start(s32[6,1,27]{2,1,0:T(1,128)} %bitcast.6), channel_id=1, source_target_pairs={{0,4},{4,0},{8,12},{12,8},{16,20},{20,16},{24,28},{28,24},{1,5},{5... | collective-permute-start | bytes 1952 | tf_op jit(solution)/shard_map/ppermute | solution.py:337
  19.4 14.1 %collective-permute-start.5 = (bf16[99,128,128]{2,1,0:T(8,128)(2,1)S(1)}, bf16[99,128,128]{2,1,0:T(8,128)(2,1)S(1)}, u32[]{:S(2)}, u32[]{:S(2)}) collective-permute-start(bf16[99,128,128]{2,1,0:T(8,128)(2,1)S(1)} %get-tuple-element.37.low_ref), channel_id=1, source_target_pairs={{0,4},{4,0},{8,12},{12,8},{16,20},{20,16},{24,28},{28,24},{1,5},{5... | collective-permute-start | bytes 9732104 | tf_op jit(solution)/shard_map/ppermute | solution.py:337
  19.4 13.8 %collective-permute-start.7 = (bf16[6,128,256]{2,1,0:T(8,128)(2,1)S(1)}, bf16[6,128,256]{2,1,0:T(8,128)(2,1)S(1)}, u32[]{:S(2)}, u32[]{:S(2)}) collective-permute-start(bf16[6,128,256]{2,1,0:T(8,128)(2,1)S(1)} %collective-permute-done.rest_1_), channel_id=1, source_target_pairs={{1,0},{2,1},{3,2},{5,4},{6,5},{7,6},{9,8},{10,9},{11,10},{13,12},{... | collective-permute-start | bytes 1179656 | tf_op jit(solution)/shard_map/ppermute | solution.py:347
  20.7 12.5 %collective-permute-start.6 = (bf16[6,128,256]{2,1,0:T(8,128)(2,1)S(1)}, bf16[6,128,256]{2,1,0:T(8,128)(2,1)S(1)}, u32[]{:S(2)}, u32[]{:S(2)}) collective-permute-start(bf16[6,128,256]{2,1,0:T(8,128)(2,1)S(1)} %collective-permute-done.1.rest_2_), channel_id=1, source_target_pairs={{0,8},{4,12},{8,0},{12,4},{16,24},{20,28},{24,16},{28,20},{1,9},{5... | collective-permute-start | bytes 1179656 | tf_op jit(solution)/shard_map/ppermute | solution.py:337
  21.9 11.5 %collective-permute-start.8 = (bf16[6,128,256]{2,1,0:T(8,128)(2,1)S(1)}, bf16[6,128,256]{2,1,0:T(8,128)(2,1)S(1)}, u32[]{:S(2)}, u32[]{:S(2)}) collective-permute-start(bf16[6,128,256]{2,1,0:T(8,128)(2,1)S(1)} %collective-permute-done.2.rest_3_), channel_id=1, source_target_pairs={{0,16},{4,20},{8,24},{12,28},{16,0},{20,4},{24,8},{28,12},{1,17},{... | collective-permute-start | bytes 1179656 | tf_op jit(solution)/shard_map/ppermute | solution.py:337
  24.7 8.7 %copy-start = (bf16[1,6,128,256]{3,2,1,0:T(8,128)(2,1)S(1)}, bf16[1,6,128,256]{3,2,1,0:T(8,128)(2,1)}, u32[]{:S(2)}) copy-start(bf16[1,6,128,256]{3,2,1,0:T(8,128)(2,1)} %param.9) | copy-start | bytes 1179652
  33.3 10.5 %collective-permute-start.9 = (bf16[6,128,256]{2,1,0:T(8,128)(2,1)S(1)}, bf16[6,128,256]{2,1,0:T(8,128)(2,1)S(1)}, u32[]{:S(2)}, u32[]{:S(2)}) collective-permute-start(bf16[6,128,256]{2,1,0:T(8,128)(2,1)S(1)} %collective-permute-done.7.rest_5_.rest_1_), channel_id=1, source_target_pairs={{0,16},{4,20},{8,24},{12,28},{16,0},{20,4},{24,8},{28,12},{1,17},{... | collective-permute-start | bytes 1179656 | tf_op jit(solution)/shard_map/ppermute | solution.py:337
  40.7 5.4 %collective-permute-start.11 = (bf16[6,128,256]{2,1,0:T(8,128)(2,1)S(1)}, bf16[6,128,256]{2,1,0:T(8,128)(2,1)S(1)}, u32[]{:S(2)}, u32[]{:S(2)}) collective-permute-start(bf16[6,128,256]{2,1,0:T(8,128)(2,1)S(1)} %get-tuple-element.50), channel_id=1, source_target_pairs={{0,4},{4,0},{8,12},{12,8},{16,20},{20,16},{24,28},{28,24},{1,5},{5... | collective-permute-start | bytes 1179656 | tf_op jit(solution)/shard_map/ppermute | solution.py:337
  43.8 2.3 %collective-permute-start.10 = (bf16[6,128,256]{2,1,0:T(8,128)(2,1)S(1)}, bf16[6,128,256]{2,1,0:T(8,128)(2,1)S(1)}, u32[]{:S(2)}, u32[]{:S(2)}) collective-permute-start(bf16[6,128,256]{2,1,0:T(8,128)(2,1)S(1)} %collective-permute-done.9.rest_0_), channel_id=1, source_target_pairs={{0,4},{4,0},{8,12},{12,8},{16,20},{20,16},{24,28},{28,24},{1,5},{5... | collective-permute-start | bytes 1179656 | tf_op jit(solution)/shard_map/ppermute | solution.py:337

commit v13 on v11

--- a/solution.py
+++ b/solution.py
@@ -11,7 +11,7 @@
 NT_DIMS = (((1,), (1,)), ((), ()))
 LANES = 128
 ROWS = 8
-UNROLL = 16
+UNROLL = 24
 TAIL = 4
 GROUP = 8
 MIB = 2**20

time: 47.7 us -> 48.2 us (1.010)
  starting transfers between devices: 12.7 us -> 13.9 us
    ppermute x10, starting transfers between devices: 10.1 us -> 11.4 us  [partner(): return lax.ppermute(array, 'dir', [(i, i ^ mask) for i in range(dir_count)])]
    pallas_call x1, Pallas kernels: 9.34 us -> 10.1 us  [shards(): pl.pallas_call(functools.partial(third_kernel, second_end, empty, [(outsi...]
    pallas_call x1, Pallas kernels: 10.5 us -> 9.79 us  [shards(): pl.pallas_call(functools.partial(first_kernel, shared, boxes, halo, regio...]
    ppermute x2, waiting for transfers between devices: 0.57 us -> 0.01 us  [beyond(): return lax.ppermute(array, ('dir', 'region'), along)]
  transfers between devices with their start and end apart: 12 -> 12, of which waited for: 3 -> 1; matrix products, arithmetic and copies ran while one was open for 0% -> 0% of each run, Pallas kernels for 64% -> 63%
where the time goes in v13:
time: 48.2 us; the launch traced here: 47.9 us
  Pallas kernels  32.9 us (68%)
  starting transfers between devices  13.9 us (29%)
  waiting for transfers between devices  0.92 us (2%)
    ppermute x10, starting transfers between devices, partner(): return lax.ppermute(array, 'dir', [(i, i ^ mask) for i in range(dir_count)])  11.4 us
    pallas_call x1, Pallas kernels, shards(): pl.pallas_call(functools.partial(third_kernel, second_end, empty, [(outsi...  10.1 us
    pallas_call x1, Pallas kernels, shards(): pl.pallas_call(functools.partial(first_kernel, shared, boxes, halo, regio...  9.79 us
    pallas_call x1, Pallas kernels, shards(): pl.pallas_call(functools.partial(second_kernel, second_end, empty, halo -...  8.2 us
    pallas_call x2, Pallas kernels, apply(): pl.pallas_call(kernel, in_specs=specs, out_specs=vmem, out_shape=pltpu.VM...  4.87 us
    ppermute x2, starting transfers between devices, beyond(): return lax.ppermute(array, ('dir', 'region'), along)  2.57 us
  transfers between devices with their start and end apart: 12, of which 1 were waited for; matrix products, arithmetic and copies ran while one was open for 0% of the time, Pallas kernels for 63%

profile of v13, /device:TPU:0, one launch (start us, length us, event | category | flops | bytes accessed | tf_op | source)
XLA Modules:
  0.0 47.9 jit_solution(2842500840973261219)
XLA Ops:
  0.0 0.5 collective-permute-start.3
  0.5 1.3 %collective-permute-start.2 = (bf16[6,128,256]{2,1,0:T(8,128)(2,1)}, bf16[6,128,256]{2,1,0:T(8,128)(2,1)S(1)}, u32[]{:S(2)}, u32[]{:S(2)}) collective-permute-start(bf16[6,128,256]{2,1,0:T(8,128)(2,1)} %bitcast.2), channel_id=1, source_target_pairs={{1,0},{2,1},{3,2},{5,4},{6,5},{7,6},{9,8},{10,9},{11,10},{13,12},{... | collective-permute-start | bytes 1179656 | tf_op jit(solution)/shard_map/ppermute | solution.py:347
  1.7 4.8 %collective-permute-start.1 = (bf16[6,128,256]{2,1,0:T(8,128)(2,1)}, bf16[6,128,256]{2,1,0:T(8,128)(2,1)S(1)}, u32[]{:S(2)}, u32[]{:S(2)}) collective-permute-start(bf16[6,128,256]{2,1,0:T(8,128)(2,1)} %bitcast.3), channel_id=1, source_target_pairs={{0,16},{4,20},{8,24},{12,28},{16,0},{20,4},{24,8},{28,12},{1,17},{... | collective-permute-start | bytes 1179656 | tf_op jit(solution)/shard_map/ppermute | solution.py:337
  6.5 1.5 %collective-permute-start = (bf16[6,128,256]{2,1,0:T(8,128)(2,1)}, bf16[6,128,256]{2,1,0:T(8,128)(2,1)S(1)}, u32[]{:S(2)}, u32[]{:S(2)}) collective-permute-start(bf16[6,128,256]{2,1,0:T(8,128)(2,1)} %bitcast.4), channel_id=1, source_target_pairs={{0,8},{4,12},{8,0},{12,4},{16,24},{20,28},{24,16},{28,20},{1,9},{5... | collective-permute-start | bytes 1179656 | tf_op jit(solution)/shard_map/ppermute | solution.py:337
  8.0 0.0 copy-start.1
  8.0 0.0 collective-permute-start.4
  8.0 9.8 %shard_map.91 = (bf16[79,128,128]{2,1,0:T(8,128)(2,1)S(1)}, bf16[128,1536]{1,0:T(8,128)(2,1)S(1)}, bf16[1536,128]{1,0:T(8,128)(2,1)S(1)}, f32[316,1536]{1,0:T(8,...) custom-call(s32[9]{0:T(128)} %off_hbm.1, s32[1,48,48]{2,1,0:T(8,128)} %src_hbm.1, s32[1,48,48]{2,1,0:T(8,128)} %tid_hbm.1, ...), custom_call_target="tpu_custom_call" | custom-call | flops 7952400384 | bytes 1048576 | tf_op jit(solution)/shard_map/pallas_call | solution.py:373
  17.8 0.0 collective-permute-done.2.rest_3_
  17.8 0.0 collective-permute-done.1.rest_2_
  17.9 0.0 collective-permute-done.rest_1_
  17.9 0.0 collective-permute-done.4.near_src_other_ref
  17.9 0.0 collective-permute-done.3.near_other_hbm
  17.9 0.1 collective-permute-start.5
  18.0 1.3 %collective-permute-start.7 = (bf16[6,128,256]{2,1,0:T(8,128)(2,1)S(1)}, bf16[6,128,256]{2,1,0:T(8,128)(2,1)S(1)}, u32[]{:S(2)}, u32[]{:S(2)}) collective-permute-start(bf16[6,128,256]{2,1,0:T(8,128)(2,1)S(1)} %collective-permute-done.rest_1_), channel_id=1, source_target_pairs={{1,0},{2,1},{3,2},{5,4},{6,5},{7,6},{9,8},{10,9},{11,10},{13,12},{... | collective-permute-start | bytes 1179656 | tf_op jit(solution)/shard_map/ppermute | solution.py:347
  19.3 1.3 %collective-permute-start.6 = (bf16[6,128,256]{2,1,0:T(8,128)(2,1)S(1)}, bf16[6,128,256]{2,1,0:T(8,128)(2,1)S(1)}, u32[]{:S(2)}, u32[]{:S(2)}) collective-permute-start(bf16[6,128,256]{2,1,0:T(8,128)(2,1)S(1)} %collective-permute-done.1.rest_2_), channel_id=1, source_target_pairs={{0,8},{4,12},{8,0},{12,4},{16,24},{20,28},{24,16},{28,20},{1,9},{5... | collective-permute-start | bytes 1179656 | tf_op jit(solution)/shard_map/ppermute | solution.py:337
  20.6 2.6 %collective-permute-start.8 = (bf16[6,128,256]{2,1,0:T(8,128)(2,1)S(1)}, bf16[6,128,256]{2,1,0:T(8,128)(2,1)S(1)}, u32[]{:S(2)}, u32[]{:S(2)}) collective-permute-start(bf16[6,128,256]{2,1,0:T(8,128)(2,1)S(1)} %collective-permute-done.2.rest_3_), channel_id=1, source_target_pairs={{0,16},{4,20},{8,24},{12,28},{16,0},{20,4},{24,8},{28,12},{1,17},{... | collective-permute-start | bytes 1179656 | tf_op jit(solution)/shard_map/ppermute | solution.py:337
  23.2 0.0 copy-done.1
  23.2 8.2 %shard_map.92 = (bf16[317,128,128]{2,1,0:T(8,128)(2,1)S(1)}, bf16[12,28,128,128]{3,2,1,0:T(8,128)(2,1)S(1)}, s32[16,128]{1,0:T(8,128)S(1)}) custom-call(s32[8,384]{1,0:T(8,128)S(1)} %get-tuple-element.29.list_ref, f32[316,1536]{1,0:T(8,128)S(1)} %get-tuple-element.30.rows_ref, bf16[128,1536]{1,0:T(8,128)(2,1)S(1)} %get-tuple-element.31.weighted_ref, ...), custom_call_target="tpu_custom_call" | custom-call | flops 7952400384 | bytes 1048576 | tf_op jit(solution)/shard_map/pallas_call | solution.py:410
  31.4 0.0 collective-permute-done.7.rest_5_.rest_1_
  31.4 0.1 collective-permute-start.9
  31.5 0.0 collective-permute-done.6.rest_4_.rest_0_
  31.5 0.9 %collective-permute-done.8.rest_6_.rest_2_ = bf16[6,128,256]{2,1,0:T(8,128)(2,1)S(1)} collective-permute-done((bf16[6,128,256]{2,1,0:T(8,128)(2,1)S(1)}, bf16[6,128,256]{2,1,0:T(8,128)(2,1)S(1)}, u32[]{:S(2)}, u32[]{:S(2)}) %collective-permute-start.8) | collective-permute-done | bytes 393248 | tf_op jit(solution)/shard_map/ppermute | solution.py:337
  32.4 0.0 collective-permute-done.5.low_ref
  32.4 0.0 copy-done
  32.4 10.1 %shard_map.93 = (bf16[317,128,128]{2,1,0:T(8,128)(2,1)S(1)}, bf16[6,128,256]{2,1,0:T(8,128)(2,1)S(1)}, f32[6,128,256]{2,1,0:T(8,128)S(1)}) custom-call(s32[8,384]{1,0:T(8,128)S(1)} %get-tuple-element.29.list_ref, s32[16,128]{1,0:T(8,128)S(1)} %get-tuple-element.28.cls_ref, ...), custom_call_target="tpu_custom_call", output_to_operand_aliasing={{0}: (15, {})} | custom-call | flops 1048576 | bytes 1048576 | tf_op jit(solution)/shard_map/pallas_call | solution.py:466
  42.5 0.1 collective-permute-start.11
  42.5 0.0 collective-permute-done.9.rest_0_
  42.6 0.5 %collective-permute-start.10 = (bf16[6,128,256]{2,1,0:T(8,128)(2,1)S(1)}, bf16[6,128,256]{2,1,0:T(8,128)(2,1)S(1)}, u32[]{:S(2)}, u32[]{:S(2)}) collective-permute-start(bf16[6,128,256]{2,1,0:T(8,128)(2,1)S(1)} %collective-permute-done.9.rest_0_), channel_id=1, source_target_pairs={{0,4},{4,0},{8,12},{12,8},{16,20},{20,16},{24,28},{28,24},{1,5},{5... | collective-permute-start | bytes 1179656 | tf_op jit(solution)/shard_map/ppermute | solution.py:337
  43.0 2.2 %shard_map.94.rest_2_ = f32[6,128,256]{2,1,0:T(8,128)S(1)} custom-call(s32[16,128]{1,0:T(8,128)S(1)} %get-tuple-element.28.cls_ref, s32[16,128]{1,0:T(8,128)S(1)} %get-tuple-element.38.near_map_ref, s32[8,384]{1,0:T(8,128)S(1)} %get-tuple-element.29.list_ref, bf16[317,128,128]{2,1,0:T(8,128)(2,1)S(1)} %get-tuple-element.46.t_ref, ...), custom_call_target="tpu_custom_call" | custom-call | flops 1048576 | bytes 1048576 | tf_op jit(solution)/shard_map/pallas_call | solution.py:445
  45.3 0.0 collective-permute-done.11.rest_3_
  45.3 0.0 collective-permute-done.10.rest_1_
  45.3 2.6 %shard_map.95 = bf16[1,6,128,256]{3,2,1,0:T(8,128)(2,1)} custom-call(s32[16,128]{1,0:T(8,128)S(1)} %get-tuple-element.28.cls_ref, s32[16,128]{1,0:T(8,128)S(1)} %get-tuple-element.38.near_map_ref, s32[8,384]{1,0:T(8,128)S(1)} %get-tuple-element.29.list_ref, bf16[317,128,128]{2,1,0:T(8,128)(2,1)S(1)} %get-tuple-element.46.t_ref, ...), custom_call_target="tpu_custom_call" | custom-call | flops 1048576 | bytes 1048576 | tf_op jit(solution)/shard_map/pallas_call | solution.py:445
  (1 shorter events, 0.0 us)
Async XLA Ops:
  0.0 17.9 %collective-permute-start.3 = (bf16[1,6,27,128,128]{4,3,2,1,0:T(8,128)(2,1)}, bf16[1,6,27,128,128]{4,3,2,1,0:T(8,128)(2,1)S(1)}, u32[]{:S(2)}, u32[]{:S(2)}) collective-permute-start(bf16[1,6,27,128,128]{4,3,2,1,0:T(8,128)(2,1)} %near_hbm.1), channel_id=1, source_target_pairs={{0,4},{4,0},{8,12},{12,8},{16,20},{20,16},{24,28},{28,24},{1,5},{5... | collective-permute-start | bytes 15925256 | tf_op jit(solution)/shard_map/ppermute | solution.py:337
  0.5 17.4 %collective-permute-start.2 = (bf16[6,128,256]{2,1,0:T(8,128)(2,1)}, bf16[6,128,256]{2,1,0:T(8,128)(2,1)S(1)}, u32[]{:S(2)}, u32[]{:S(2)}) collective-permute-start(bf16[6,128,256]{2,1,0:T(8,128)(2,1)} %bitcast.2), channel_id=1, source_target_pairs={{1,0},{2,1},{3,2},{5,4},{6,5},{7,6},{9,8},{10,9},{11,10},{13,12},{... | collective-permute-start | bytes 1179656 | tf_op jit(solution)/shard_map/ppermute | solution.py:347
  1.7 16.1 %collective-permute-start.1 = (bf16[6,128,256]{2,1,0:T(8,128)(2,1)}, bf16[6,128,256]{2,1,0:T(8,128)(2,1)S(1)}, u32[]{:S(2)}, u32[]{:S(2)}) collective-permute-start(bf16[6,128,256]{2,1,0:T(8,128)(2,1)} %bitcast.3), channel_id=1, source_target_pairs={{0,16},{4,20},{8,24},{12,28},{16,0},{20,4},{24,8},{28,12},{1,17},{... | collective-permute-start | bytes 1179656 | tf_op jit(solution)/shard_map/ppermute | solution.py:337
  6.5 11.3 %collective-permute-start = (bf16[6,128,256]{2,1,0:T(8,128)(2,1)}, bf16[6,128,256]{2,1,0:T(8,128)(2,1)S(1)}, u32[]{:S(2)}, u32[]{:S(2)}) collective-permute-start(bf16[6,128,256]{2,1,0:T(8,128)(2,1)} %bitcast.4), channel_id=1, source_target_pairs={{0,8},{4,12},{8,0},{12,4},{16,24},{20,28},{24,16},{28,20},{1,9},{5... | collective-permute-start | bytes 1179656 | tf_op jit(solution)/shard_map/ppermute | solution.py:337
  8.0 15.1 %copy-start.1 = (s32[1,6,27]{2,0,1:T(1,128)S(1)}, s32[1,6,27]{2,0,1:T(1,128)}, u32[]{:S(2)}) copy-start(s32[1,6,27]{2,0,1:T(1,128)} %param.17) | copy-start | bytes 1948
  8.0 9.8 %collective-permute-start.4 = (s32[6,1,27]{2,1,0:T(1,128)}, s32[6,1,27]{2,1,0:T(1,128)S(1)}, u32[]{:S(2)}, u32[]{:S(2)}) collective-permute-start(s32[6,1,27]{2,1,0:T(1,128)} %bitcast.6), channel_id=1, source_target_pairs={{0,4},{4,0},{8,12},{12,8},{16,20},{20,16},{24,28},{28,24},{1,5},{5... | collective-permute-start | bytes 1952 | tf_op jit(solution)/shard_map/ppermute | solution.py:337
  17.9 14.5 %collective-permute-start.5 = (bf16[79,128,128]{2,1,0:T(8,128)(2,1)S(1)}, bf16[79,128,128]{2,1,0:T(8,128)(2,1)S(1)}, u32[]{:S(2)}, u32[]{:S(2)}) collective-permute-start(bf16[79,128,128]{2,1,0:T(8,128)(2,1)S(1)} %get-tuple-element.37.low_ref), channel_id=1, source_target_pairs={{0,4},{4,0},{8,12},{12,8},{16,20},{20,16},{24,28},{28,24},{1,5},{5... | collective-permute-start | bytes 7766024 | tf_op jit(solution)/shard_map/ppermute | solution.py:337
  18.0 13.4 %collective-permute-start.7 = (bf16[6,128,256]{2,1,0:T(8,128)(2,1)S(1)}, bf16[6,128,256]{2,1,0:T(8,128)(2,1)S(1)}, u32[]{:S(2)}, u32[]{:S(2)}) collective-permute-start(bf16[6,128,256]{2,1,0:T(8,128)(2,1)S(1)} %collective-permute-done.rest_1_), channel_id=1, source_target_pairs={{1,0},{2,1},{3,2},{5,4},{6,5},{7,6},{9,8},{10,9},{11,10},{13,12},{... | collective-permute-start | bytes 1179656 | tf_op jit(solution)/shard_map/ppermute | solution.py:347
  19.3 12.2 %collective-permute-start.6 = (bf16[6,128,256]{2,1,0:T(8,128)(2,1)S(1)}, bf16[6,128,256]{2,1,0:T(8,128)(2,1)S(1)}, u32[]{:S(2)}, u32[]{:S(2)}) collective-permute-start(bf16[6,128,256]{2,1,0:T(8,128)(2,1)S(1)} %collective-permute-done.1.rest_2_), channel_id=1, source_target_pairs={{0,8},{4,12},{8,0},{12,4},{16,24},{20,28},{24,16},{28,20},{1,9},{5... | collective-permute-start | bytes 1179656 | tf_op jit(solution)/shard_map/ppermute | solution.py:337
  20.6 11.8 %collective-permute-start.8 = (bf16[6,128,256]{2,1,0:T(8,128)(2,1)S(1)}, bf16[6,128,256]{2,1,0:T(8,128)(2,1)S(1)}, u32[]{:S(2)}, u32[]{:S(2)}) collective-permute-start(bf16[6,128,256]{2,1,0:T(8,128)(2,1)S(1)} %collective-permute-done.2.rest_3_), channel_id=1, source_target_pairs={{0,16},{4,20},{8,24},{12,28},{16,0},{20,4},{24,8},{28,12},{1,17},{... | collective-permute-start | bytes 1179656 | tf_op jit(solution)/shard_map/ppermute | solution.py:337
  23.2 9.2 %copy-start = (bf16[1,6,128,256]{3,2,1,0:T(8,128)(2,1)S(1)}, bf16[1,6,128,256]{3,2,1,0:T(8,128)(2,1)}, u32[]{:S(2)}) copy-start(bf16[1,6,128,256]{3,2,1,0:T(8,128)(2,1)} %param.9) | copy-start | bytes 1179652
  31.4 11.2 %collective-permute-start.9 = (bf16[6,128,256]{2,1,0:T(8,128)(2,1)S(1)}, bf16[6,128,256]{2,1,0:T(8,128)(2,1)S(1)}, u32[]{:S(2)}, u32[]{:S(2)}) collective-permute-start(bf16[6,128,256]{2,1,0:T(8,128)(2,1)S(1)} %collective-permute-done.7.rest_5_.rest_1_), channel_id=1, source_target_pairs={{0,16},{4,20},{8,24},{12,28},{16,0},{20,4},{24,8},{28,12},{1,17},{... | collective-permute-start | bytes 1179656 | tf_op jit(solution)/shard_map/ppermute | solution.py:337
  42.5 2.8 %collective-permute-start.11 = (bf16[6,128,256]{2,1,0:T(8,128)(2,1)S(1)}, bf16[6,128,256]{2,1,0:T(8,128)(2,1)S(1)}, u32[]{:S(2)}, u32[]{:S(2)}) collective-permute-start(bf16[6,128,256]{2,1,0:T(8,128)(2,1)S(1)} %get-tuple-element.50), channel_id=1, source_target_pairs={{0,4},{4,0},{8,12},{12,8},{16,20},{20,16},{24,28},{28,24},{1,5},{5... | collective-permute-start | bytes 1179656 | tf_op jit(solution)/shard_map/ppermute | solution.py:337
  42.6 2.7 %collective-permute-start.10 = (bf16[6,128,256]{2,1,0:T(8,128)(2,1)S(1)}, bf16[6,128,256]{2,1,0:T(8,128)(2,1)S(1)}, u32[]{:S(2)}, u32[]{:S(2)}) collective-permute-start(bf16[6,128,256]{2,1,0:T(8,128)(2,1)S(1)} %collective-permute-done.9.rest_0_), channel_id=1, source_target_pairs={{0,4},{4,0},{8,12},{12,8},{16,20},{20,16},{24,28},{28,24},{1,5},{5... | collective-permute-start | bytes 1179656 | tf_op jit(solution)/shard_map/ppermute | solution.py:337
